TPU v7x, 256 devices: a whole 4x4x8 slice. The times are simulated.
256 devices in a mesh: row: 8 (over y, x_hi), col: 32 (over z, x_lo, core).
Axes of the slice: x: 4 (x_hi: 2, x_lo: 2; x = x_hi * 2 + x_lo), y: 4, z: 8, core: 2. Of those that a mesh axis runs over, the one named last changes fastest.
Arguments:
- density: bfloat16 [512, 11, 128, 128], P(('row', 'col')), as said below
- cotangent: bfloat16 [512, 11, 128, 128], P(('row', 'col')), may hold values from -6 to 6
- s_mask: int32 [512, 11], P(('row', 'col')), may hold values from 0 to 1, as said below
- t_mask: int32 [512, 11], P(('row', 'col')), may hold values from 0 to 1, as said below
Outputs:
- purified: float32 [512, 11, 128, 128], P(('row', 'col'))
- gradient: float32 [512, 11, 128, 128], P(('row', 'col'))
Inputs may be any that keep to these rules, and one draw needn't show every extreme that they name: `density`: symmetric: entry [i, a] is the transpose of entry [i + a - 5, 10 - a] wherever that row exists. `s_mask`: symmetric in the same sense, one at slot 5, zero where the block column i + a - 5 lies outside the matrix, and every one of it is also one in t_mask. `t_mask`: symmetric in the same sense, one at slot 5, zero where the block column lies outside the matrix.
All inputs are finite; a program needn't handle non-finite values.
Results may differ from a plain program's by a relative error of at most 0.0026.
Values may be sent and summed in bfloat16 or wider, within the bound.
No kernel may reach another device: no remote copies, remote signals or barrier semaphores. Data moves between devices by JAX's collectives and lax.ppermute only.
A program may use at most 384 MiB of HBM per device.

v0:
```python
import jax
import jax.numpy as jnp
from jax import lax
from jax.sharding import PartitionSpec as P

HALF = 5


def for_sending(shard):

    def short(part):
        return part.astype(jnp.bfloat16) if part.dtype == jnp.float32 else part

    return jax.tree.map(short, shard)


def from_behind(shard, axis, by):
    peers = lax.axis_size(axis)
    pairs = [(i, i + by) for i in range(peers) if 0 <= i + by < peers]
    return lax.ppermute(shard, axis, pairs)


def band_local(left_side, right_rows):
    row_count = left_side.shape[0]
    slot_count = left_side.shape[1]
    half_width = (slot_count - 1) // 2
    pieces = []
    for offset in range(slot_count):
        shift_by = offset - half_width
        window = right_rows[offset : offset + row_count]
        if shift_by >= 0:
            shifted = jnp.pad(
                window[:, : slot_count - shift_by], ((0, 0), (shift_by, 0), (0, 0), (0, 0))
            )
        else:
            shifted = jnp.pad(window[:, -shift_by:], ((0, 0), (0, -shift_by), (0, 0), (0, 0)))
        pieces.append(shifted)
    stacked = jnp.stack(pieces, axis=1)
    return jnp.einsum("reab,recbd->rcad", left_side, stacked, preferred_element_type=jnp.float32)


def extend_rows(pieces_in, depth, mover):
    row_count = pieces_in[0].shape[0]
    hop_count = -(-depth // row_count)
    below = []
    above = []
    for hop in range(hop_count, 0, -1):
        take_count = min(row_count, depth - (hop - 1) * row_count)
        below.append(mover(tuple((piece[row_count - take_count :] for piece in pieces_in)), hop))
    for hop in range(1, hop_count + 1):
        take_count = min(row_count, depth - (hop - 1) * row_count)
        above.append(mover(tuple((piece[:take_count] for piece in pieces_in)), -hop))
    joined = []
    for member in range(len(pieces_in)):
        parts_list = (
            [got[member] for got in below] + [pieces_in[member]] + [got[member] for got in above]
        )
        joined.append(jnp.concatenate(parts_list, axis=0))
    return tuple(joined)


def on_device(density, cotangent, s_mask, t_mask):
    row_count = density.shape[0]
    pattern_keep = s_mask.astype(jnp.float32)[:, :, None, None]
    trunc_keep = t_mask.astype(jnp.float32)[:, :, None, None]
    density_kept = density * s_mask.astype(jnp.bfloat16)[:, :, None, None]
    cotan_kept = cotangent * t_mask.astype(jnp.bfloat16)[:, :, None, None]

    def move_inputs(pieces, by):
        return jax.tree.map(
            lambda part, own: part.astype(own.dtype),
            from_behind(for_sending(pieces), ("row", "col"), by),
            pieces,
        )

    def move_products(pieces, by):
        return jax.tree.map(
            lambda part, own: part.astype(own.dtype),
            from_behind(for_sending(pieces), ("row", "col"), by),
            pieces,
        )

    density_near, cotan_near = extend_rows((density_kept, cotan_kept), HALF, move_inputs)
    square = band_local(density_kept, density_near) * trunc_keep
    with_cotan = band_local(density_kept, cotan_near) * trunc_keep
    grad_square = 3.0 * cotan_kept.astype(jnp.float32) - 2.0 * with_cotan
    square_b_near, grad_b_near = extend_rows(
        (square.astype(jnp.bfloat16), grad_square.astype(jnp.bfloat16)), HALF, move_products
    )
    grad_b = grad_b_near[HALF : HALF + row_count]
    cubed = band_local(density_kept, square_b_near) * trunc_keep
    purified = 3.0 * square - 2.0 * cubed
    first_term = band_local(grad_b, density_near)
    second_term = band_local(density_kept, grad_b_near)
    third_term = band_local(cotan_kept, square_b_near)
    gradient = (first_term + second_term - 2.0 * third_term) * pattern_keep
    return (purified, gradient)


def solution(mesh):
    in_specs = (
        P(("row", "col"), None, None, None),
        P(("row", "col"), None, None, None),
        P(("row", "col"), None),
        P(("row", "col"), None),
    )
    out_specs = (P(("row", "col"), None, None, None), P(("row", "col"), None, None, None))
    return jax.shard_map(
        on_device, mesh=mesh, in_specs=in_specs, out_specs=out_specs, check_vma=False
    )
```

profile of v0, /device:TPU:25, one launch (start us, length us, event | category | flops | bytes accessed | tf_op | source)
XLA Modules:
  0.0 257.3 jit_solution(13705139758200461150)
XLA Ops:
  2.3 3.1 %collective-permute-start.1 = (bf16[2,11,128,128]{2,3,1,0:T(8,128)(2,1)S(1)}, bf16[2,11,128,128]{2,3,1,0:T(8,128)(2,1)}, u32[]{:S(2)}, u32[]{:S(2)}) collective-permute-start(bf16[2,11,128,128]{2,3,1,0:T(8,128)(2,1)S(1)} %broadcast_multiply_fusion.1), channel_id=1, source_target_pairs={{0,2},{1,3},{2,4},{3,5},{4,6},{5,7},{6,8},{7,9},{8,10},{9,11},{10,... | collective-permute-start | bytes 2162696 | tf_op jit(solution)/shard_map/ppermute | solution.py:20
  5.4 4.4 %collective-permute-start.2 = (bf16[2,11,128,128]{2,3,1,0:T(8,128)(2,1)S(1)}, bf16[2,11,128,128]{2,3,1,0:T(8,128)(2,1)}, u32[]{:S(2)}, u32[]{:S(2)}) collective-permute-start(bf16[2,11,128,128]{2,3,1,0:T(8,128)(2,1)S(1)} %broadcast_multiply_fusion.1), channel_id=1, source_target_pairs={{0,1},{1,2},{2,3},{3,4},{4,5},{5,6},{6,7},{7,8},{8,9},{9,10},{10,1... | collective-permute-start | bytes 2162696 | tf_op jit(solution)/shard_map/ppermute | solution.py:20
  9.8 1.9 collective-permute-start.3
  11.7 6.9 %collective-permute-start.4 = (bf16[2,11,128,128]{2,3,1,0:T(8,128)(2,1)S(1)}, bf16[2,11,128,128]{2,3,1,0:T(8,128)(2,1)}, u32[]{:S(2)}, u32[]{:S(2)}) collective-permute-start(bf16[2,11,128,128]{2,3,1,0:T(8,128)(2,1)S(1)} %broadcast_multiply_fusion.1), channel_id=1, source_target_pairs={{2,0},{3,1},{4,2},{5,3},{6,4},{7,5},{8,6},{9,7},{10,8},{11,9},{12,... | collective-permute-start | bytes 2162696 | tf_op jit(solution)/shard_map/ppermute | solution.py:20
  23.1 24.1 %collective-permute-done.1 = bf16[2,11,128,128]{2,3,1,0:T(8,128)(2,1)} collective-permute-done((bf16[2,11,128,128]{2,3,1,0:T(8,128)(2,1)S(1)}, bf16[2,11,128,128]{2,3,1,0:T(8,128)(2,1)}, u32[]{:S(2)}, u32[]{:S(2)}) %collective-permute-start.1) | collective-permute-done | bytes 720928 | tf_op jit(solution)/shard_map/ppermute | solution.py:20
  47.2 4.2 %collective-permute-start.13 = (bf16[2,11,128,128]{2,3,1,0:T(8,128)(2,1)S(1)}, bf16[2,11,128,128]{2,3,1,0:T(8,128)(2,1)S(1)}, u32[]{:S(2)}, u32[]{:S(2)}) collective-permute-start(bf16[2,11,128,128]{2,3,1,0:T(8,128)(2,1)S(1)} %broadcast_multiply_fusion), channel_id=1, source_target_pairs={{0,2},{1,3},{2,4},{3,5},{4,6},{5,7},{6,8},{7,9},{8,10},{9,11},{10,... | collective-permute-start | bytes 2162696 | tf_op jit(solution)/shard_map/ppermute | solution.py:20
  52.5 10.2 %collective-permute-done.2 = bf16[2,11,128,128]{2,3,1,0:T(8,128)(2,1)} collective-permute-done((bf16[2,11,128,128]{2,3,1,0:T(8,128)(2,1)S(1)}, bf16[2,11,128,128]{2,3,1,0:T(8,128)(2,1)}, u32[]{:S(2)}, u32[]{:S(2)}) %collective-permute-start.2) | collective-permute-done | bytes 720928 | tf_op jit(solution)/shard_map/ppermute | solution.py:20
  62.7 4.5 %collective-permute-start.14 = (bf16[2,11,128,128]{2,3,1,0:T(8,128)(2,1)S(1)}, bf16[2,11,128,128]{2,3,1,0:T(8,128)(2,1)S(1)}, u32[]{:S(2)}, u32[]{:S(2)}) collective-permute-start(bf16[2,11,128,128]{2,3,1,0:T(8,128)(2,1)S(1)} %broadcast_multiply_fusion), channel_id=1, source_target_pairs={{0,1},{1,2},{2,3},{3,4},{4,5},{5,6},{6,7},{7,8},{8,9},{9,10},{10,1... | collective-permute-start | bytes 2162696 | tf_op jit(solution)/shard_map/ppermute | solution.py:20
  77.0 16.0 %collective-permute-start.5 = (bf16[1,11,128,128]{2,3,1,0:T(8,128)(2,1)S(1)}, bf16[1,11,128,128]{2,3,1,0:T(8,128)(2,1)S(1)}, u32[]{:S(2)}, u32[]{:S(2)}) collective-permute-start(bf16[1,11,128,128]{2,3,1,0:T(8,128)(2,1)S(1)} %copy-done.5), channel_id=1, source_target_pairs={{3,0},{4,1},{5,2},{6,3},{7,4},{8,5},{9,6},{10,7},{11,8},{12,9},{13... | collective-permute-start | bytes 1081352 | tf_op jit(solution)/shard_map/ppermute | solution.py:20
  95.5 4.2 %collective-permute-done.5 = bf16[1,11,128,128]{2,3,1,0:T(8,128)(2,1)S(1)} collective-permute-done((bf16[1,11,128,128]{2,3,1,0:T(8,128)(2,1)S(1)}, bf16[1,11,128,128]{2,3,1,0:T(8,128)(2,1)S(1)}, u32[]{:S(2)}, u32[]{:S(2)}) %collective-permute-start.5) | collective-permute-done | bytes 360480 | tf_op jit(solution)/shard_map/ppermute | solution.py:20
  99.7 3.6 %collective-permute-start.12 = (bf16[1,11,128,128]{2,3,1,0:T(8,128)(2,1)S(1)}, bf16[1,11,128,128]{2,3,1,0:T(8,128)(2,1)S(1)}, u32[]{:S(2)}, u32[]{:S(2)}) collective-permute-start(bf16[1,11,128,128]{2,3,1,0:T(8,128)(2,1)S(1)} %get-tuple-element.7), channel_id=1, source_target_pairs={{0,3},{1,4},{2,5},{3,6},{4,7},{5,8},{6,9},{7,10},{8,11},{9,12},{10... | collective-permute-start | bytes 1081352 | tf_op jit(solution)/shard_map/ppermute | solution.py:20
  104.4 2.2 fusion.8
  107.5 6.9 %collective-permute-start.17 = (bf16[1,11,128,128]{2,3,1,0:T(8,128)(2,1)S(1)}, bf16[1,11,128,128]{2,3,1,0:T(8,128)(2,1)S(1)}, u32[]{:S(2)}, u32[]{:S(2)}) collective-permute-start(bf16[1,11,128,128]{2,3,1,0:T(8,128)(2,1)S(1)} %get-tuple-element.6), channel_id=1, source_target_pairs={{3,0},{4,1},{5,2},{6,3},{7,4},{8,5},{9,6},{10,7},{11,8},{12,9},{13... | collective-permute-start | bytes 1081352 | tf_op jit(solution)/shard_map/ppermute | solution.py:20
  114.6 7.2 %collective-permute-done.14 = bf16[2,11,128,128]{2,3,1,0:T(8,128)(2,1)S(1)} collective-permute-done((bf16[2,11,128,128]{2,3,1,0:T(8,128)(2,1)S(1)}, bf16[2,11,128,128]{2,3,1,0:T(8,128)(2,1)S(1)}, u32[]{:S(2)}, u32[]{:S(2)}) %collective-permute-start.14) | collective-permute-done | bytes 720928 | tf_op jit(solution)/shard_map/ppermute | solution.py:20
  123.7 4.4 %collective-permute-start.8 = (bf16[2,11,128,128]{2,3,1,0:T(8,128)(2,1)S(1)}, bf16[2,11,128,128]{2,3,1,0:T(8,128)(2,1)S(1)}, u32[]{:S(2)}, u32[]{:S(2)}) collective-permute-start(bf16[2,11,128,128]{2,3,1,0:T(8,128)(2,1)S(1)} %convert_bitcast_fusion), channel_id=1, source_target_pairs={{0,1},{1,2},{2,3},{3,4},{4,5},{5,6},{6,7},{7,8},{8,9},{9,10},{10,1... | collective-permute-start | bytes 2162696 | tf_op jit(solution)/shard_map/ppermute | solution.py:20
  128.5 2.4 collective-permute-start.9
  131.8 7.5 %collective-permute-start.10 = (bf16[2,11,128,128]{2,3,1,0:T(8,128)(2,1)S(1)}, bf16[2,11,128,128]{2,3,1,0:T(8,128)(2,1)S(1)}, u32[]{:S(2)}, u32[]{:S(2)}) collective-permute-start(bf16[2,11,128,128]{2,3,1,0:T(8,128)(2,1)S(1)} %convert_bitcast_fusion), channel_id=1, source_target_pairs={{2,0},{3,1},{4,2},{5,3},{6,4},{7,5},{8,6},{9,7},{10,8},{11,9},{12,... | collective-permute-start | bytes 2162696 | tf_op jit(solution)/shard_map/ppermute | solution.py:20
  139.7 4.8 %collective-permute-start.6 = (bf16[1,11,128,128]{2,3,1,0:T(8,128)(2,1)S(1)}, bf16[1,11,128,128]{2,3,1,0:T(8,128)(2,1)S(1)}, u32[]{:S(2)}, u32[]{:S(2)}) collective-permute-start(bf16[1,11,128,128]{2,3,1,0:T(8,128)(2,1)S(1)} %get-tuple-element.9), channel_id=1, source_target_pairs={{0,3},{1,4},{2,5},{3,6},{4,7},{5,8},{6,9},{7,10},{8,11},{9,12},{10... | collective-permute-start | bytes 1081352 | tf_op jit(solution)/shard_map/ppermute | solution.py:20
  144.7 2.3 fusion.2
  148.3 16.1 %collective-permute-done.7 = bf16[2,11,128,128]{2,3,1,0:T(8,128)(2,1)S(1)} collective-permute-done((bf16[2,11,128,128]{2,3,1,0:T(8,128)(2,1)S(1)}, bf16[2,11,128,128]{2,3,1,0:T(8,128)(2,1)S(1)}, u32[]{:S(2)}, u32[]{:S(2)}) %collective-permute-start.7) | collective-permute-done | bytes 720928 | tf_op jit(solution)/shard_map/ppermute | solution.py:20
  164.5 4.8 %collective-permute-start.19 = (bf16[2,11,128,128]{2,3,1,0:T(8,128)(2,1)S(1)}, bf16[2,11,128,128]{2,3,1,0:T(8,128)(2,1)}, u32[]{:S(2)}, u32[]{:S(2)}) collective-permute-start(bf16[2,11,128,128]{2,3,1,0:T(8,128)(2,1)S(1)} %fusion.60), channel_id=1, source_target_pairs={{0,2},{1,3},{2,4},{3,5},{4,6},{5,7},{6,8},{7,9},{8,10},{9,11},{10,... | collective-permute-start | bytes 2162696 | tf_op jit(solution)/shard_map/ppermute | solution.py:20
  170.5 2.4 collective-permute-start.20
  173.2 8.5 %collective-permute-done.8 = bf16[2,11,128,128]{2,3,1,0:T(8,128)(2,1)S(1)} collective-permute-done((bf16[2,11,128,128]{2,3,1,0:T(8,128)(2,1)S(1)}, bf16[2,11,128,128]{2,3,1,0:T(8,128)(2,1)S(1)}, u32[]{:S(2)}, u32[]{:S(2)}) %collective-permute-start.8) | collective-permute-done | bytes 720928 | tf_op jit(solution)/shard_map/ppermute | solution.py:20
  183.8 2.6 %collective-permute-start.22 = (bf16[2,11,128,128]{2,3,1,0:T(8,128)(2,1)S(1)}, bf16[2,11,128,128]{2,3,1,0:T(8,128)(2,1)}, u32[]{:S(2)}, u32[]{:S(2)}) collective-permute-start(bf16[2,11,128,128]{2,3,1,0:T(8,128)(2,1)S(1)} %fusion.60), channel_id=1, source_target_pairs={{2,0},{3,1},{4,2},{5,3},{6,4},{7,5},{8,6},{9,7},{10,8},{11,9},{12,... | collective-permute-start | bytes 2162696 | tf_op jit(solution)/shard_map/ppermute | solution.py:20
  187.1 27.0 %collective-permute-start.11 = (bf16[1,11,128,128]{2,3,1,0:T(8,128)(2,1)S(1)}, bf16[1,11,128,128]{2,3,1,0:T(8,128)(2,1)S(1)}, u32[]{:S(2)}, u32[]{:S(2)}) collective-permute-start(bf16[1,11,128,128]{2,3,1,0:T(8,128)(2,1)S(1)} %get-tuple-element.8), channel_id=1, source_target_pairs={{3,0},{4,1},{5,2},{6,3},{7,4},{8,5},{9,6},{10,7},{11,8},{12,9},{13... | collective-permute-start | bytes 1081352 | tf_op jit(solution)/shard_map/ppermute | solution.py:20
  214.5 5.4 %collective-permute-done.11 = bf16[1,11,128,128]{2,3,1,0:T(8,128)(2,1)S(1)} collective-permute-done((bf16[1,11,128,128]{2,3,1,0:T(8,128)(2,1)S(1)}, bf16[1,11,128,128]{2,3,1,0:T(8,128)(2,1)S(1)}, u32[]{:S(2)}, u32[]{:S(2)}) %collective-permute-start.11) | collective-permute-done | bytes 360480 | tf_op jit(solution)/shard_map/ppermute | solution.py:20
  222.1 2.3 fusion.6
  226.5 2.9 %copy.29 = f32[2,11,128,128]{3,2,1,0:T(8,128)} copy(f32[2,11,128,128]{2,3,1,0:T(8,128)} %fusion.64) | data formatting | bytes 2883584
  229.4 8.6 %collective-permute-start.23 = (bf16[1,11,128,128]{2,3,1,0:T(8,128)(2,1)}, bf16[1,11,128,128]{2,3,1,0:T(8,128)(2,1)S(1)}, u32[]{:S(2)}, u32[]{:S(2)}) collective-permute-start(bf16[1,11,128,128]{2,3,1,0:T(8,128)(2,1)} %get-tuple-element.4), channel_id=1, source_target_pairs={{3,0},{4,1},{5,2},{6,3},{7,4},{8,5},{9,6},{10,7},{11,8},{12,9},{13... | collective-permute-start | bytes 1081352 | tf_op jit(solution)/shard_map/ppermute | solution.py:20
  245.0 2.3 fusion.4
  251.0 2.3 fusion
  253.4 2.3 fusion.59
  (127 shorter events, 47.2 us)
Async XLA Ops:
  2.3 20.6 %copy-start.8 = (s32[2,11]{1,0:T(2,128)S(1)}, s32[2,11]{1,0:T(2,128)}, u32[]{:S(2)}) copy-start(s32[2,11]{1,0:T(2,128)} %param.7) | copy-start | bytes 268
  2.3 44.9 %collective-permute-start.1 = (bf16[2,11,128,128]{2,3,1,0:T(8,128)(2,1)S(1)}, bf16[2,11,128,128]{2,3,1,0:T(8,128)(2,1)}, u32[]{:S(2)}, u32[]{:S(2)}) collective-permute-start(bf16[2,11,128,128]{2,3,1,0:T(8,128)(2,1)S(1)} %broadcast_multiply_fusion.1), channel_id=1, source_target_pairs={{0,2},{1,3},{2,4},{3,5},{4,6},{5,7},{6,8},{7,9},{8,10},{9,11},{10,... | collective-permute-start | bytes 2162696 | tf_op jit(solution)/shard_map/ppermute | solution.py:20
  5.4 57.3 %collective-permute-start.2 = (bf16[2,11,128,128]{2,3,1,0:T(8,128)(2,1)S(1)}, bf16[2,11,128,128]{2,3,1,0:T(8,128)(2,1)}, u32[]{:S(2)}, u32[]{:S(2)}) collective-permute-start(bf16[2,11,128,128]{2,3,1,0:T(8,128)(2,1)S(1)} %broadcast_multiply_fusion.1), channel_id=1, source_target_pairs={{0,1},{1,2},{2,3},{3,4},{4,5},{5,6},{6,7},{7,8},{8,9},{9,10},{10,1... | collective-permute-start | bytes 2162696 | tf_op jit(solution)/shard_map/ppermute | solution.py:20
  9.8 61.6 %collective-permute-start.3 = (bf16[2,11,128,128]{2,3,1,0:T(8,128)(2,1)S(1)}, bf16[2,11,128,128]{2,3,1,0:T(8,128)(2,1)S(1)}, u32[]{:S(2)}, u32[]{:S(2)}) collective-permute-start(bf16[2,11,128,128]{2,3,1,0:T(8,128)(2,1)S(1)} %broadcast_multiply_fusion.1), channel_id=1, source_target_pairs={{1,0},{2,1},{3,2},{4,3},{5,4},{6,5},{7,6},{8,7},{9,8},{10,9},{11,1... | collective-permute-start | bytes 2162696 | tf_op jit(solution)/shard_map/ppermute | solution.py:20
  11.7 64.5 %collective-permute-start.4 = (bf16[2,11,128,128]{2,3,1,0:T(8,128)(2,1)S(1)}, bf16[2,11,128,128]{2,3,1,0:T(8,128)(2,1)}, u32[]{:S(2)}, u32[]{:S(2)}) collective-permute-start(bf16[2,11,128,128]{2,3,1,0:T(8,128)(2,1)S(1)} %broadcast_multiply_fusion.1), channel_id=1, source_target_pairs={{2,0},{3,1},{4,2},{5,3},{6,4},{7,5},{8,6},{9,7},{10,8},{11,9},{12,... | collective-permute-start | bytes 2162696 | tf_op jit(solution)/shard_map/ppermute | solution.py:20
  19.5 48.8 %collective-permute-start = (bf16[1,11,128,128]{2,3,1,0:T(8,128)(2,1)}, bf16[1,11,128,128]{2,3,1,0:T(8,128)(2,1)S(1)}, u32[]{:S(2)}, u32[]{:S(2)}) collective-permute-start(bf16[1,11,128,128]{2,3,1,0:T(8,128)(2,1)} %get-tuple-element.11), channel_id=1, source_target_pairs={{0,3},{1,4},{2,5},{3,6},{4,7},{5,8},{6,9},{7,10},{8,11},{9,12},{10... | collective-permute-start | bytes 1081352 | tf_op jit(solution)/shard_map/ppermute | solution.py:20
  47.2 60.3 %collective-permute-start.13 = (bf16[2,11,128,128]{2,3,1,0:T(8,128)(2,1)S(1)}, bf16[2,11,128,128]{2,3,1,0:T(8,128)(2,1)S(1)}, u32[]{:S(2)}, u32[]{:S(2)}) collective-permute-start(bf16[2,11,128,128]{2,3,1,0:T(8,128)(2,1)S(1)} %broadcast_multiply_fusion), channel_id=1, source_target_pairs={{0,2},{1,3},{2,4},{3,5},{4,6},{5,7},{6,8},{7,9},{8,10},{9,11},{10,... | collective-permute-start | bytes 2162696 | tf_op jit(solution)/shard_map/ppermute | solution.py:20
  62.7 59.1 %collective-permute-start.14 = (bf16[2,11,128,128]{2,3,1,0:T(8,128)(2,1)S(1)}, bf16[2,11,128,128]{2,3,1,0:T(8,128)(2,1)S(1)}, u32[]{:S(2)}, u32[]{:S(2)}) collective-permute-start(bf16[2,11,128,128]{2,3,1,0:T(8,128)(2,1)S(1)} %broadcast_multiply_fusion), channel_id=1, source_target_pairs={{0,1},{1,2},{2,3},{3,4},{4,5},{5,6},{6,7},{7,8},{8,9},{9,10},{10,1... | collective-permute-start | bytes 2162696 | tf_op jit(solution)/shard_map/ppermute | solution.py:20
  68.3 60.2 %collective-permute-start.15 = (bf16[2,11,128,128]{2,3,1,0:T(8,128)(2,1)S(1)}, bf16[2,11,128,128]{2,3,1,0:T(8,128)(2,1)S(1)}, u32[]{:S(2)}, u32[]{:S(2)}) collective-permute-start(bf16[2,11,128,128]{2,3,1,0:T(8,128)(2,1)S(1)} %broadcast_multiply_fusion), channel_id=1, source_target_pairs={{1,0},{2,1},{3,2},{4,3},{5,4},{6,5},{7,6},{8,7},{9,8},{10,9},{11,1... | collective-permute-start | bytes 2162696 | tf_op jit(solution)/shard_map/ppermute | solution.py:20
  71.4 60.4 %collective-permute-start.16 = (bf16[2,11,128,128]{2,3,1,0:T(8,128)(2,1)S(1)}, bf16[2,11,128,128]{2,3,1,0:T(8,128)(2,1)S(1)}, u32[]{:S(2)}, u32[]{:S(2)}) collective-permute-start(bf16[2,11,128,128]{2,3,1,0:T(8,128)(2,1)S(1)} %broadcast_multiply_fusion), channel_id=1, source_target_pairs={{2,0},{3,1},{4,2},{5,3},{6,4},{7,5},{8,6},{9,7},{10,8},{11,9},{12,... | collective-permute-start | bytes 2162696 | tf_op jit(solution)/shard_map/ppermute | solution.py:20
  77.0 22.6 %collective-permute-start.5 = (bf16[1,11,128,128]{2,3,1,0:T(8,128)(2,1)S(1)}, bf16[1,11,128,128]{2,3,1,0:T(8,128)(2,1)S(1)}, u32[]{:S(2)}, u32[]{:S(2)}) collective-permute-start(bf16[1,11,128,128]{2,3,1,0:T(8,128)(2,1)S(1)} %copy-done.5), channel_id=1, source_target_pairs={{3,0},{4,1},{5,2},{6,3},{7,4},{8,5},{9,6},{10,7},{11,8},{12,9},{13... | collective-permute-start | bytes 1081352 | tf_op jit(solution)/shard_map/ppermute | solution.py:20
  99.7 24.0 %collective-permute-start.12 = (bf16[1,11,128,128]{2,3,1,0:T(8,128)(2,1)S(1)}, bf16[1,11,128,128]{2,3,1,0:T(8,128)(2,1)S(1)}, u32[]{:S(2)}, u32[]{:S(2)}) collective-permute-start(bf16[1,11,128,128]{2,3,1,0:T(8,128)(2,1)S(1)} %get-tuple-element.7), channel_id=1, source_target_pairs={{0,3},{1,4},{2,5},{3,6},{4,7},{5,8},{6,9},{7,10},{8,11},{9,12},{10... | collective-permute-start | bytes 1081352 | tf_op jit(solution)/shard_map/ppermute | solution.py:20
  104.4 3.1 %copy-start = (bf16[2,11,11,128,128]{3,4,1,2,0:T(8,128)(2,1)}, bf16[2,11,11,128,128]{3,4,1,2,0:T(8,128)(2,1)S(1)}, u32[]{:S(2)}) copy-start(bf16[2,11,11,128,128]{3,4,1,2,0:T(8,128)(2,1)S(1)} %fusion.127) | copy-start | bytes 23789572
  107.5 32.2 %collective-permute-start.17 = (bf16[1,11,128,128]{2,3,1,0:T(8,128)(2,1)S(1)}, bf16[1,11,128,128]{2,3,1,0:T(8,128)(2,1)S(1)}, u32[]{:S(2)}, u32[]{:S(2)}) collective-permute-start(bf16[1,11,128,128]{2,3,1,0:T(8,128)(2,1)S(1)} %get-tuple-element.6), channel_id=1, source_target_pairs={{3,0},{4,1},{5,2},{6,3},{7,4},{8,5},{9,6},{10,7},{11,8},{12,9},{13... | collective-permute-start | bytes 1081352 | tf_op jit(solution)/shard_map/ppermute | solution.py:20
  121.7 6.6 %copy-start.1 = (bf16[2,11,128,128]{2,3,1,0:T(8,128)(2,1)}, bf16[2,11,128,128]{2,3,1,0:T(8,128)(2,1)S(1)}, u32[]{:S(2)}) copy-start(bf16[2,11,128,128]{2,3,1,0:T(8,128)(2,1)S(1)} %collective-permute-done.14) | copy-start | bytes 2162692
  121.7 42.7 %collective-permute-start.7 = (bf16[2,11,128,128]{2,3,1,0:T(8,128)(2,1)S(1)}, bf16[2,11,128,128]{2,3,1,0:T(8,128)(2,1)S(1)}, u32[]{:S(2)}, u32[]{:S(2)}) collective-permute-start(bf16[2,11,128,128]{2,3,1,0:T(8,128)(2,1)S(1)} %convert_bitcast_fusion), channel_id=1, source_target_pairs={{0,2},{1,3},{2,4},{3,5},{4,6},{5,7},{6,8},{7,9},{8,10},{9,11},{10,... | collective-permute-start | bytes 2162696 | tf_op jit(solution)/shard_map/ppermute | solution.py:20
  123.7 58.0 %collective-permute-start.8 = (bf16[2,11,128,128]{2,3,1,0:T(8,128)(2,1)S(1)}, bf16[2,11,128,128]{2,3,1,0:T(8,128)(2,1)S(1)}, u32[]{:S(2)}, u32[]{:S(2)}) collective-permute-start(bf16[2,11,128,128]{2,3,1,0:T(8,128)(2,1)S(1)} %convert_bitcast_fusion), channel_id=1, source_target_pairs={{0,1},{1,2},{2,3},{3,4},{4,5},{5,6},{6,7},{7,8},{8,9},{9,10},{10,1... | collective-permute-start | bytes 2162696 | tf_op jit(solution)/shard_map/ppermute | solution.py:20
  128.5 55.3 %collective-permute-start.9 = (bf16[2,11,128,128]{2,3,1,0:T(8,128)(2,1)S(1)}, bf16[2,11,128,128]{2,3,1,0:T(8,128)(2,1)S(1)}, u32[]{:S(2)}, u32[]{:S(2)}) collective-permute-start(bf16[2,11,128,128]{2,3,1,0:T(8,128)(2,1)S(1)} %convert_bitcast_fusion), channel_id=1, source_target_pairs={{1,0},{2,1},{3,2},{4,3},{5,4},{6,5},{7,6},{8,7},{9,8},{10,9},{11,1... | collective-permute-start | bytes 2162696 | tf_op jit(solution)/shard_map/ppermute | solution.py:20
  131.8 55.3 %collective-permute-start.10 = (bf16[2,11,128,128]{2,3,1,0:T(8,128)(2,1)S(1)}, bf16[2,11,128,128]{2,3,1,0:T(8,128)(2,1)S(1)}, u32[]{:S(2)}, u32[]{:S(2)}) collective-permute-start(bf16[2,11,128,128]{2,3,1,0:T(8,128)(2,1)S(1)} %convert_bitcast_fusion), channel_id=1, source_target_pairs={{2,0},{3,1},{4,2},{5,3},{6,4},{7,5},{8,6},{9,7},{10,8},{11,9},{12,... | collective-permute-start | bytes 2162696 | tf_op jit(solution)/shard_map/ppermute | solution.py:20
  139.7 30.8 %collective-permute-start.6 = (bf16[1,11,128,128]{2,3,1,0:T(8,128)(2,1)S(1)}, bf16[1,11,128,128]{2,3,1,0:T(8,128)(2,1)S(1)}, u32[]{:S(2)}, u32[]{:S(2)}) collective-permute-start(bf16[1,11,128,128]{2,3,1,0:T(8,128)(2,1)S(1)} %get-tuple-element.9), channel_id=1, source_target_pairs={{0,3},{1,4},{2,5},{3,6},{4,7},{5,8},{6,9},{7,10},{8,11},{9,12},{10... | collective-permute-start | bytes 1081352 | tf_op jit(solution)/shard_map/ppermute | solution.py:20
  164.5 64.9 %collective-permute-start.19 = (bf16[2,11,128,128]{2,3,1,0:T(8,128)(2,1)S(1)}, bf16[2,11,128,128]{2,3,1,0:T(8,128)(2,1)}, u32[]{:S(2)}, u32[]{:S(2)}) collective-permute-start(bf16[2,11,128,128]{2,3,1,0:T(8,128)(2,1)S(1)} %fusion.60), channel_id=1, source_target_pairs={{0,2},{1,3},{2,4},{3,5},{4,6},{5,7},{6,8},{7,9},{8,10},{9,11},{10,... | collective-permute-start | bytes 2162696 | tf_op jit(solution)/shard_map/ppermute | solution.py:20
  170.5 69.7 %collective-permute-start.20 = (bf16[2,11,128,128]{2,3,1,0:T(8,128)(2,1)S(1)}, bf16[2,11,128,128]{2,3,1,0:T(8,128)(2,1)}, u32[]{:S(2)}, u32[]{:S(2)}) collective-permute-start(bf16[2,11,128,128]{2,3,1,0:T(8,128)(2,1)S(1)} %fusion.60), channel_id=1, source_target_pairs={{0,1},{1,2},{2,3},{3,4},{4,5},{5,6},{6,7},{7,8},{8,9},{9,10},{10,1... | collective-permute-start | bytes 2162696 | tf_op jit(solution)/shard_map/ppermute | solution.py:20
  181.7 62.7 %collective-permute-start.21 = (bf16[2,11,128,128]{2,3,1,0:T(8,128)(2,1)S(1)}, bf16[2,11,128,128]{2,3,1,0:T(8,128)(2,1)S(1)}, u32[]{:S(2)}, u32[]{:S(2)}) collective-permute-start(bf16[2,11,128,128]{2,3,1,0:T(8,128)(2,1)S(1)} %fusion.60), channel_id=1, source_target_pairs={{1,0},{2,1},{3,2},{4,3},{5,4},{6,5},{7,6},{8,7},{9,8},{10,9},{11,1... | collective-permute-start | bytes 2162696 | tf_op jit(solution)/shard_map/ppermute | solution.py:20
  183.8 2.7 %slice-start.3 = ((bf16[2,11,128,128]{2,3,1,0:T(8,128)(2,1)}), bf16[2,9,128,128]{2,3,1,0:T(8,128)(2,1)S(1)}, s32[]{:S(2)}) async-start(bf16[2,11,128,128]{2,3,1,0:T(8,128)(2,1)} %copy-done.3), calls=%async_computation.3 | async-start | bytes 1179648 | tf_op jit(solution)/shard_map/slice | solution.py:36
  183.8 2.9 %copy-start.4 = (bf16[2,11,128,128]{2,3,1,0:T(8,128)(2,1)S(1)}, bf16[2,11,128,128]{2,3,1,0:T(8,128)(2,1)}, u32[]{:S(2)}) copy-start(bf16[2,11,128,128]{2,3,1,0:T(8,128)(2,1)} %copy-done.3) | copy-start | bytes 2162692
  183.8 63.5 %collective-permute-start.22 = (bf16[2,11,128,128]{2,3,1,0:T(8,128)(2,1)S(1)}, bf16[2,11,128,128]{2,3,1,0:T(8,128)(2,1)}, u32[]{:S(2)}, u32[]{:S(2)}) collective-permute-start(bf16[2,11,128,128]{2,3,1,0:T(8,128)(2,1)S(1)} %fusion.60), channel_id=1, source_target_pairs={{2,0},{3,1},{4,2},{5,3},{6,4},{7,5},{8,6},{9,7},{10,8},{11,9},{12,... | collective-permute-start | bytes 2162696 | tf_op jit(solution)/shard_map/ppermute | solution.py:20
  187.1 32.8 %collective-permute-start.11 = (bf16[1,11,128,128]{2,3,1,0:T(8,128)(2,1)S(1)}, bf16[1,11,128,128]{2,3,1,0:T(8,128)(2,1)S(1)}, u32[]{:S(2)}, u32[]{:S(2)}) collective-permute-start(bf16[1,11,128,128]{2,3,1,0:T(8,128)(2,1)S(1)} %get-tuple-element.8), channel_id=1, source_target_pairs={{3,0},{4,1},{5,2},{6,3},{7,4},{8,5},{9,6},{10,7},{11,8},{12,9},{13... | collective-permute-start | bytes 1081352 | tf_op jit(solution)/shard_map/ppermute | solution.py:20
  220.0 19.1 %collective-permute-start.18 = (bf16[1,11,128,128]{2,3,1,0:T(8,128)(2,1)}, bf16[1,11,128,128]{2,3,1,0:T(8,128)(2,1)S(1)}, u32[]{:S(2)}, u32[]{:S(2)}) collective-permute-start(bf16[1,11,128,128]{2,3,1,0:T(8,128)(2,1)} %get-tuple-element.5), channel_id=1, source_target_pairs={{0,3},{1,4},{2,5},{3,6},{4,7},{5,8},{6,9},{7,10},{8,11},{9,12},{10... | collective-permute-start | bytes 1081352 | tf_op jit(solution)/shard_map/ppermute | solution.py:20
  222.0 3.1 %copy-start.6 = (bf16[2,11,11,128,128]{3,4,2,0,1:T(8,128)(2,1)}, bf16[2,11,11,128,128]{3,4,2,0,1:T(8,128)(2,1)S(1)}, u32[]{:S(2)}) copy-start(bf16[2,11,11,128,128]{3,4,2,0,1:T(8,128)(2,1)S(1)} %fusion.130) | copy-start | bytes 23789572
  229.4 20.4 %collective-permute-start.23 = (bf16[1,11,128,128]{2,3,1,0:T(8,128)(2,1)}, bf16[1,11,128,128]{2,3,1,0:T(8,128)(2,1)S(1)}, u32[]{:S(2)}, u32[]{:S(2)}) collective-permute-start(bf16[1,11,128,128]{2,3,1,0:T(8,128)(2,1)} %get-tuple-element.4), channel_id=1, source_target_pairs={{3,0},{4,1},{5,2},{6,3},{7,4},{8,5},{9,6},{10,7},{11,8},{12,9},{13... | collective-permute-start | bytes 1081352 | tf_op jit(solution)/shard_map/ppermute | solution.py:20
  239.1 5.5 %slice-start.4 = ((s8[7929856]{0:T(1024)(128)(4,1)}), s8[4194304]{0:T(1024)(128)(4,1)S(1)}, s32[]{:S(2)}) async-start(s8[7929856]{0:T(1024)(128)(4,1)} %bitcast.231), calls=%async_computation.4 | async-start | bytes 8388608
  249.8 3.5 %slice-start = ((s8[7929856]{0:T(1024)(128)(4,1)}), s8[4194304]{0:T(1024)(128)(4,1)S(1)}, s32[]{:S(2)}) async-start(s8[7929856]{0:T(1024)(128)(4,1)} %bitcast.229), calls=%async_computation | async-start | bytes 8388608
  (7 other events, 14.3 us)
where the time goes:
time: 260 us; the launch traced here: 257 us
  starting transfers between devices  128 us (49%)
  waiting for transfers between devices  77 us (30%)
  local copies, waits for them, and re-layouts  21.6 us (8%)
  other arithmetic  15.8 us (6%)
  matrix products  13.8 us (5%)
    ppermute x24, starting transfers between devices, from_behind(): return lax.ppermute(shard, axis, pairs)  128 us
    ppermute x24, waiting for transfers between devices, from_behind(): return lax.ppermute(shard, axis, pairs)  77 us
    dot_general x6, matrix products, band_local(): jnp.einsum('reab,recbd->rcad', left_side, stacked, preferred_element_type...  13.8 us
    unnamed x47, local copies, waits for them, and re-layouts  12.7 us
    unnamed x25, other arithmetic  11.1 us
  transfers between devices with their start and end apart: 24, of which 8 were waited for; matrix products, arithmetic and copies ran while one was open for 15% of the time, Pallas kernels for 0%

commit v1 on v0

v1 whole, which is shorter than its diff:
```python
import functools

import jax
import jax.numpy as jnp
from jax import lax
from jax.experimental import pallas as pl
from jax.experimental.pallas import tpu as pltpu
from jax.sharding import PartitionSpec as P

B = 128
HALF = 5
SLOTS = 11
AXES = ("row", "col")
MASK_ROWS = 32
BF16 = jnp.bfloat16
F32 = jnp.float32

NEAR2, FAR2, NEAR4, FAR4, NEAR6 = (1, 2), (3, 4), (5, 6), (7, 8), (9, 10)
P_BLOCKS = {NEAR2: 13, FAR2: 12, NEAR4: 6}
G_PAIRS = (NEAR2, FAR2, NEAR4, FAR4, NEAR6)


def g_blocks(pair):
    return sum(SLOTS - t for t in pair)


def is_near(pair):
    return pair in (NEAR2, NEAR4, NEAR6)


def hop(pair):
    return {NEAR2: 2, FAR2: 2, NEAR4: 4, FAR4: 4, NEAR6: 6}[pair]


def route(pair, devices):
    pairs = []
    for source in range(devices):
        up = (source % 2 == 1) == is_near(pair)
        target = source + hop(pair) if up else source - hop(pair)
        if 0 <= target < devices:
            pairs.append((source, target))
    return pairs


def rows_of(block):
    start = block * B
    if not isinstance(start, int):
        start = pl.multiple_of(start, B)
    return pl.ds(start, B)


def masked(values_ref, mask_ref, row, slot):
    keep = mask_ref[row, slot].astype(F32)
    return (values_ref[row, slot].astype(F32) * keep).astype(BF16)


def pack_density(core_ref, s_ref, t_ref, density_ref, own_ref, near2_ref, far2_ref, near4_ref):
    q = core_ref[0]
    o = 1 - q

    def put(out_ref, at, row, slot):
        out_ref[rows_of(at), :] = masked(density_ref, s_ref, row, slot)

    for s in range(6):
        put(near2_ref, s, q, 5 * o + s)
        put(near2_ref, 6 + s, o, 5 * o + s)
        put(far2_ref, s, o, 5 * q + s)
        put(far2_ref, 6 + s, q, 5 * q + s)
        put(near4_ref, s, q, 5 * o + s)
    put(near2_ref, 12, q, 10 * q)
    for row in range(2):
        for slot in range(SLOTS):
            put(own_ref, row * SLOTS + slot, row, slot)
    line = lax.broadcasted_iota(jnp.int32, (MASK_ROWS, B), 0)
    mask = jnp.zeros((MASK_ROWS, B), F32)
    for row in range(2):
        for slot in range(SLOTS):
            mask = jnp.where(line == row * 16 + slot + 2, t_ref[row, slot].astype(F32), mask)
    mask = mask.astype(BF16)
    for out_ref, count in ((own_ref, 22), (near2_ref, 13), (far2_ref, 12), (near4_ref, 6)):
        out_ref[pl.ds(count * B, MASK_ROWS), :] = mask


def pack_cotangent(core_ref, t_ref, cotangent_ref, own_ref, *out_refs):
    q = core_ref[0]
    o = 1 - q
    for pair, out_ref in zip(G_PAIRS, out_refs):
        up = q if is_near(pair) else o
        at = 0
        for place, t in enumerate(pair):
            row = up if place == 0 else 1 - up
            for s in range(SLOTS - t):
                out_ref[rows_of(at), :] = masked(cotangent_ref, t_ref, row, t * up + s)
                at += 1
    for row in range(2):
        for slot in range(SLOTS):
            own_ref[rows_of(row * SLOTS + slot), :] = masked(cotangent_ref, t_ref, row, slot)


def fetch(copies):
    for copy in copies:
        copy.start()
    for copy in copies:
        copy.wait()


def tile_loop(body):
    for delta in range(-3, 4):
        body_of = functools.partial(body, delta)

        def step(index, carry, body_of=body_of, first=max(0, -delta)):
            body_of(index + first)
            return carry

        lax.fori_loop(0, 6 - abs(delta), step, 0)


def mask_tile(t_ref, first_k, first_j, height):
    rows = []
    for k in range(height):
        pieces = []
        for j in range(2):
            line = (first_k + k) * 16 + (first_j + j) - (first_k + k) + HALF + 2
            pieces.append(jnp.broadcast_to(t_ref[pl.ds(line, 1), :], (B, B)))
        rows.append(jnp.concatenate(pieces, axis=1))
    return jnp.concatenate(rows, axis=0)


def span(j0):
    low = max(0, j0 - 5)
    high = min(11, j0 + 6)
    return low, high - low + 1


NT = (((1,), (1,)), ((), ()))


def square_kernel(
    core_ref, own_p, mate_p, n2_r, n2_x, f2_r, f2_x, n4_r, n4_x, own_g,
    purified_ref, third_ref, pk_ref, t_out_ref,
    row_s, n2_s, f2_s, n4_s, g_s, sw, lhs, t_ref, sems,
):
    p = core_ref[0]
    o = 1 - p
    plan = (
        (own_p, row_s.at[p]), (mate_p, row_s.at[o]),
        (n2_r, n2_s.at[o]), (n2_x, n2_s.at[p]),
        (f2_r, f2_s.at[p]), (f2_x, f2_s.at[o]),
        (n4_r, n4_s.at[o]), (n4_x, n4_s.at[p]),
        (own_g, g_s),
    )
    fetch([pltpu.make_async_copy(a, b, sems.at[i]) for i, (a, b) in enumerate(plan)])

    def held(k, slot):
        if 5 <= k <= 8:
            return row_s[(k - 5) // 2, rows_of(((k - 5) % 2) * SLOTS + slot), :]
        side = 0 if k < 5 else 1
        t = 5 - k if k < 5 else k - 8
        at = slot if k < 5 else slot - 5
        if t <= 2:
            return n2_s[side, rows_of(6 * (t - 1) + at), :]
        if t <= 4:
            return f2_s[side, rows_of(6 * (t - 3) + at), :]
        return n4_s[side, rows_of(at), :]

    def block(k, slot):
        if 5 <= k <= 8 or (k < 5 and slot <= 5) or (k > 8 and slot >= 5):
            return held(k, slot)
        if (k, slot) == (4, 10):
            return n2_s[0, rows_of(12), :]
        if (k, slot) == (9, 0):
            return n2_s[1, rows_of(12), :]
        return held(k + slot - 5, 10 - slot).T

    zero = jnp.zeros((B, B), BF16)
    for pair in range(7):
        for e in range(2):
            rows = pl.ds(e * B, B)
            pk_ref[pair, rows, pl.ds((11 if e == 0 else 0) * B, B)] = zero
            for slot in range(SLOTS):
                pk_ref[pair, rows, pl.ds((slot + e) * B, B)] = block(2 * pair + e, slot)

    for k in range(14):
        if 5 <= k <= 8:
            part = row_s[(k - 5) // 2, pl.ds(22 * B, MASK_ROWS), :]
            r = (k - 5) % 2
        else:
            side = 0 if k < 5 else 1
            t = 5 - k if k < 5 else k - 8
            r = (t % 2) if side == 0 else (1 - t % 2)
            if t <= 2:
                part = n2_s[side, pl.ds(13 * B, MASK_ROWS), :]
            elif t <= 4:
                part = f2_s[side, pl.ds(12 * B, MASK_ROWS), :]
            else:
                part = n4_s[side, pl.ds(6 * B, MASK_ROWS), :]
        t_ref[pl.ds(k * 16, 16), :] = part.astype(F32)[r * 16 : r * 16 + 16, :]
    t_out_ref[...] = t_ref[...]

    for r in range(2):
        hole = pl.ds((11 if r == 0 else 0) * B, B)
        lhs[pl.ds(r * B, B), hole] = zero
        lhs[pl.ds((2 + r) * B, B), hole] = zero
        for slot in range(SLOTS):
            cols = pl.ds((slot + r) * B, B)
            lhs[pl.ds(r * B, B), cols] = row_s[p, rows_of(r * SLOTS + slot), :]
            lhs[pl.ds((2 + r) * B, B), cols] = g_s[rows_of(r * SLOTS + slot), :]

    def tile(delta, j):
        k = j + delta
        count = (12 - 2 * abs(delta)) * B
        left = pk_ref[k + p, :, pl.ds(max(0, -delta) * 2 * B, count)]
        right = pk_ref[j + p, :, pl.ds(max(0, delta) * 2 * B, count)]
        found = lax.dot_general(left, right, NT, preferred_element_type=F32)
        found = found * mask_tile(t_ref, 2 * (k + p), 2 * (j + p), 2)
        sw[pl.ds(pl.multiple_of(k * 256, 256), 256), pl.ds(pl.multiple_of(j * 256, 256), 256)] = (
            found.astype(BF16)
        )

    tile_loop(tile)

    for j in range(6):
        low, count = span(2 * j)
        cols = pl.ds(low * B, count * B)
        right = pk_ref[j + p, :, pl.ds((low + 5 - 2 * j) * B, count * B)]
        square = lax.dot_general(lhs[pl.ds(0, 256), cols], right, NT, preferred_element_type=F32)
        both = jnp.dot(
            lhs[:, cols], sw[pl.ds(low * B, count * B), pl.ds(j * 256, 256)],
            preferred_element_type=F32,
        )
        third_ref[:, pl.ds(j * 256, 256)] = both[256:]
        pure = (3.0 * square - 2.0 * both[:256]) * mask_tile(t_ref, 5 + 2 * p, 2 * j + 2 * p, 2)
        for r in range(2):
            for e in range(2):
                slot = 2 * j + e - r
                if 0 <= slot < SLOTS:
                    purified_ref[r, slot] = pure[r * B : r * B + B, e * B : e * B + B]


def gradient_kernel(
    core_ref, s_ref, own_g, mate_g, n2_r, n2_x, f2_r, f2_x, n4_r, n4_x, f4_r, f4_x, n6_r, n6_x,
    own_p, pk_in, third_in, t_in,
    grad_ref,
    row_s, n2_s, f2_s, n4_s, f4_s, n6_s, own_s, pk_ref, third_s, t_ref, gk, gb, lhs, sems,
):
    p = core_ref[0]
    o = 1 - p
    plan = (
        (own_g, row_s.at[p]), (mate_g, row_s.at[o]),
        (n2_r, n2_s.at[o]), (n2_x, n2_s.at[p]),
        (f2_r, f2_s.at[p]), (f2_x, f2_s.at[o]),
        (n4_r, n4_s.at[o]), (n4_x, n4_s.at[p]),
        (f4_r, f4_s.at[p]), (f4_x, f4_s.at[o]),
        (n6_r, n6_s.at[o]), (n6_x, n6_s.at[p]),
        (own_p, own_s), (t_in, t_ref), (pk_in.at[pl.ds(p, 6)], pk_ref), (third_in, third_s),
    )
    copies = [pltpu.make_async_copy(a, b, sems.at[i]) for i, (a, b) in enumerate(plan)]
    for copy in copies:
        copy.start()
    for copy in copies[:13]:
        copy.wait()

    def block(m, slot):
        if 10 <= m <= 13:
            return row_s[(m - 10) // 2, rows_of(((m - 10) % 2) * SLOTS + slot), :]
        side = 0 if m < 10 else 1
        t = 10 - m if m < 10 else m - 13
        at = slot - t if side == 0 else slot
        store = (n2_s, f2_s, n4_s, f4_s, n6_s)[(t - 1) // 2]
        if t % 2 == 0:
            at += SLOTS - (t - 1)
        return store[side, rows_of(at), :]

    zero = jnp.zeros((B, B), BF16)
    for pair in range(7):
        for e in range(2):
            cols = pl.ds(e * B, B)
            for hole in ((0, 12, 13), (0, 1, 13))[e]:
                gk[pair, pl.ds(hole * B, B), cols] = zero
            j = 2 * pair + e
            for m in range(j, j + 11):
                gk[pair, pl.ds((m - 2 * pair + 1) * B, B), cols] = block(m, j - m + 10)
    for r in range(2):
        lhs[pl.ds(r * B, B), pl.ds((11 if r == 0 else 0) * B, B)] = zero
        for slot in range(SLOTS):
            lhs[pl.ds(r * B, B), pl.ds((slot + r) * B, B)] = own_s[rows_of(r * SLOTS + slot), :]
    for copy in copies[13:]:
        copy.wait()

    def tile(delta, j):
        k = j + delta
        count = (12 - 2 * abs(delta)) * B
        left = pk_ref[k, :, pl.ds(max(0, -delta) * 2 * B, count)]
        right = gk[j + p, pl.ds((max(0, delta) * 2 + 1) * B, count), :]
        found = jnp.dot(left, right, preferred_element_type=F32)
        found = found * mask_tile(t_ref, 2 * (k + p), 2 * (j + p), 2)
        given = gk[j + p, pl.ds((2 * delta + 6) * B, 256), :].astype(F32)
        gb[pl.ds(pl.multiple_of(k * 256, 256), 256), pl.ds(pl.multiple_of(j * 256, 256), 256)] = (
            3.0 * given - 2.0 * found
        ).astype(BF16)

    tile_loop(tile)

    for j in range(6):
        low, count = span(2 * j)
        cols = pl.ds(low * B, count * B)
        right = pk_ref[j, :, pl.ds((low + 5 - 2 * j) * B, count * B)]
        total = lax.dot_general(gb[pl.ds(5 * B, 256), cols], right, NT, preferred_element_type=F32)
        total += jnp.dot(
            lhs[:, cols], gb[pl.ds(low * B, count * B), pl.ds(j * 256, 256)],
            preferred_element_type=F32,
        )
        total -= 2.0 * third_s[:, pl.ds(j * 256, 256)]
        for r in range(2):
            for e in range(2):
                slot = 2 * j + e - r
                if 0 <= slot < SLOTS:
                    keep = s_ref[r, slot].astype(F32)
                    grad_ref[r, slot] = total[r * B : r * B + B, e * B : e * B + B] * keep


SMEM = pl.BlockSpec(memory_space=pltpu.SMEM)
VMEM = pl.BlockSpec(memory_space=pltpu.VMEM)
ANY = pl.BlockSpec(memory_space=pl.ANY)


def flat(blocks, extra=0):
    return jax.ShapeDtypeStruct((blocks * B + extra, B), BF16)


def pair_of(blocks, extra=0):
    return pltpu.VMEM((2, blocks * B + extra, B), BF16)


def on_device(density, cotangent, s_mask, t_mask):
    devices = lax.axis_size(AXES)
    core = (lax.axis_index(AXES) % 2).astype(jnp.int32).reshape(1)
    swap = [(i, i ^ 1) for i in range(devices)]

    def send(message, pair):
        return lax.ppermute(message, AXES, route(pair, devices))

    def to_mate(message):
        return lax.ppermute(message, AXES, swap)

    params = pltpu.CompilerParams(vmem_limit_bytes=48 * 1024 * 1024)
    p_pairs = (NEAR2, FAR2, NEAR4)
    p_out = pl.pallas_call(
        pack_density,
        in_specs=[SMEM, SMEM, SMEM, VMEM],
        out_specs=[VMEM] * 4,
        out_shape=[flat(22, MASK_ROWS)] + [flat(P_BLOCKS[pair], MASK_ROWS) for pair in p_pairs],
        compiler_params=params,
        name="pack_density",
    )(core, s_mask, t_mask, density)
    g_out = pl.pallas_call(
        pack_cotangent,
        in_specs=[SMEM, SMEM, VMEM],
        out_specs=[VMEM] * 6,
        out_shape=[flat(22)] + [flat(g_blocks(pair)) for pair in G_PAIRS],
        compiler_params=params,
        name="pack_cotangent",
    )(core, t_mask, cotangent)
    p_far = [send(message, pair) for message, pair in zip(p_out[1:], p_pairs)]
    mate_p = to_mate(p_out[0])
    mate_g = to_mate(g_out[0])
    p_mate = [to_mate(message) for message in p_far]
    g_far = [send(message, pair) for message, pair in zip(g_out[1:], G_PAIRS)]
    g_mate = [to_mate(message) for message in g_far]

    def zipped(far, mate):
        return [one for both in zip(far, mate) for one in both]

    purified, third, pk, t_all = pl.pallas_call(
        square_kernel,
        in_specs=[SMEM] + [ANY] * 9,
        out_specs=[VMEM] * 4,
        out_shape=[
            jax.ShapeDtypeStruct((2, SLOTS, B, B), F32),
            jax.ShapeDtypeStruct((256, 1536), F32),
            jax.ShapeDtypeStruct((7, 256, 1536), BF16),
            jax.ShapeDtypeStruct((14 * 16, B), F32),
        ],
        scratch_shapes=[
            pair_of(22, MASK_ROWS), pair_of(13, MASK_ROWS), pair_of(12, MASK_ROWS),
            pair_of(6, MASK_ROWS), pltpu.VMEM((22 * B, B), BF16),
            pltpu.VMEM((1536, 1536), BF16), pltpu.VMEM((512, 1536), BF16),
            pltpu.VMEM((14 * 16, B), F32), pltpu.SemaphoreType.DMA((9,)),
        ],
        cost_estimate=pl.CostEstimate(flops=7 * 10**9, bytes_accessed=16 * 10**6, transcendentals=0),
        compiler_params=params,
        name="square",
    )(core, p_out[0], mate_p, *zipped(p_far, p_mate), g_out[0])

    gradient = pl.pallas_call(
        gradient_kernel,
        in_specs=[SMEM, SMEM] + [ANY] * 16,
        out_specs=VMEM,
        out_shape=jax.ShapeDtypeStruct((2, SLOTS, B, B), F32),
        scratch_shapes=[pair_of(22)]
        + [pair_of(g_blocks(pair)) for pair in G_PAIRS]
        + [
            pltpu.VMEM((22 * B + MASK_ROWS, B), BF16), pltpu.VMEM((6, 256, 1536), BF16),
            pltpu.VMEM((256, 1536), F32), pltpu.VMEM((14 * 16, B), F32),
            pltpu.VMEM((7, 14 * B, 256), BF16), pltpu.VMEM((1536, 1536), BF16),
            pltpu.VMEM((256, 1536), BF16), pltpu.SemaphoreType.DMA((16,)),
        ],
        cost_estimate=pl.CostEstimate(flops=7 * 10**9, bytes_accessed=16 * 10**6, transcendentals=0),
        compiler_params=params,
        name="gradient",
    )(core, s_mask, g_out[0], mate_g, *zipped(g_far, g_mate), p_out[0], pk, third, t_all)
    return (purified, gradient)


def solution(mesh):
    band = P(AXES, None, None, None)
    in_specs = (band, band, P(AXES, None), P(AXES, None))
    return jax.shard_map(
        on_device, mesh=mesh, in_specs=in_specs, out_specs=(band, band), check_vma=False
    )
```

time: 260 us -> 113 us (0.43)
  starting transfers between devices: 128 us -> 48.6 us
  waiting for transfers between devices: 77 us -> 14.7 us
  Pallas kernels: 0 us -> 41.6 us
  local copies, waits for them, and re-layouts: 21.6 us -> 5.41 us
  other arithmetic: 15.8 us -> 0 us
  matrix products: 13.8 us -> 0 us
    ppermute x24 -> x18, starting transfers between devices: 128 us -> 48.6 us  [the longest x8 34.6 us: send(): return lax.ppermute(message, AXES, route(pair, devices))]
    ppermute x24 -> x18, waiting for transfers between devices: 77 us -> 14.7 us  [the longest x8 14.6 us: send(): return lax.ppermute(message, AXES, route(pair, devices))]
    pallas_call x0 -> x4, Pallas kernels: none -> 41.6 us  [the longest x1 19.9 us: on_device(): pl.pallas_call(gradient_kernel, in_specs=[SMEM, SMEM] + [ANY] * 16, out_s...]
    dot_general x6 -> x0, matrix products: 13.8 us -> none  [band_local(): jnp.einsum('reab,recbd->rcad', left_side, stacked, preferred_element_type...]
    unnamed x25 -> x0, other arithmetic: 11.1 us -> none
    slice x22 -> x0, local copies, waits for them, and re-layouts: 8.86 us -> none  [the longest x10 4.57 us: band_local(): window[:, -shift_by:]]
    unnamed x47 -> x14, local copies, waits for them, and re-layouts: 12.7 us -> 5.41 us
  transfers between devices with their start and end apart: 24 -> 18, of which waited for: 8 -> 2; matrix products, arithmetic and copies ran while one was open for 15% -> 0% of each run, Pallas kernels for 0% -> 19%
where the time goes in v1:
time: 113 us; the launch traced here: 111 us
  starting transfers between devices  48.6 us (43%)
  Pallas kernels  41.6 us (37%)
  waiting for transfers between devices  14.7 us (13%)
  local copies, waits for them, and re-layouts  5.41 us (5%)
    ppermute x8, starting transfers between devices, send(): return lax.ppermute(message, AXES, route(pair, devices))  34.6 us
    pallas_call x1, Pallas kernels, on_device(): pl.pallas_call(gradient_kernel, in_specs=[SMEM, SMEM] + [ANY] * 16, out_s...  19.9 us
    pallas_call x1, Pallas kernels, on_device(): pl.pallas_call(square_kernel, in_specs=[SMEM] + [ANY] * 9, out_specs=[VME...  19.8 us
    ppermute x8, waiting for transfers between devices, send(): return lax.ppermute(message, AXES, route(pair, devices))  14.6 us
    ppermute x10, starting transfers between devices, to_mate(): return lax.ppermute(message, AXES, swap)  14 us
    unnamed x14, local copies, waits for them, and re-layouts  5.41 us
  transfers between devices with their start and end apart: 18, of which 2 were waited for; matrix products, arithmetic and copies ran while one was open for 0% of the time, Pallas kernels for 19%

profile of v1, /device:TPU:25, one launch (start us, length us, event | category | flops | bytes accessed | tf_op | source)
XLA Modules:
  0.0 111.2 jit_solution(7444094338086476251)
XLA Ops:
  0.7 1.1 copy-done
  1.8 0.7 copy-done.2
  2.4 1.0 pack_cotangent.1
  3.4 4.5 %collective-permute-start.16 = (bf16[384,128]{1,0:T(8,128)(2,1)S(1)}, bf16[384,128]{1,0:T(8,128)(2,1)S(1)}, u32[]{:S(2)}, u32[]{:S(2)}) collective-permute-start(bf16[384,128]{1,0:T(8,128)(2,1)S(1)} %get-tuple-element.26), channel_id=1, source_target_pairs={{1,7},{3,9},{5,11},{6,0},{7,13},{8,2},{9,15},{10,4},{11,17},{12,6}... | collective-permute-start | bytes 294920 | tf_op jit(solution)/shard_map/ppermute | solution.py:341
  7.9 3.5 %collective-permute-start.12 = (bf16[1408,128]{1,0:T(8,128)(2,1)S(1)}, bf16[1408,128]{1,0:T(8,128)(2,1)S(1)}, u32[]{:S(2)}, u32[]{:S(2)}) collective-permute-start(bf16[1408,128]{1,0:T(8,128)(2,1)S(1)} %get-tuple-element.24), channel_id=1, source_target_pairs={{1,5},{3,7},{4,0},{5,9},{6,2},{7,11},{8,4},{9,13},{10,6},{11,15},{... | collective-permute-start | bytes 1081352 | tf_op jit(solution)/shard_map/ppermute | solution.py:341
  11.4 0.0 copy-start.1
  11.5 1.1 copy-done.1
  12.6 0.7 copy-done.3
  13.2 0.7 copy-done.4
  13.9 0.9 pack_density.1
  14.8 7.3 %collective-permute-start.3 = (bf16[1568,128]{1,0:T(8,128)(2,1)S(1)}, bf16[1568,128]{1,0:T(8,128)(2,1)S(1)}, u32[]{:S(2)}, u32[]{:S(2)}) collective-permute-start(bf16[1568,128]{1,0:T(8,128)(2,1)S(1)} %get-tuple-element.18), channel_id=1, source_target_pairs={{0,2},{2,4},{3,1},{4,6},{5,3},{6,8},{7,5},{8,10},{9,7},{10,12},{11... | collective-permute-start | bytes 1204232 | tf_op jit(solution)/shard_map/ppermute | solution.py:341
  22.1 0.0 collective-permute-done.16.n6_r
  22.1 1.8 %collective-permute-start.17 = (bf16[384,128]{1,0:T(8,128)(2,1)S(1)}, bf16[384,128]{1,0:T(8,128)(2,1)S(1)}, u32[]{:S(2)}, u32[]{:S(2)}) collective-permute-start(bf16[384,128]{1,0:T(8,128)(2,1)S(1)} %collective-permute-done.16.n6_r), channel_id=1, source_target_pairs={{0,1},{1,0},{2,3},{3,2},{4,5},{5,4},{6,7},{7,6},{8,9},{9,8},{10,11... | collective-permute-start | bytes 294920 | tf_op jit(solution)/shard_map/ppermute | solution.py:344
  23.9 1.9 %collective-permute-start.5 = (bf16[800,128]{1,0:T(8,128)(2,1)S(1)}, bf16[800,128]{1,0:T(8,128)(2,1)S(1)}, u32[]{:S(2)}, u32[]{:S(2)}) collective-permute-start(bf16[800,128]{1,0:T(8,128)(2,1)S(1)} %get-tuple-element.19), channel_id=1, source_target_pairs={{1,5},{3,7},{4,0},{5,9},{6,2},{7,11},{8,4},{9,13},{10,6},{11,15},{... | collective-permute-start | bytes 614408 | tf_op jit(solution)/shard_map/ppermute | solution.py:341
  25.8 3.9 %collective-permute-start.1 = (bf16[1696,128]{1,0:T(8,128)(2,1)S(1)}, bf16[1696,128]{1,0:T(8,128)(2,1)S(1)}, u32[]{:S(2)}, u32[]{:S(2)}) collective-permute-start(bf16[1696,128]{1,0:T(8,128)(2,1)S(1)} %get-tuple-element.17), channel_id=1, source_target_pairs={{1,3},{2,0},{3,5},{4,2},{5,7},{6,4},{7,9},{8,6},{9,11},{10,8},{11,... | collective-permute-start | bytes 1302536 | tf_op jit(solution)/shard_map/ppermute | solution.py:341
  29.7 7.8 %collective-permute-start.14 = (bf16[896,128]{1,0:T(8,128)(2,1)S(1)}, bf16[896,128]{1,0:T(8,128)(2,1)S(1)}, u32[]{:S(2)}, u32[]{:S(2)}) collective-permute-start(bf16[896,128]{1,0:T(8,128)(2,1)S(1)} %get-tuple-element.25), channel_id=1, source_target_pairs={{0,4},{2,6},{4,8},{5,1},{6,10},{7,3},{8,12},{9,5},{10,14},{11,7},{... | collective-permute-start | bytes 688136 | tf_op jit(solution)/shard_map/ppermute | solution.py:341
  37.5 0.8 collective-permute-start
  38.3 4.1 %collective-permute-done.14.f4_r = bf16[896,128]{1,0:T(8,128)(2,1)S(1)} collective-permute-done((bf16[896,128]{1,0:T(8,128)(2,1)S(1)}, bf16[896,128]{1,0:T(8,128)(2,1)S(1)}, u32[]{:S(2)}, u32[]{:S(2)}) %collective-permute-start.14) | collective-permute-done | bytes 229408 | tf_op jit(solution)/shard_map/ppermute | solution.py:341
  42.4 1.9 %collective-permute-start.8 = (bf16[2432,128]{1,0:T(8,128)(2,1)S(1)}, bf16[2432,128]{1,0:T(8,128)(2,1)S(1)}, u32[]{:S(2)}, u32[]{:S(2)}) collective-permute-start(bf16[2432,128]{1,0:T(8,128)(2,1)S(1)} %get-tuple-element.22), channel_id=1, source_target_pairs={{1,3},{2,0},{3,5},{4,2},{5,7},{6,4},{7,9},{8,6},{9,11},{10,8},{11,... | collective-permute-start | bytes 1867784 | tf_op jit(solution)/shard_map/ppermute | solution.py:341
  44.3 4.2 %collective-permute-start.6 = (bf16[800,128]{1,0:T(8,128)(2,1)S(1)}, bf16[800,128]{1,0:T(8,128)(2,1)S(1)}, u32[]{:S(2)}, u32[]{:S(2)}) collective-permute-start(bf16[800,128]{1,0:T(8,128)(2,1)S(1)} %collective-permute-done.5.n4_r), channel_id=1, source_target_pairs={{0,1},{1,0},{2,3},{3,2},{4,5},{5,4},{6,7},{7,6},{8,9},{9,8},{10,11... | collective-permute-start | bytes 614408 | tf_op jit(solution)/shard_map/ppermute | solution.py:344
  48.5 3.8 %collective-permute-start.10 = (bf16[1920,128]{1,0:T(8,128)(2,1)S(1)}, bf16[1920,128]{1,0:T(8,128)(2,1)S(1)}, u32[]{:S(2)}, u32[]{:S(2)}) collective-permute-start(bf16[1920,128]{1,0:T(8,128)(2,1)S(1)} %get-tuple-element.23), channel_id=1, source_target_pairs={{0,2},{2,4},{3,1},{4,6},{5,3},{6,8},{7,5},{8,10},{9,7},{10,12},{11... | collective-permute-start | bytes 1474568 | tf_op jit(solution)/shard_map/ppermute | solution.py:341
  52.4 0.2 collective-permute-start.2
  52.6 0.4 collective-permute-start.4
  53.0 10.5 %collective-permute-done.10.f2_r = bf16[1920,128]{1,0:T(8,128)(2,1)S(1)} collective-permute-done((bf16[1920,128]{1,0:T(8,128)(2,1)S(1)}, bf16[1920,128]{1,0:T(8,128)(2,1)S(1)}, u32[]{:S(2)}, u32[]{:S(2)}) %collective-permute-start.10) | collective-permute-done | bytes 491552 | tf_op jit(solution)/shard_map/ppermute | solution.py:341
  63.5 5.6 %collective-permute-start.7 = (bf16[2816,128]{1,0:T(8,128)(2,1)S(1)}, bf16[2816,128]{1,0:T(8,128)(2,1)S(1)}, u32[]{:S(2)}, u32[]{:S(2)}) collective-permute-start(bf16[2816,128]{1,0:T(8,128)(2,1)S(1)} %get-tuple-element.20.own_g), channel_id=1, source_target_pairs={{0,1},{1,0},{2,3},{3,2},{4,5},{5,4},{6,7},{7,6},{8,9},{9,8},{10,11... | collective-permute-start | bytes 2162696 | tf_op jit(solution)/shard_map/ppermute | solution.py:344
  69.1 0.1 collective-permute-start.15
  69.2 0.4 collective-permute-start.13
  69.6 0.1 collective-permute-start.11
  69.7 0.4 collective-permute-start.9
  70.1 19.8 %square.1 = (f32[2,11,128,128]{3,2,1,0:T(8,128)}, f32[256,1536]{1,0:T(8,128)S(1)}, bf16[7,256,1536]{2,1,0:T(8,128)(2,1)}, f32[224,128]{1,0:T(8,128)S(1)}) custom-call(s32[1]{0:T(128)} %bitcast.core_ref, bf16[2848,128]{1,0:T(8,128)(2,1)S(1)} %get-tuple-element.16.own_p, bf16[2848,128]{1,0:T(8,128)(2,1)S(1)} %collective-permute-done.mate_p, ...), custom_call_target="tpu_custom_call" | custom-call | flops 7000000000 | bytes 16000000 | tf_op jit(solution)/shard_map/square/pallas_call | solution.py:374
  89.9 1.2 %copy-done.6 = f32[256,1536]{1,0:T(8,128)} copy-done((f32[256,1536]{1,0:T(8,128)}, f32[256,1536]{1,0:T(8,128)S(1)}, u32[]{:S(2)}) %copy-start.6) | copy-done | bytes 1572888
  91.1 19.9 %gradient.1 = f32[2,11,128,128]{3,2,1,0:T(8,128)} custom-call(s32[1]{0:T(128)} %bitcast.core_ref, s32[2,11]{1,0:T(2,128)S(1)} %copy-done.5, bf16[2816,128]{1,0:T(8,128)(2,1)S(1)} %get-tuple-element.20.own_g, bf16[2816,128]{1,0:T(8,128)(2,1)S(1)} %collective-permute-done.7.mate_g, bf16[2432,128]{1,0:T(8,128)(2,1)S(1)} %collective-permute-done.8.n2_r, ...), custom_call_target="tpu_custom_call" | custom-call | flops 7000000000 | bytes 16000000 | tf_op jit(solution)/shard_map/gradient/pallas_call | solution.py:395
  (22 shorter events, 0.1 us)
Async XLA Ops:
  0.6 1.1 copy-start
  1.8 0.7 copy-start.2
  3.4 18.7 %collective-permute-start.16 = (bf16[384,128]{1,0:T(8,128)(2,1)S(1)}, bf16[384,128]{1,0:T(8,128)(2,1)S(1)}, u32[]{:S(2)}, u32[]{:S(2)}) collective-permute-start(bf16[384,128]{1,0:T(8,128)(2,1)S(1)} %get-tuple-element.26), channel_id=1, source_target_pairs={{1,7},{3,9},{5,11},{6,0},{7,13},{8,2},{9,15},{10,4},{11,17},{12,6}... | collective-permute-start | bytes 294920 | tf_op jit(solution)/shard_map/ppermute | solution.py:341
  7.9 36.4 %collective-permute-start.12 = (bf16[1408,128]{1,0:T(8,128)(2,1)S(1)}, bf16[1408,128]{1,0:T(8,128)(2,1)S(1)}, u32[]{:S(2)}, u32[]{:S(2)}) collective-permute-start(bf16[1408,128]{1,0:T(8,128)(2,1)S(1)} %get-tuple-element.24), channel_id=1, source_target_pairs={{1,5},{3,7},{4,0},{5,9},{6,2},{7,11},{8,4},{9,13},{10,6},{11,15},{... | collective-permute-start | bytes 1081352 | tf_op jit(solution)/shard_map/ppermute | solution.py:341
  11.4 1.1 %copy-start.1 = (bf16[2,11,128,128]{3,2,1,0:T(8,128)(2,1)S(1)}, bf16[2,11,128,128]{3,2,1,0:T(8,128)(2,1)}, u32[]{:S(2)}) copy-start(bf16[2,11,128,128]{3,2,1,0:T(8,128)(2,1)} %density_ref.1) | copy-start | bytes 2162692
  12.6 0.7 copy-start.3
  13.2 0.7 copy-start.4
  14.8 33.7 %collective-permute-start.3 = (bf16[1568,128]{1,0:T(8,128)(2,1)S(1)}, bf16[1568,128]{1,0:T(8,128)(2,1)S(1)}, u32[]{:S(2)}, u32[]{:S(2)}) collective-permute-start(bf16[1568,128]{1,0:T(8,128)(2,1)S(1)} %get-tuple-element.18), channel_id=1, source_target_pairs={{0,2},{2,4},{3,1},{4,6},{5,3},{6,8},{7,5},{8,10},{9,7},{10,12},{11... | collective-permute-start | bytes 1204232 | tf_op jit(solution)/shard_map/ppermute | solution.py:341
  22.1 7.6 %collective-permute-start.17 = (bf16[384,128]{1,0:T(8,128)(2,1)S(1)}, bf16[384,128]{1,0:T(8,128)(2,1)S(1)}, u32[]{:S(2)}, u32[]{:S(2)}) collective-permute-start(bf16[384,128]{1,0:T(8,128)(2,1)S(1)} %collective-permute-done.16.n6_r), channel_id=1, source_target_pairs={{0,1},{1,0},{2,3},{3,2},{4,5},{5,4},{6,7},{7,6},{8,9},{9,8},{10,11... | collective-permute-start | bytes 294920 | tf_op jit(solution)/shard_map/ppermute | solution.py:344
  23.9 13.6 %collective-permute-start.5 = (bf16[800,128]{1,0:T(8,128)(2,1)S(1)}, bf16[800,128]{1,0:T(8,128)(2,1)S(1)}, u32[]{:S(2)}, u32[]{:S(2)}) collective-permute-start(bf16[800,128]{1,0:T(8,128)(2,1)S(1)} %get-tuple-element.19), channel_id=1, source_target_pairs={{1,5},{3,7},{4,0},{5,9},{6,2},{7,11},{8,4},{9,13},{10,6},{11,15},{... | collective-permute-start | bytes 614408 | tf_op jit(solution)/shard_map/ppermute | solution.py:341
  25.8 26.6 %collective-permute-start.1 = (bf16[1696,128]{1,0:T(8,128)(2,1)S(1)}, bf16[1696,128]{1,0:T(8,128)(2,1)S(1)}, u32[]{:S(2)}, u32[]{:S(2)}) collective-permute-start(bf16[1696,128]{1,0:T(8,128)(2,1)S(1)} %get-tuple-element.17), channel_id=1, source_target_pairs={{1,3},{2,0},{3,5},{4,2},{5,7},{6,4},{7,9},{8,6},{9,11},{10,8},{11,... | collective-permute-start | bytes 1302536 | tf_op jit(solution)/shard_map/ppermute | solution.py:341
  29.7 12.7 %collective-permute-start.14 = (bf16[896,128]{1,0:T(8,128)(2,1)S(1)}, bf16[896,128]{1,0:T(8,128)(2,1)S(1)}, u32[]{:S(2)}, u32[]{:S(2)}) collective-permute-start(bf16[896,128]{1,0:T(8,128)(2,1)S(1)} %get-tuple-element.25), channel_id=1, source_target_pairs={{0,4},{2,6},{4,8},{5,1},{6,10},{7,3},{8,12},{9,5},{10,14},{11,7},{... | collective-permute-start | bytes 688136 | tf_op jit(solution)/shard_map/ppermute | solution.py:341
  37.5 31.7 %collective-permute-start = (bf16[2848,128]{1,0:T(8,128)(2,1)S(1)}, bf16[2848,128]{1,0:T(8,128)(2,1)S(1)}, u32[]{:S(2)}, u32[]{:S(2)}) collective-permute-start(bf16[2848,128]{1,0:T(8,128)(2,1)S(1)} %get-tuple-element.16.own_p), channel_id=1, source_target_pairs={{0,1},{1,0},{2,3},{3,2},{4,5},{5,4},{6,7},{7,6},{8,9},{9,8},{10,11... | collective-permute-start | bytes 2187272 | tf_op jit(solution)/shard_map/ppermute | solution.py:344
  42.4 26.7 %collective-permute-start.8 = (bf16[2432,128]{1,0:T(8,128)(2,1)S(1)}, bf16[2432,128]{1,0:T(8,128)(2,1)S(1)}, u32[]{:S(2)}, u32[]{:S(2)}) collective-permute-start(bf16[2432,128]{1,0:T(8,128)(2,1)S(1)} %get-tuple-element.22), channel_id=1, source_target_pairs={{1,3},{2,0},{3,5},{4,2},{5,7},{6,4},{7,9},{8,6},{9,11},{10,8},{11,... | collective-permute-start | bytes 1867784 | tf_op jit(solution)/shard_map/ppermute | solution.py:341
  44.3 8.2 %collective-permute-start.6 = (bf16[800,128]{1,0:T(8,128)(2,1)S(1)}, bf16[800,128]{1,0:T(8,128)(2,1)S(1)}, u32[]{:S(2)}, u32[]{:S(2)}) collective-permute-start(bf16[800,128]{1,0:T(8,128)(2,1)S(1)} %collective-permute-done.5.n4_r), channel_id=1, source_target_pairs={{0,1},{1,0},{2,3},{3,2},{4,5},{5,4},{6,7},{7,6},{8,9},{9,8},{10,11... | collective-permute-start | bytes 614408 | tf_op jit(solution)/shard_map/ppermute | solution.py:344
  48.5 15.0 %collective-permute-start.10 = (bf16[1920,128]{1,0:T(8,128)(2,1)S(1)}, bf16[1920,128]{1,0:T(8,128)(2,1)S(1)}, u32[]{:S(2)}, u32[]{:S(2)}) collective-permute-start(bf16[1920,128]{1,0:T(8,128)(2,1)S(1)} %get-tuple-element.23), channel_id=1, source_target_pairs={{0,2},{2,4},{3,1},{4,6},{5,3},{6,8},{7,5},{8,10},{9,7},{10,12},{11... | collective-permute-start | bytes 1474568 | tf_op jit(solution)/shard_map/ppermute | solution.py:341
  52.4 17.3 %collective-permute-start.2 = (bf16[1696,128]{1,0:T(8,128)(2,1)S(1)}, bf16[1696,128]{1,0:T(8,128)(2,1)S(1)}, u32[]{:S(2)}, u32[]{:S(2)}) collective-permute-start(bf16[1696,128]{1,0:T(8,128)(2,1)S(1)} %collective-permute-done.1.n2_r), channel_id=1, source_target_pairs={{0,1},{1,0},{2,3},{3,2},{4,5},{5,4},{6,7},{7,6},{8,9},{9,8},{10,11... | collective-permute-start | bytes 1302536 | tf_op jit(solution)/shard_map/ppermute | solution.py:344
  52.6 17.0 %collective-permute-start.4 = (bf16[1568,128]{1,0:T(8,128)(2,1)S(1)}, bf16[1568,128]{1,0:T(8,128)(2,1)S(1)}, u32[]{:S(2)}, u32[]{:S(2)}) collective-permute-start(bf16[1568,128]{1,0:T(8,128)(2,1)S(1)} %collective-permute-done.3.f2_r), channel_id=1, source_target_pairs={{0,1},{1,0},{2,3},{3,2},{4,5},{5,4},{6,7},{7,6},{8,9},{9,8},{10,11... | collective-permute-start | bytes 1204232 | tf_op jit(solution)/shard_map/ppermute | solution.py:344
  63.5 27.7 %copy-start.5 = (s32[2,11]{1,0:T(2,128)S(1)}, s32[2,11]{1,0:T(2,128)}, u32[]{:S(2)}) copy-start(s32[2,11]{1,0:T(2,128)} %s_ref.3) | copy-start | bytes 268
  63.5 27.6 %collective-permute-start.7 = (bf16[2816,128]{1,0:T(8,128)(2,1)S(1)}, bf16[2816,128]{1,0:T(8,128)(2,1)S(1)}, u32[]{:S(2)}, u32[]{:S(2)}) collective-permute-start(bf16[2816,128]{1,0:T(8,128)(2,1)S(1)} %get-tuple-element.20.own_g), channel_id=1, source_target_pairs={{0,1},{1,0},{2,3},{3,2},{4,5},{5,4},{6,7},{7,6},{8,9},{9,8},{10,11... | collective-permute-start | bytes 2162696 | tf_op jit(solution)/shard_map/ppermute | solution.py:344
  69.1 22.0 %collective-permute-start.15 = (bf16[896,128]{1,0:T(8,128)(2,1)S(1)}, bf16[896,128]{1,0:T(8,128)(2,1)S(1)}, u32[]{:S(2)}, u32[]{:S(2)}) collective-permute-start(bf16[896,128]{1,0:T(8,128)(2,1)S(1)} %collective-permute-done.14.f4_r), channel_id=1, source_target_pairs={{0,1},{1,0},{2,3},{3,2},{4,5},{5,4},{6,7},{7,6},{8,9},{9,8},{10,11... | collective-permute-start | bytes 688136 | tf_op jit(solution)/shard_map/ppermute | solution.py:344
  69.2 21.9 %collective-permute-start.13 = (bf16[1408,128]{1,0:T(8,128)(2,1)S(1)}, bf16[1408,128]{1,0:T(8,128)(2,1)S(1)}, u32[]{:S(2)}, u32[]{:S(2)}) collective-permute-start(bf16[1408,128]{1,0:T(8,128)(2,1)S(1)} %collective-permute-done.12.n4_r), channel_id=1, source_target_pairs={{0,1},{1,0},{2,3},{3,2},{4,5},{5,4},{6,7},{7,6},{8,9},{9,8},{10,11... | collective-permute-start | bytes 1081352 | tf_op jit(solution)/shard_map/ppermute | solution.py:344
  69.6 21.5 %collective-permute-start.11 = (bf16[1920,128]{1,0:T(8,128)(2,1)S(1)}, bf16[1920,128]{1,0:T(8,128)(2,1)S(1)}, u32[]{:S(2)}, u32[]{:S(2)}) collective-permute-start(bf16[1920,128]{1,0:T(8,128)(2,1)S(1)} %collective-permute-done.10.f2_r), channel_id=1, source_target_pairs={{0,1},{1,0},{2,3},{3,2},{4,5},{5,4},{6,7},{7,6},{8,9},{9,8},{10,11... | collective-permute-start | bytes 1474568 | tf_op jit(solution)/shard_map/ppermute | solution.py:344
  69.7 21.4 %collective-permute-start.9 = (bf16[2432,128]{1,0:T(8,128)(2,1)S(1)}, bf16[2432,128]{1,0:T(8,128)(2,1)S(1)}, u32[]{:S(2)}, u32[]{:S(2)}) collective-permute-start(bf16[2432,128]{1,0:T(8,128)(2,1)S(1)} %collective-permute-done.8.n2_r), channel_id=1, source_target_pairs={{0,1},{1,0},{2,3},{3,2},{4,5},{5,4},{6,7},{7,6},{8,9},{9,8},{10,11... | collective-permute-start | bytes 1867784 | tf_op jit(solution)/shard_map/ppermute | solution.py:344
  89.9 1.2 %copy-start.6 = (f32[256,1536]{1,0:T(8,128)}, f32[256,1536]{1,0:T(8,128)S(1)}, u32[]{:S(2)}) copy-start(f32[256,1536]{1,0:T(8,128)S(1)} %get-tuple-element.28.third_in) | copy-start | bytes 4718596

commit v2 on v1

v2 whole, which is shorter than its diff:
```python
import functools

import jax
import jax.numpy as jnp
from jax import lax
from jax.experimental import pallas as pl
from jax.experimental.pallas import tpu as pltpu
from jax.sharding import PartitionSpec as P

B = 128
HALF = 5
SLOTS = 11
AXES = ("row", "col")
MASK_ROWS = 32
BF16 = jnp.bfloat16
F32 = jnp.float32

NEAR2, FAR2, NEAR4, FAR4, NEAR6 = (1, 2), (3, 4), (5, 6), (7, 8), (9, 10)
P_BLOCKS = {NEAR2: 13, FAR2: 12, NEAR4: 6}
G_PAIRS = (NEAR2, FAR2, NEAR4, FAR4, NEAR6)


def g_blocks(pair):
    return sum(SLOTS - t for t in pair)


def is_near(pair):
    return pair in (NEAR2, NEAR4, NEAR6)


def hop(pair):
    return {NEAR2: 2, FAR2: 2, NEAR4: 4, FAR4: 4, NEAR6: 6}[pair]


def route(pair, devices):
    pairs = []
    for source in range(devices):
        up = (source % 2 == 1) == is_near(pair)
        target = source + hop(pair) if up else source - hop(pair)
        if 0 <= target < devices:
            pairs.append((source, target))
    return pairs


def rows_of(block):
    start = block * B
    if not isinstance(start, int):
        start = pl.multiple_of(start, B)
    return pl.ds(start, B)


def masked(values_ref, mask_ref, row, slot):
    keep = mask_ref[row, slot].astype(F32)
    return (values_ref[row, slot].astype(F32) * keep).astype(BF16)


def pack(
    core_ref, s_ref, t_ref, density_any, cotangent_any,
    own_p, near2_ref, far2_ref, near4_ref, own_g, n2_g, f2_g, n4_g, f4_g, n6_g,
    density_ref, cotangent_ref, sems,
):
    first = pltpu.make_async_copy(density_any, density_ref, sems.at[0])
    second = pltpu.make_async_copy(cotangent_any, cotangent_ref, sems.at[1])
    first.start()
    second.start()
    q = core_ref[0]
    o = 1 - q

    line = lax.broadcasted_iota(jnp.int32, (MASK_ROWS, B), 0)
    mask = jnp.zeros((MASK_ROWS, B), F32)
    for row in range(2):
        for slot in range(SLOTS):
            mask = jnp.where(line == row * 16 + slot + 2, t_ref[row, slot].astype(F32), mask)
    mask = mask.astype(BF16)
    for out_ref, count in ((own_p, 22), (near2_ref, 13), (far2_ref, 12), (near4_ref, 6)):
        out_ref[pl.ds(count * B, MASK_ROWS), :] = mask

    first.wait()

    def put(out_ref, at, row, slot):
        out_ref[rows_of(at), :] = masked(density_ref, s_ref, row, slot)

    for s in range(6):
        put(near2_ref, s, q, 5 * o + s)
        put(near2_ref, 6 + s, o, 5 * o + s)
        put(far2_ref, s, o, 5 * q + s)
        put(far2_ref, 6 + s, q, 5 * q + s)
        put(near4_ref, s, q, 5 * o + s)
    put(near2_ref, 12, q, 10 * q)
    for row in range(2):
        for slot in range(SLOTS):
            put(own_p, row * SLOTS + slot, row, slot)

    second.wait()
    for pair, out_ref in zip(G_PAIRS, (n2_g, f2_g, n4_g, f4_g, n6_g)):
        up = q if is_near(pair) else o
        at = 0
        for place, t in enumerate(pair):
            row = up if place == 0 else 1 - up
            for s in range(SLOTS - t):
                out_ref[rows_of(at), :] = masked(cotangent_ref, t_ref, row, t * up + s)
                at += 1
    for row in range(2):
        for slot in range(SLOTS):
            own_g[rows_of(row * SLOTS + slot), :] = masked(cotangent_ref, t_ref, row, slot)


def by_side(core, near, received, other):
    return (other, received) if (core == 0) == near else (received, other)


def in_block(core_ref, work):
    pl.when(core_ref[0] >= 0)(work)


def tile_loop(core_ref, body):
    for delta in range(-3, 4):

        def diagonal(delta=delta):
            for j in range(max(0, -delta), min(6, 6 - delta)):
                body(delta, j)

        in_block(core_ref, diagonal)


def mask_tile(t_ref, first_k, first_j, height):
    rows = []
    for k in range(height):
        pieces = []
        for j in range(2):
            line = (first_k + k) * 16 + (first_j + j) - (first_k + k) + HALF + 2
            pieces.append(jnp.broadcast_to(t_ref[pl.ds(line, 1), :], (B, B)))
        rows.append(jnp.concatenate(pieces, axis=1))
    return jnp.concatenate(rows, axis=0)


def span(j0):
    low = max(0, j0 - 5)
    high = min(11, j0 + 6)
    return low, high - low + 1


NT = (((1,), (1,)), ((), ()))


def square_kernel(
    core_ref, own_p, mate_p, n2_r, n2_x, f2_r, f2_x, n4_r, n4_x, own_g,
    purified_ref, third_ref, pk_ref, t_ref,
    sw, lhs,
):
    p = core_ref[0]
    zero = jnp.zeros((B, B), BF16)

    def assemble(core):
        full = (own_p, mate_p) if core == 0 else (mate_p, own_p)
        n2 = by_side(core, True, n2_r, n2_x)
        f2 = by_side(core, False, f2_r, f2_x)
        n4 = by_side(core, True, n4_r, n4_x)

        def held(k, slot):
            if 5 <= k <= 8:
                return full[(k - 5) // 2][rows_of(((k - 5) % 2) * SLOTS + slot), :]
            side = 0 if k < 5 else 1
            t = 5 - k if k < 5 else k - 8
            at = slot if k < 5 else slot - 5
            if t <= 2:
                return n2[side][rows_of(6 * (t - 1) + at), :]
            if t <= 4:
                return f2[side][rows_of(6 * (t - 3) + at), :]
            return n4[side][rows_of(at), :]

        def block(k, slot):
            if 5 <= k <= 8 or (k < 5 and slot <= 5) or (k > 8 and slot >= 5):
                return held(k, slot)
            if (k, slot) == (4, 10):
                return n2[0][rows_of(12), :]
            if (k, slot) == (9, 0):
                return n2[1][rows_of(12), :]
            return held(k + slot - 5, 10 - slot).T

        for pair in range(core, core + 6):
            for e in range(2):
                rows = pl.ds(e * B, B)
                pk_ref[pair, rows, pl.ds((11 if e == 0 else 0) * B, B)] = zero
                for slot in range(SLOTS):
                    pk_ref[pair, rows, pl.ds((slot + e) * B, B)] = block(2 * pair + e, slot)

        for k in range(14):
            if 5 <= k <= 8:
                part = full[(k - 5) // 2][pl.ds(22 * B, MASK_ROWS), :]
                r = (k - 5) % 2
            else:
                side = 0 if k < 5 else 1
                t = 5 - k if k < 5 else k - 8
                r = (t % 2) if side == 0 else (1 - t % 2)
                if t <= 2:
                    part = n2[side][pl.ds(13 * B, MASK_ROWS), :]
                elif t <= 4:
                    part = f2[side][pl.ds(12 * B, MASK_ROWS), :]
                else:
                    part = n4[side][pl.ds(6 * B, MASK_ROWS), :]
            t_ref[pl.ds(k * 16, 16), :] = part.astype(F32)[r * 16 : r * 16 + 16, :]

    for core in range(2):
        pl.when(p == core)(functools.partial(assemble, core))

    for r in range(2):
        hole = pl.ds((11 if r == 0 else 0) * B, B)
        lhs[pl.ds(r * B, B), hole] = zero
        lhs[pl.ds((2 + r) * B, B), hole] = zero
        for slot in range(SLOTS):
            cols = pl.ds((slot + r) * B, B)
            lhs[pl.ds(r * B, B), cols] = own_p[rows_of(r * SLOTS + slot), :]
            lhs[pl.ds((2 + r) * B, B), cols] = own_g[rows_of(r * SLOTS + slot), :]

    def tile(delta, j):
        k = j + delta
        count = (12 - 2 * abs(delta)) * B
        left = pk_ref[k + p, :, pl.ds(max(0, -delta) * 2 * B, count)]
        right = pk_ref[j + p, :, pl.ds(max(0, delta) * 2 * B, count)]
        found = lax.dot_general(left, right, NT, preferred_element_type=F32)
        found = found * mask_tile(t_ref, 2 * (k + p), 2 * (j + p), 2)
        sw[pl.ds(pl.multiple_of(k * 256, 256), 256), pl.ds(pl.multiple_of(j * 256, 256), 256)] = (
            found.astype(BF16)
        )

    tile_loop(core_ref, tile)

    def finish(j):
        low, count = span(2 * j)
        cols = pl.ds(low * B, count * B)
        right = pk_ref[j + p, :, pl.ds((low + 5 - 2 * j) * B, count * B)]
        square = lax.dot_general(lhs[pl.ds(0, 256), cols], right, NT, preferred_element_type=F32)
        both = jnp.dot(
            lhs[:, cols], sw[pl.ds(low * B, count * B), pl.ds(j * 256, 256)],
            preferred_element_type=F32,
        )
        third_ref[:, pl.ds(j * 256, 256)] = both[256:]
        pure = (3.0 * square - 2.0 * both[:256]) * mask_tile(t_ref, 5 + 2 * p, 2 * j + 2 * p, 2)
        for r in range(2):
            for e in range(2):
                slot = 2 * j + e - r
                if 0 <= slot < SLOTS:
                    purified_ref[r, slot] = pure[r * B : r * B + B, e * B : e * B + B]

    for j in range(6):
        in_block(core_ref, functools.partial(finish, j))


def gradient_kernel(
    core_ref, s_ref, own_g, mate_g, n2_r, n2_x, f2_r, f2_x, n4_r, n4_x, f4_r, f4_x, n6_r, n6_x,
    own_p, pk_ref, third_s, t_ref,
    grad_ref,
    gk, gb, lhs,
):
    p = core_ref[0]
    zero = jnp.zeros((B, B), BF16)

    def assemble(core):
        full = (own_g, mate_g) if core == 0 else (mate_g, own_g)
        stores = (
            by_side(core, True, n2_r, n2_x), by_side(core, False, f2_r, f2_x),
            by_side(core, True, n4_r, n4_x), by_side(core, False, f4_r, f4_x),
            by_side(core, True, n6_r, n6_x),
        )

        def block(m, slot):
            if 10 <= m <= 13:
                return full[(m - 10) // 2][rows_of(((m - 10) % 2) * SLOTS + slot), :]
            side = 0 if m < 10 else 1
            t = 10 - m if m < 10 else m - 13
            at = slot - t if side == 0 else slot
            if t % 2 == 0:
                at += SLOTS - (t - 1)
            return stores[(t - 1) // 2][side][rows_of(at), :]

        for pair in range(core, core + 6):
            for e in range(2):
                cols = pl.ds(e * B, B)
                for hole in ((0, 12, 13), (0, 1, 13))[e]:
                    gk[pair, pl.ds(hole * B, B), cols] = zero
                j = 2 * pair + e
                for m in range(j, j + 11):
                    gk[pair, pl.ds((m - 2 * pair + 1) * B, B), cols] = block(m, j - m + 10)

    for core in range(2):
        pl.when(p == core)(functools.partial(assemble, core))

    for r in range(2):
        lhs[pl.ds(r * B, B), pl.ds((11 if r == 0 else 0) * B, B)] = zero
        for slot in range(SLOTS):
            lhs[pl.ds(r * B, B), pl.ds((slot + r) * B, B)] = own_p[rows_of(r * SLOTS + slot), :]

    def tile(delta, j):
        k = j + delta
        count = (12 - 2 * abs(delta)) * B
        left = pk_ref[k + p, :, pl.ds(max(0, -delta) * 2 * B, count)]
        right = gk[j + p, pl.ds((max(0, delta) * 2 + 1) * B, count), :]
        found = jnp.dot(left, right, preferred_element_type=F32)
        found = found * mask_tile(t_ref, 2 * (k + p), 2 * (j + p), 2)
        given = gk[j + p, pl.ds((2 * delta + 6) * B, 256), :].astype(F32)
        gb[pl.ds(pl.multiple_of(k * 256, 256), 256), pl.ds(pl.multiple_of(j * 256, 256), 256)] = (
            3.0 * given - 2.0 * found
        ).astype(BF16)

    tile_loop(core_ref, tile)

    def finish(j):
        low, count = span(2 * j)
        cols = pl.ds(low * B, count * B)
        right = pk_ref[j + p, :, pl.ds((low + 5 - 2 * j) * B, count * B)]
        total = lax.dot_general(gb[pl.ds(5 * B, 256), cols], right, NT, preferred_element_type=F32)
        total += jnp.dot(
            lhs[:, cols], gb[pl.ds(low * B, count * B), pl.ds(j * 256, 256)],
            preferred_element_type=F32,
        )
        total -= 2.0 * third_s[:, pl.ds(j * 256, 256)]
        for r in range(2):
            for e in range(2):
                slot = 2 * j + e - r
                if 0 <= slot < SLOTS:
                    keep = s_ref[r, slot].astype(F32)
                    grad_ref[r, slot] = total[r * B : r * B + B, e * B : e * B + B] * keep

    for j in range(6):
        in_block(core_ref, functools.partial(finish, j))


SMEM = pl.BlockSpec(memory_space=pltpu.SMEM)
VMEM = pl.BlockSpec(memory_space=pltpu.VMEM)
ANY = pl.BlockSpec(memory_space=pl.ANY)


def flat(blocks, extra=0):
    return jax.ShapeDtypeStruct((blocks * B + extra, B), BF16)


def on_device(density, cotangent, s_mask, t_mask):
    devices = lax.axis_size(AXES)
    core = (lax.axis_index(AXES) % 2).astype(jnp.int32).reshape(1)
    swap = [(i, i ^ 1) for i in range(devices)]

    def send(message, pair):
        return lax.ppermute(message, AXES, route(pair, devices))

    def to_mate(message):
        return lax.ppermute(message, AXES, swap)

    def both_to_mate(messages):
        got = to_mate(jnp.concatenate(messages, axis=0))
        places = [0]
        for message in messages:
            places.append(places[-1] + message.shape[0])
        return [got[a:b] for a, b in zip(places, places[1:])]

    params = pltpu.CompilerParams(vmem_limit_bytes=30 * 1024 * 1024)
    p_pairs = (NEAR2, FAR2, NEAR4)
    packed = pl.pallas_call(
        pack,
        in_specs=[SMEM, SMEM, SMEM, ANY, ANY],
        out_specs=[VMEM] * 10,
        out_shape=[flat(22, MASK_ROWS)]
        + [flat(P_BLOCKS[pair], MASK_ROWS) for pair in p_pairs]
        + [flat(22)]
        + [flat(g_blocks(pair)) for pair in G_PAIRS],
        scratch_shapes=[
            pltpu.VMEM(density.shape, BF16), pltpu.VMEM(cotangent.shape, BF16),
            pltpu.SemaphoreType.DMA((2,)),
        ],
        compiler_params=params,
        name="pack",
    )(core, s_mask, t_mask, density, cotangent)
    p_out, g_out = packed[:4], packed[4:]
    p_far = [send(message, pair) for message, pair in zip(p_out[1:], p_pairs)]
    g_far = [send(message, pair) for message, pair in zip(g_out[1:], G_PAIRS)]
    mate_p = to_mate(p_out[0])
    mate_g = to_mate(g_out[0])
    p_mate = both_to_mate(p_far)
    def zipped(far, mate):
        return [one for both in zip(far, mate) for one in both]

    purified, third, pk, t_all = pl.pallas_call(
        square_kernel,
        in_specs=[SMEM] + [VMEM] * 9,
        out_specs=[VMEM] * 4,
        out_shape=[
            jax.ShapeDtypeStruct((2, SLOTS, B, B), F32),
            jax.ShapeDtypeStruct((256, 1536), F32),
            jax.ShapeDtypeStruct((7, 256, 1536), BF16),
            jax.ShapeDtypeStruct((14 * 16, B), F32),
        ],
        scratch_shapes=[pltpu.VMEM((1536, 1536), BF16), pltpu.VMEM((512, 1536), BF16)],
        cost_estimate=pl.CostEstimate(flops=10**6, bytes_accessed=10**4, transcendentals=0),
        compiler_params=params,
        name="square",
    )(core, p_out[0], mate_p, *zipped(p_far, p_mate), g_out[0])

    *g_far, t_all = lax.optimization_barrier((*g_far, t_all))
    g_mate = [to_mate(g_far[0]), to_mate(g_far[1]), *both_to_mate(g_far[2:])]

    gradient = pl.pallas_call(
        gradient_kernel,
        in_specs=[SMEM, SMEM] + [VMEM] * 16,
        out_specs=VMEM,
        out_shape=jax.ShapeDtypeStruct((2, SLOTS, B, B), F32),
        scratch_shapes=[
            pltpu.VMEM((7, 14 * B, 256), BF16), pltpu.VMEM((1536, 1536), BF16),
            pltpu.VMEM((256, 1536), BF16),
        ],
        cost_estimate=pl.CostEstimate(flops=7 * 10**9, bytes_accessed=16 * 10**6, transcendentals=0),
        compiler_params=params,
        name="gradient",
    )(core, s_mask, g_out[0], mate_g, *zipped(g_far, g_mate), p_out[0], pk, third, t_all)
    return (purified, gradient)


def solution(mesh):
    band = P(AXES, None, None, None)
    in_specs = (band, band, P(AXES, None), P(AXES, None))
    return jax.shard_map(
        on_device, mesh=mesh, in_specs=in_specs, out_specs=(band, band), check_vma=False
    )
```

time: 113 us -> 90.4 us (0.80)
  the two profiles are of different devices: /device:TPU:25 before, /device:TPU:57 now
where the time goes in v2:
time: 90.4 us; the launch traced here: 90 us
  starting transfers between devices  42.3 us (47%)
  Pallas kernels  26.1 us (29%)
  waiting for transfers between devices  17 us (19%)
  local copies, waits for them, and re-layouts  3.69 us (4%)
    ppermute x8, starting transfers between devices, send(): return lax.ppermute(message, AXES, route(pair, devices))  28 us
    ppermute x6, starting transfers between devices, to_mate(): return lax.ppermute(message, AXES, swap)  14.3 us
    ppermute x8, waiting for transfers between devices, send(): return lax.ppermute(message, AXES, route(pair, devices))  13.4 us
    pallas_call x1, Pallas kernels, on_device(): pl.pallas_call(square_kernel, in_specs=[SMEM] + [VMEM] * 9, out_specs=[VM...  12.6 us
    pallas_call x1, Pallas kernels, on_device(): pl.pallas_call(gradient_kernel, in_specs=[SMEM, SMEM] + [VMEM] * 16, out_...  11.7 us
    unnamed x10, local copies, waits for them, and re-layouts  3.57 us
    ppermute x6, waiting for transfers between devices, to_mate(): return lax.ppermute(message, AXES, swap)  3.56 us
    pallas_call x1, Pallas kernels, on_device(): pl.pallas_call(pack, in_specs=[SMEM, SMEM, SMEM, ANY, ANY], out_specs=[VM...  1.88 us
  transfers between devices with their start and end apart: 14, of which 4 were waited for; matrix products, arithmetic and copies ran while one was open for 0% of the time, Pallas kernels for 14%

profile of v2, /device:TPU:57, one launch (start us, length us, event | category | flops | bytes accessed | tf_op | source)
XLA Modules:
  0.0 90.0 jit_solution(1311591047843851219)
XLA Ops:
  0.7 1.1 %copy-done = bf16[2,11,128,128]{3,2,1,0:T(8,128)(2,1)S(1)} copy-done((bf16[2,11,128,128]{3,2,1,0:T(8,128)(2,1)S(1)}, bf16[2,11,128,128]{3,2,1,0:T(8,128)(2,1)}, u32[]{:S(2)}) %copy-start) | copy-done | bytes 720920
  1.8 1.1 %copy-done.1 = bf16[2,11,128,128]{3,2,1,0:T(8,128)(2,1)S(1)} copy-done((bf16[2,11,128,128]{3,2,1,0:T(8,128)(2,1)S(1)}, bf16[2,11,128,128]{3,2,1,0:T(8,128)(2,1)}, u32[]{:S(2)}) %copy-start.1) | copy-done | bytes 720920
  2.9 0.7 copy-done.2
  3.5 0.7 copy-done.3
  4.2 1.9 %pack.1 = (bf16[2848,128]{1,0:T(8,128)(2,1)S(1)}, bf16[1696,128]{1,0:T(8,128)(2,1)S(1)}, bf16[1568,128]{1,0:T(8,128)(2,1)S(1)}, bf16[800,128]{1,0:T(8,128)(2,1)S...) custom-call(s32[1]{0:T(128)} %bitcast.core_ref, ...), custom_call_target="tpu_custom_call" | custom-call | tf_op jit(solution)/shard_map/pack/pallas_call | solution.py:358
  6.1 3.1 %collective-permute-start.1 = (bf16[1696,128]{1,0:T(8,128)(2,1)S(1)}, bf16[1696,128]{1,0:T(8,128)(2,1)S(1)}, u32[]{:S(2)}, u32[]{:S(2)}) collective-permute-start(bf16[1696,128]{1,0:T(8,128)(2,1)S(1)} %get-tuple-element.23), channel_id=1, source_target_pairs={{1,3},{2,0},{3,5},{4,2},{5,7},{6,4},{7,9},{8,6},{9,11},{10,8},{11,... | collective-permute-start | bytes 1302536 | tf_op jit(solution)/shard_map/ppermute | solution.py:344
  9.2 3.1 %collective-permute-start.2 = (bf16[1568,128]{1,0:T(8,128)(2,1)S(1)}, bf16[1568,128]{1,0:T(8,128)(2,1)S(1)}, u32[]{:S(2)}, u32[]{:S(2)}) collective-permute-start(bf16[1568,128]{1,0:T(8,128)(2,1)S(1)} %get-tuple-element.24), channel_id=1, source_target_pairs={{0,2},{2,4},{3,1},{4,6},{5,3},{6,8},{7,5},{8,10},{9,7},{10,12},{11... | collective-permute-start | bytes 1204232 | tf_op jit(solution)/shard_map/ppermute | solution.py:344
  12.3 3.5 %collective-permute-start.3 = (bf16[800,128]{1,0:T(8,128)(2,1)S(1)}, bf16[800,128]{1,0:T(8,128)(2,1)S(1)}, u32[]{:S(2)}, u32[]{:S(2)}) collective-permute-start(bf16[800,128]{1,0:T(8,128)(2,1)S(1)} %get-tuple-element.25), channel_id=1, source_target_pairs={{1,5},{3,7},{4,0},{5,9},{6,2},{7,11},{8,4},{9,13},{10,6},{11,15},{... | collective-permute-start | bytes 614408 | tf_op jit(solution)/shard_map/ppermute | solution.py:344
  15.9 7.2 %collective-permute-done.3.n4_r = bf16[800,128]{1,0:T(8,128)(2,1)S(1)} collective-permute-done((bf16[800,128]{1,0:T(8,128)(2,1)S(1)}, bf16[800,128]{1,0:T(8,128)(2,1)S(1)}, u32[]{:S(2)}, u32[]{:S(2)}) %collective-permute-start.3) | collective-permute-done | bytes 204832 | tf_op jit(solution)/shard_map/ppermute | solution.py:344
  23.1 6.2 %collective-permute-done.2.f2_r = bf16[1568,128]{1,0:T(8,128)(2,1)S(1)} collective-permute-done((bf16[1568,128]{1,0:T(8,128)(2,1)S(1)}, bf16[1568,128]{1,0:T(8,128)(2,1)S(1)}, u32[]{:S(2)}, u32[]{:S(2)}) %collective-permute-start.2) | collective-permute-done | bytes 401440 | tf_op jit(solution)/shard_map/ppermute | solution.py:344
  29.3 0.0 collective-permute-done.1.n2_r
  29.3 0.1 pad_maximum_fusion
  29.3 0.7 collective-permute-start.4
  30.1 0.1 collective-permute-start
  30.2 2.2 %collective-permute-start.6 = (bf16[2432,128]{1,0:T(8,128)(2,1)S(1)}, bf16[2432,128]{1,0:T(8,128)(2,1)S(1)}, u32[]{:S(2)}, u32[]{:S(2)}) collective-permute-start(bf16[2432,128]{1,0:T(8,128)(2,1)S(1)} %get-tuple-element.28), channel_id=1, source_target_pairs={{1,3},{2,0},{3,5},{4,2},{5,7},{6,4},{7,9},{8,6},{9,11},{10,8},{11,... | collective-permute-start | bytes 1867784 | tf_op jit(solution)/shard_map/ppermute | solution.py:344
  32.4 4.0 %collective-permute-start.7 = (bf16[1920,128]{1,0:T(8,128)(2,1)S(1)}, bf16[1920,128]{1,0:T(8,128)(2,1)S(1)}, u32[]{:S(2)}, u32[]{:S(2)}) collective-permute-start(bf16[1920,128]{1,0:T(8,128)(2,1)S(1)} %get-tuple-element.29), channel_id=1, source_target_pairs={{0,2},{2,4},{3,1},{4,6},{5,3},{6,8},{7,5},{8,10},{9,7},{10,12},{11... | collective-permute-start | bytes 1474568 | tf_op jit(solution)/shard_map/ppermute | solution.py:344
  36.4 3.5 %collective-permute-start.8 = (bf16[1408,128]{1,0:T(8,128)(2,1)S(1)}, bf16[1408,128]{1,0:T(8,128)(2,1)S(1)}, u32[]{:S(2)}, u32[]{:S(2)}) collective-permute-start(bf16[1408,128]{1,0:T(8,128)(2,1)S(1)} %get-tuple-element.30), channel_id=1, source_target_pairs={{1,5},{3,7},{4,0},{5,9},{6,2},{7,11},{8,4},{9,13},{10,6},{11,15},{... | collective-permute-start | bytes 1081352 | tf_op jit(solution)/shard_map/ppermute | solution.py:344
  39.9 6.6 %collective-permute-start.9 = (bf16[896,128]{1,0:T(8,128)(2,1)S(1)}, bf16[896,128]{1,0:T(8,128)(2,1)S(1)}, u32[]{:S(2)}, u32[]{:S(2)}) collective-permute-start(bf16[896,128]{1,0:T(8,128)(2,1)S(1)} %get-tuple-element.31), channel_id=1, source_target_pairs={{0,4},{2,6},{4,8},{5,1},{6,10},{7,3},{8,12},{9,5},{10,14},{11,7},{... | collective-permute-start | bytes 688136 | tf_op jit(solution)/shard_map/ppermute | solution.py:344
  46.6 1.9 %collective-permute-start.10 = (bf16[384,128]{1,0:T(8,128)(2,1)S(1)}, bf16[384,128]{1,0:T(8,128)(2,1)S(1)}, u32[]{:S(2)}, u32[]{:S(2)}) collective-permute-start(bf16[384,128]{1,0:T(8,128)(2,1)S(1)} %get-tuple-element.32), channel_id=1, source_target_pairs={{1,7},{3,9},{5,11},{6,0},{7,13},{8,2},{9,15},{10,4},{11,17},{12,6}... | collective-permute-start | bytes 294920 | tf_op jit(solution)/shard_map/ppermute | solution.py:344
  48.6 12.6 %square.1 = (f32[2,11,128,128]{3,2,1,0:T(8,128)}, f32[256,1536]{1,0:T(8,128)S(1)}, bf16[7,256,1536]{2,1,0:T(8,128)(2,1)S(1)}, f32[224,128]{1,0:T(8,128)S(1)}) custom-call(s32[1]{0:T(128)} %bitcast.core_ref, bf16[2848,128]{1,0:T(8,128)(2,1)S(1)} %get-tuple-element.22.own_p, bf16[2848,128]{1,0:T(8,128)(2,1)S(1)} %collective-permute-done.mate_p, ...), custom_call_target="tpu_custom_call" | custom-call | flops 1000000 | bytes 10000 | tf_op jit(solution)/shard_map/square/pallas_call | solution.py:382
  61.2 0.0 collective-permute-done.10.n6_r
  61.2 12.8 %collective-permute-start.5 = (bf16[2816,128]{1,0:T(8,128)(2,1)S(1)}, bf16[2816,128]{1,0:T(8,128)(2,1)S(1)}, u32[]{:S(2)}, u32[]{:S(2)}) collective-permute-start(bf16[2816,128]{1,0:T(8,128)(2,1)S(1)} %get-tuple-element.26.own_g), channel_id=1, source_target_pairs={{0,1},{1,0},{2,3},{3,2},{4,5},{5,4},{6,7},{7,6},{8,9},{9,8},{10,11... | collective-permute-start | bytes 2162696 | tf_op jit(solution)/shard_map/ppermute | solution.py:347
  74.0 0.0 collective-permute-done.8.n4_r
  74.0 0.0 collective-permute-done.7.f2_r
  74.0 0.1 collective-permute-start.13
  74.1 0.5 collective-permute-start.11
  74.6 0.1 collective-permute-start.12
  74.7 2.0 %collective-permute-done.13 = bf16[2688,128]{1,0:T(8,128)(2,1)S(1)} collective-permute-done((bf16[2688,128]{1,0:T(8,128)(2,1)S(1)}, bf16[2688,128]{1,0:T(8,128)(2,1)S(1)}, u32[]{:S(2)}, u32[]{:S(2)}) %collective-permute-start.13) | collective-permute-done | bytes 688160 | tf_op jit(solution)/shard_map/ppermute | solution.py:347
  76.8 0.0 collective-permute-done.5.mate_g
  76.8 1.5 %collective-permute-done.12.f2_x = bf16[1920,128]{1,0:T(8,128)(2,1)S(1)} collective-permute-done((bf16[1920,128]{1,0:T(8,128)(2,1)S(1)}, bf16[1920,128]{1,0:T(8,128)(2,1)S(1)}, u32[]{:S(2)}, u32[]{:S(2)}) %collective-permute-start.12) | collective-permute-done | bytes 491552 | tf_op jit(solution)/shard_map/ppermute | solution.py:347
  78.4 0.0 collective-permute-done.11.n2_x
  78.4 11.7 %gradient.1 = f32[2,11,128,128]{3,2,1,0:T(8,128)} custom-call(s32[1]{0:T(128)} %bitcast.core_ref, s32[2,11]{1,0:T(2,128)S(1)} %copy-done.4, bf16[2816,128]{1,0:T(8,128)(2,1)S(1)} %get-tuple-element.26.own_g, bf16[2816,128]{1,0:T(8,128)(2,1)S(1)} %collective-permute-done.5.mate_g, bf16[2432,128]{1,0:T(8,128)(2,1)S(1)} %collective-permute-done.6.n2_r, ...), custom_call_target="tpu_custom_call" | custom-call | flops 7000000000 | bytes 16000000 | tf_op jit(solution)/shard_map/gradient/pallas_call | solution.py:401
  (17 shorter events, 0.2 us)
Async XLA Ops:
  0.6 1.1 %copy-start = (bf16[2,11,128,128]{3,2,1,0:T(8,128)(2,1)S(1)}, bf16[2,11,128,128]{3,2,1,0:T(8,128)(2,1)}, u32[]{:S(2)}) copy-start(bf16[2,11,128,128]{3,2,1,0:T(8,128)(2,1)} %density_any.1) | copy-start | bytes 2162692
  1.8 1.1 %copy-start.1 = (bf16[2,11,128,128]{3,2,1,0:T(8,128)(2,1)S(1)}, bf16[2,11,128,128]{3,2,1,0:T(8,128)(2,1)}, u32[]{:S(2)}) copy-start(bf16[2,11,128,128]{3,2,1,0:T(8,128)(2,1)} %cotangent_any.1) | copy-start | bytes 2162692
  2.9 0.7 copy-start.2
  3.5 0.7 copy-start.3
  6.1 23.2 %collective-permute-start.1 = (bf16[1696,128]{1,0:T(8,128)(2,1)S(1)}, bf16[1696,128]{1,0:T(8,128)(2,1)S(1)}, u32[]{:S(2)}, u32[]{:S(2)}) collective-permute-start(bf16[1696,128]{1,0:T(8,128)(2,1)S(1)} %get-tuple-element.23), channel_id=1, source_target_pairs={{1,3},{2,0},{3,5},{4,2},{5,7},{6,4},{7,9},{8,6},{9,11},{10,8},{11,... | collective-permute-start | bytes 1302536 | tf_op jit(solution)/shard_map/ppermute | solution.py:344
  9.2 20.0 %collective-permute-start.2 = (bf16[1568,128]{1,0:T(8,128)(2,1)S(1)}, bf16[1568,128]{1,0:T(8,128)(2,1)S(1)}, u32[]{:S(2)}, u32[]{:S(2)}) collective-permute-start(bf16[1568,128]{1,0:T(8,128)(2,1)S(1)} %get-tuple-element.24), channel_id=1, source_target_pairs={{0,2},{2,4},{3,1},{4,6},{5,3},{6,8},{7,5},{8,10},{9,7},{10,12},{11... | collective-permute-start | bytes 1204232 | tf_op jit(solution)/shard_map/ppermute | solution.py:344
  12.3 10.8 %collective-permute-start.3 = (bf16[800,128]{1,0:T(8,128)(2,1)S(1)}, bf16[800,128]{1,0:T(8,128)(2,1)S(1)}, u32[]{:S(2)}, u32[]{:S(2)}) collective-permute-start(bf16[800,128]{1,0:T(8,128)(2,1)S(1)} %get-tuple-element.25), channel_id=1, source_target_pairs={{1,5},{3,7},{4,0},{5,9},{6,2},{7,11},{8,4},{9,13},{10,6},{11,15},{... | collective-permute-start | bytes 614408 | tf_op jit(solution)/shard_map/ppermute | solution.py:344
  29.3 17.2 %collective-permute-start.4 = (bf16[4064,128]{1,0:T(8,128)(2,1)S(1)}, bf16[4064,128]{1,0:T(8,128)(2,1)S(1)}, u32[]{:S(2)}, u32[]{:S(2)}) collective-permute-start(bf16[4064,128]{1,0:T(8,128)(2,1)S(1)} %pad_maximum_fusion), channel_id=1, source_target_pairs={{0,1},{1,0},{2,3},{3,2},{4,5},{5,4},{6,7},{7,6},{8,9},{9,8},{10,11... | collective-permute-start | bytes 3121160 | tf_op jit(solution)/shard_map/ppermute | solution.py:347
  30.1 9.8 %collective-permute-start = (bf16[2848,128]{1,0:T(8,128)(2,1)S(1)}, bf16[2848,128]{1,0:T(8,128)(2,1)S(1)}, u32[]{:S(2)}, u32[]{:S(2)}) collective-permute-start(bf16[2848,128]{1,0:T(8,128)(2,1)S(1)} %get-tuple-element.22.own_p), channel_id=1, source_target_pairs={{0,1},{1,0},{2,3},{3,2},{4,5},{5,4},{6,7},{7,6},{8,9},{9,8},{10,11... | collective-permute-start | bytes 2187272 | tf_op jit(solution)/shard_map/ppermute | solution.py:347
  30.2 43.8 %collective-permute-start.6 = (bf16[2432,128]{1,0:T(8,128)(2,1)S(1)}, bf16[2432,128]{1,0:T(8,128)(2,1)S(1)}, u32[]{:S(2)}, u32[]{:S(2)}) collective-permute-start(bf16[2432,128]{1,0:T(8,128)(2,1)S(1)} %get-tuple-element.28), channel_id=1, source_target_pairs={{1,3},{2,0},{3,5},{4,2},{5,7},{6,4},{7,9},{8,6},{9,11},{10,8},{11,... | collective-permute-start | bytes 1867784 | tf_op jit(solution)/shard_map/ppermute | solution.py:344
  32.4 41.6 %collective-permute-start.7 = (bf16[1920,128]{1,0:T(8,128)(2,1)S(1)}, bf16[1920,128]{1,0:T(8,128)(2,1)S(1)}, u32[]{:S(2)}, u32[]{:S(2)}) collective-permute-start(bf16[1920,128]{1,0:T(8,128)(2,1)S(1)} %get-tuple-element.29), channel_id=1, source_target_pairs={{0,2},{2,4},{3,1},{4,6},{5,3},{6,8},{7,5},{8,10},{9,7},{10,12},{11... | collective-permute-start | bytes 1474568 | tf_op jit(solution)/shard_map/ppermute | solution.py:344
  36.4 37.6 %collective-permute-start.8 = (bf16[1408,128]{1,0:T(8,128)(2,1)S(1)}, bf16[1408,128]{1,0:T(8,128)(2,1)S(1)}, u32[]{:S(2)}, u32[]{:S(2)}) collective-permute-start(bf16[1408,128]{1,0:T(8,128)(2,1)S(1)} %get-tuple-element.30), channel_id=1, source_target_pairs={{1,5},{3,7},{4,0},{5,9},{6,2},{7,11},{8,4},{9,13},{10,6},{11,15},{... | collective-permute-start | bytes 1081352 | tf_op jit(solution)/shard_map/ppermute | solution.py:344
  39.9 34.0 %collective-permute-start.9 = (bf16[896,128]{1,0:T(8,128)(2,1)S(1)}, bf16[896,128]{1,0:T(8,128)(2,1)S(1)}, u32[]{:S(2)}, u32[]{:S(2)}) collective-permute-start(bf16[896,128]{1,0:T(8,128)(2,1)S(1)} %get-tuple-element.31), channel_id=1, source_target_pairs={{0,4},{2,6},{4,8},{5,1},{6,10},{7,3},{8,12},{9,5},{10,14},{11,7},{... | collective-permute-start | bytes 688136 | tf_op jit(solution)/shard_map/ppermute | solution.py:344
  46.6 14.6 %collective-permute-start.10 = (bf16[384,128]{1,0:T(8,128)(2,1)S(1)}, bf16[384,128]{1,0:T(8,128)(2,1)S(1)}, u32[]{:S(2)}, u32[]{:S(2)}) collective-permute-start(bf16[384,128]{1,0:T(8,128)(2,1)S(1)} %get-tuple-element.32), channel_id=1, source_target_pairs={{1,7},{3,9},{5,11},{6,0},{7,13},{8,2},{9,15},{10,4},{11,17},{12,6}... | collective-permute-start | bytes 294920 | tf_op jit(solution)/shard_map/ppermute | solution.py:344
  61.2 17.2 %copy-start.4 = (s32[2,11]{1,0:T(2,128)S(1)}, s32[2,11]{1,0:T(2,128)}, u32[]{:S(2)}) copy-start(s32[2,11]{1,0:T(2,128)} %s_ref.3) | copy-start | bytes 268
  61.2 15.6 %collective-permute-start.5 = (bf16[2816,128]{1,0:T(8,128)(2,1)S(1)}, bf16[2816,128]{1,0:T(8,128)(2,1)S(1)}, u32[]{:S(2)}, u32[]{:S(2)}) collective-permute-start(bf16[2816,128]{1,0:T(8,128)(2,1)S(1)} %get-tuple-element.26.own_g), channel_id=1, source_target_pairs={{0,1},{1,0},{2,3},{3,2},{4,5},{5,4},{6,7},{7,6},{8,9},{9,8},{10,11... | collective-permute-start | bytes 2162696 | tf_op jit(solution)/shard_map/ppermute | solution.py:347
  74.0 2.7 %collective-permute-start.13 = (bf16[2688,128]{1,0:T(8,128)(2,1)S(1)}, bf16[2688,128]{1,0:T(8,128)(2,1)S(1)}, u32[]{:S(2)}, u32[]{:S(2)}) collective-permute-start(bf16[2688,128]{1,0:T(8,128)(2,1)S(1)} %pad_maximum_fusion.1), channel_id=1, source_target_pairs={{0,1},{1,0},{2,3},{3,2},{4,5},{5,4},{6,7},{7,6},{8,9},{9,8},{10,11... | collective-permute-start | bytes 2064392 | tf_op jit(solution)/shard_map/ppermute | solution.py:347
  74.1 4.2 %collective-permute-start.11 = (bf16[2432,128]{1,0:T(8,128)(2,1)S(1)}, bf16[2432,128]{1,0:T(8,128)(2,1)S(1)}, u32[]{:S(2)}, u32[]{:S(2)}) collective-permute-start(bf16[2432,128]{1,0:T(8,128)(2,1)S(1)} %collective-permute-done.6.n2_r), channel_id=1, source_target_pairs={{0,1},{1,0},{2,3},{3,2},{4,5},{5,4},{6,7},{7,6},{8,9},{9,8},{10,11... | collective-permute-start | bytes 1867784 | tf_op jit(solution)/shard_map/ppermute | solution.py:347
  74.6 3.7 %collective-permute-start.12 = (bf16[1920,128]{1,0:T(8,128)(2,1)S(1)}, bf16[1920,128]{1,0:T(8,128)(2,1)S(1)}, u32[]{:S(2)}, u32[]{:S(2)}) collective-permute-start(bf16[1920,128]{1,0:T(8,128)(2,1)S(1)} %collective-permute-done.7.f2_r), channel_id=1, source_target_pairs={{0,1},{1,0},{2,3},{3,2},{4,5},{5,4},{6,7},{7,6},{8,9},{9,8},{10,11... | collective-permute-start | bytes 1474568 | tf_op jit(solution)/shard_map/ppermute | solution.py:347

commit v3 on v2

--- a/solution.py
+++ b/solution.py
@@ -15,37 +15,35 @@
 BF16 = jnp.bfloat16
 F32 = jnp.float32
 
-NEAR2, FAR2, NEAR4, FAR4, NEAR6 = (1, 2), (3, 4), (5, 6), (7, 8), (9, 10)
-P_BLOCKS = {NEAR2: 13, FAR2: 12, NEAR4: 6}
-G_PAIRS = (NEAR2, FAR2, NEAR4, FAR4, NEAR6)
-
-
-def g_blocks(pair):
-    return sum(SLOTS - t for t in pair)
-
-
-def is_near(pair):
-    return pair in (NEAR2, NEAR4, NEAR6)
-
-
-def hop(pair):
-    return {NEAR2: 2, FAR2: 2, NEAR4: 4, FAR4: 4, NEAR6: 6}[pair]
-
-
-def route(pair, devices):
+G_OFFSET = 22 * B + MASK_ROWS
+
+
+def place_in(ts, t):
+    return sum(SLOTS - u for u in ts if u < t)
+
+
+ONE_CHIP, TWO_CHIPS, THREE_CHIPS = (1, 2, 3, 4), (5, 6, 7, 8), (9, 10)
+ONE_BLOCKS, TWO_BLOCKS, THREE_BLOCKS = (
+    place_in(ts, SLOTS) for ts in (ONE_CHIP, TWO_CHIPS, THREE_CHIPS)
+)
+N2_ROWS = 13 * B + MASK_ROWS
+F2_ROWS = 12 * B + MASK_ROWS
+
+
+def route(hop, near, devices):
     pairs = []
     for source in range(devices):
-        up = (source % 2 == 1) == is_near(pair)
-        target = source + hop(pair) if up else source - hop(pair)
+        up = (source % 2 == 1) == near
+        target = source + hop if up else source - hop
         if 0 <= target < devices:
             pairs.append((source, target))
     return pairs
 
 
-def rows_of(block):
-    start = block * B
+def rows_of(block, base=0):
+    start = block * B + base
     if not isinstance(start, int):
-        start = pl.multiple_of(start, B)
+        start = pl.multiple_of(start, MASK_ROWS)
     return pl.ds(start, B)
 
 
@@ -54,17 +52,23 @@
     return (values_ref[row, slot].astype(F32) * keep).astype(BF16)
 
 
-def pack(
-    core_ref, s_ref, t_ref, density_any, cotangent_any,
-    own_p, near2_ref, far2_ref, near4_ref, own_g, n2_g, f2_g, n4_g, f4_g, n6_g,
-    density_ref, cotangent_ref, sems,
+def pack_own(
+    core_ref, s_any, t_any, density_any, cotangent_any,
+    near2_ref, far2_ref, near4_ref, own_ref, w6_ref,
+    density_ref, cotangent_ref, s_ref, t_ref, sems,
 ):
     first = pltpu.make_async_copy(density_any, density_ref, sems.at[0])
     second = pltpu.make_async_copy(cotangent_any, cotangent_ref, sems.at[1])
+    s_copy = pltpu.make_async_copy(s_any, s_ref, sems.at[2])
+    t_copy = pltpu.make_async_copy(t_any, t_ref, sems.at[3])
+    s_copy.start()
+    t_copy.start()
     first.start()
     second.start()
     q = core_ref[0]
     o = 1 - q
+    s_copy.wait()
+    t_copy.wait()
 
     line = lax.broadcasted_iota(jnp.int32, (MASK_ROWS, B), 0)
     mask = jnp.zeros((MASK_ROWS, B), F32)
@@ -72,7 +76,7 @@
         for slot in range(SLOTS):
             mask = jnp.where(line == row * 16 + slot + 2, t_ref[row, slot].astype(F32), mask)
     mask = mask.astype(BF16)
-    for out_ref, count in ((own_p, 22), (near2_ref, 13), (far2_ref, 12), (near4_ref, 6)):
+    for out_ref, count in ((own_ref, 22), (near2_ref, 13), (far2_ref, 12), (near4_ref, 6)):
         out_ref[pl.ds(count * B, MASK_ROWS), :] = mask
 
     first.wait()
@@ -89,20 +93,35 @@
     put(near2_ref, 12, q, 10 * q)
     for row in range(2):
         for slot in range(SLOTS):
-            put(own_p, row * SLOTS + slot, row, slot)
+            put(own_ref, row * SLOTS + slot, row, slot)
 
     second.wait()
-    for pair, out_ref in zip(G_PAIRS, (n2_g, f2_g, n4_g, f4_g, n6_g)):
-        up = q if is_near(pair) else o
-        at = 0
-        for place, t in enumerate(pair):
-            row = up if place == 0 else 1 - up
-            for s in range(SLOTS - t):
-                out_ref[rows_of(at), :] = masked(cotangent_ref, t_ref, row, t * up + s)
-                at += 1
     for row in range(2):
         for slot in range(SLOTS):
-            own_g[rows_of(row * SLOTS + slot), :] = masked(cotangent_ref, t_ref, row, slot)
+            own_ref[rows_of(row * SLOTS + slot, G_OFFSET), :] = masked(
+                cotangent_ref, t_ref, row, slot
+            )
+    at = 0
+    for t in THREE_CHIPS:
+        row = q if t % 2 else o
+        for s in range(SLOTS - t):
+            w6_ref[rows_of(at), :] = masked(cotangent_ref, t_ref, row, t * q + s)
+            at += 1
+
+
+def pack_chip(core_ref, own_ref, mate_ref, w2_ref, w4_ref):
+    q = core_ref[0]
+    o = 1 - q
+    for ts, out_ref in ((ONE_CHIP, w2_ref), (TWO_CHIPS, w4_ref)):
+        at = 0
+        for place, t in enumerate(ts):
+            source = own_ref if place < 2 else mate_ref
+            row = q if t % 2 else o
+            for s in range(SLOTS - t):
+                out_ref[rows_of(at), :] = source[
+                    rows_of(row * SLOTS + t * q + s, G_OFFSET), :
+                ]
+                at += 1
 
 
 def by_side(core, near, received, other):
@@ -144,7 +163,7 @@
 
 
 def square_kernel(
-    core_ref, own_p, mate_p, n2_r, n2_x, f2_r, f2_x, n4_r, n4_x, own_g,
+    core_ref, own, mate, n2_r, f2_r, n4_r, parts_x,
     purified_ref, third_ref, pk_ref, t_ref,
     sw, lhs,
 ):
@@ -152,10 +171,10 @@
     zero = jnp.zeros((B, B), BF16)
 
     def assemble(core):
-        full = (own_p, mate_p) if core == 0 else (mate_p, own_p)
-        n2 = by_side(core, True, n2_r, n2_x)
-        f2 = by_side(core, False, f2_r, f2_x)
-        n4 = by_side(core, True, n4_r, n4_x)
+        full = (own, mate) if core == 0 else (mate, own)
+        n2 = by_side(core, True, (n2_r, 0), (parts_x, 0))
+        f2 = by_side(core, False, (f2_r, 0), (parts_x, N2_ROWS))
+        n4 = by_side(core, True, (n4_r, 0), (parts_x, N2_ROWS + F2_ROWS))
 
         def held(k, slot):
             if 5 <= k <= 8:
@@ -163,19 +182,16 @@
             side = 0 if k < 5 else 1
             t = 5 - k if k < 5 else k - 8
             at = slot if k < 5 else slot - 5
-            if t <= 2:
-                return n2[side][rows_of(6 * (t - 1) + at), :]
-            if t <= 4:
-                return f2[side][rows_of(6 * (t - 3) + at), :]
-            return n4[side][rows_of(at), :]
+            ref, base = n2[side] if t <= 2 else f2[side] if t <= 4 else n4[side]
+            return ref[rows_of(at if t % 2 else at + 6, base), :]
 
         def block(k, slot):
             if 5 <= k <= 8 or (k < 5 and slot <= 5) or (k > 8 and slot >= 5):
                 return held(k, slot)
             if (k, slot) == (4, 10):
-                return n2[0][rows_of(12), :]
+                return n2[0][0][rows_of(12, n2[0][1]), :]
             if (k, slot) == (9, 0):
-                return n2[1][rows_of(12), :]
+                return n2[1][0][rows_of(12, n2[1][1]), :]
             return held(k + slot - 5, 10 - slot).T
 
         for pair in range(core, core + 6):
@@ -193,12 +209,10 @@
                 side = 0 if k < 5 else 1
                 t = 5 - k if k < 5 else k - 8
                 r = (t % 2) if side == 0 else (1 - t % 2)
-                if t <= 2:
-                    part = n2[side][pl.ds(13 * B, MASK_ROWS), :]
-                elif t <= 4:
-                    part = f2[side][pl.ds(12 * B, MASK_ROWS), :]
-                else:
-                    part = n4[side][pl.ds(6 * B, MASK_ROWS), :]
+                (ref, base), count = (
+                    (n2[side], 13) if t <= 2 else (f2[side], 12) if t <= 4 else (n4[side], 6)
+                )
+                part = ref[pl.ds(base + count * B, MASK_ROWS), :]
             t_ref[pl.ds(k * 16, 16), :] = part.astype(F32)[r * 16 : r * 16 + 16, :]
 
     for core in range(2):
@@ -210,8 +224,8 @@
         lhs[pl.ds((2 + r) * B, B), hole] = zero
         for slot in range(SLOTS):
             cols = pl.ds((slot + r) * B, B)
-            lhs[pl.ds(r * B, B), cols] = own_p[rows_of(r * SLOTS + slot), :]
-            lhs[pl.ds((2 + r) * B, B), cols] = own_g[rows_of(r * SLOTS + slot), :]
+            lhs[pl.ds(r * B, B), cols] = own[rows_of(r * SLOTS + slot), :]
+            lhs[pl.ds((2 + r) * B, B), cols] = own[rows_of(r * SLOTS + slot, G_OFFSET), :]
 
     def tile(delta, j):
         k = j + delta
@@ -248,8 +262,7 @@
 
 
 def gradient_kernel(
-    core_ref, s_ref, own_g, mate_g, n2_r, n2_x, f2_r, f2_x, n4_r, n4_x, f4_r, f4_x, n6_r, n6_x,
-    own_p, pk_ref, third_s, t_ref,
+    core_ref, s_ref, own, mate, w2_r, w2_x, w4_r, w6_r, parts_x, pk_ref, third_s, t_ref,
     grad_ref,
     gk, gb, lhs,
 ):
@@ -257,22 +270,22 @@
     zero = jnp.zeros((B, B), BF16)
 
     def assemble(core):
-        full = (own_g, mate_g) if core == 0 else (mate_g, own_g)
+        full = (own, mate) if core == 0 else (mate, own)
         stores = (
-            by_side(core, True, n2_r, n2_x), by_side(core, False, f2_r, f2_x),
-            by_side(core, True, n4_r, n4_x), by_side(core, False, f4_r, f4_x),
-            by_side(core, True, n6_r, n6_x),
+            (ONE_CHIP, by_side(core, True, (w2_r, 0), (w2_x, 0))),
+            (TWO_CHIPS, by_side(core, True, (w4_r, 0), (parts_x, 0))),
+            (THREE_CHIPS, by_side(core, True, (w6_r, 0), (parts_x, TWO_BLOCKS * B))),
         )
 
         def block(m, slot):
             if 10 <= m <= 13:
-                return full[(m - 10) // 2][rows_of(((m - 10) % 2) * SLOTS + slot), :]
+                return full[(m - 10) // 2][rows_of(((m - 10) % 2) * SLOTS + slot, G_OFFSET), :]
             side = 0 if m < 10 else 1
             t = 10 - m if m < 10 else m - 13
             at = slot - t if side == 0 else slot
-            if t % 2 == 0:
-                at += SLOTS - (t - 1)
-            return stores[(t - 1) // 2][side][rows_of(at), :]
+            ts, sides = stores[(t - 1) // 4]
+            ref, base = sides[side]
+            return ref[rows_of(at + place_in(ts, t), base), :]
 
         for pair in range(core, core + 6):
             for e in range(2):
@@ -289,7 +302,7 @@
     for r in range(2):
         lhs[pl.ds(r * B, B), pl.ds((11 if r == 0 else 0) * B, B)] = zero
         for slot in range(SLOTS):
-            lhs[pl.ds(r * B, B), pl.ds((slot + r) * B, B)] = own_p[rows_of(r * SLOTS + slot), :]
+            lhs[pl.ds(r * B, B), pl.ds((slot + r) * B, B)] = own[rows_of(r * SLOTS + slot), :]
 
     def tile(delta, j):
         k = j + delta
@@ -328,7 +341,7 @@
 
 SMEM = pl.BlockSpec(memory_space=pltpu.SMEM)
 VMEM = pl.BlockSpec(memory_space=pltpu.VMEM)
-ANY = pl.BlockSpec(memory_space=pl.ANY)
+HBM = pl.BlockSpec(memory_space=pltpu.HBM)
 
 
 def flat(blocks, extra=0):
@@ -340,48 +353,50 @@
     core = (lax.axis_index(AXES) % 2).astype(jnp.int32).reshape(1)
     swap = [(i, i ^ 1) for i in range(devices)]
 
-    def send(message, pair):
-        return lax.ppermute(message, AXES, route(pair, devices))
-
-    def to_mate(message):
-        return lax.ppermute(message, AXES, swap)
-
-    def both_to_mate(messages):
-        got = to_mate(jnp.concatenate(messages, axis=0))
-        places = [0]
-        for message in messages:
-            places.append(places[-1] + message.shape[0])
-        return [got[a:b] for a, b in zip(places, places[1:])]
+    def send(message, hop, near=True):
+        return lax.ppermute(message, AXES, route(hop, near, devices))
+
+    def to_mate(*messages):
+        return lax.ppermute(jnp.concatenate(messages, axis=0), AXES, swap)
 
     params = pltpu.CompilerParams(vmem_limit_bytes=30 * 1024 * 1024)
-    p_pairs = (NEAR2, FAR2, NEAR4)
-    packed = pl.pallas_call(
-        pack,
-        in_specs=[SMEM, SMEM, SMEM, ANY, ANY],
-        out_specs=[VMEM] * 10,
-        out_shape=[flat(22, MASK_ROWS)]
-        + [flat(P_BLOCKS[pair], MASK_ROWS) for pair in p_pairs]
-        + [flat(22)]
-        + [flat(g_blocks(pair)) for pair in G_PAIRS],
+    n2, f2, n4, own, w6 = pl.pallas_call(
+        pack_own,
+        in_specs=[SMEM, HBM, HBM, HBM, HBM],
+        out_specs=[VMEM] * 5,
+        out_shape=[
+            flat(13, MASK_ROWS), flat(12, MASK_ROWS), flat(6, MASK_ROWS), flat(44, MASK_ROWS),
+            flat(THREE_BLOCKS),
+        ],
         scratch_shapes=[
             pltpu.VMEM(density.shape, BF16), pltpu.VMEM(cotangent.shape, BF16),
-            pltpu.SemaphoreType.DMA((2,)),
+            pltpu.SMEM((2, SLOTS), jnp.int32), pltpu.SMEM((2, SLOTS), jnp.int32),
+            pltpu.SemaphoreType.DMA((4,)),
         ],
+        compiler_params=pltpu.CompilerParams(vmem_limit_bytes=62 * 1024 * 1024),
+        name="pack_own",
+    )(core, s_mask, t_mask, density, cotangent)
+    n2_r = send(n2, 2)
+    f2_r = send(f2, 2, near=False)
+    n4_r = send(n4, 4)
+    mate = to_mate(own)
+    w2, w4 = pl.pallas_call(
+        pack_chip,
+        in_specs=[SMEM, VMEM, VMEM],
+        out_specs=[VMEM] * 2,
+        out_shape=[flat(ONE_BLOCKS), flat(TWO_BLOCKS)],
         compiler_params=params,
-        name="pack",
-    )(core, s_mask, t_mask, density, cotangent)
-    p_out, g_out = packed[:4], packed[4:]
-    p_far = [send(message, pair) for message, pair in zip(p_out[1:], p_pairs)]
-    g_far = [send(message, pair) for message, pair in zip(g_out[1:], G_PAIRS)]
-    mate_p = to_mate(p_out[0])
-    mate_g = to_mate(g_out[0])
-    p_mate = both_to_mate(p_far)
-    def zipped(far, mate):
-        return [one for both in zip(far, mate) for one in both]
+        name="pack_chip",
+    )(core, own, mate)
+    f2_r, w2 = lax.optimization_barrier((f2_r, w2))
+    w2_r = send(w2, 2)
+    w4_r = send(w4, 4)
+    w6_r = send(w6, 6)
+    p_parts = to_mate(n2_r, f2_r, n4_r)
 
     purified, third, pk, t_all = pl.pallas_call(
         square_kernel,
-        in_specs=[SMEM] + [VMEM] * 9,
+        in_specs=[SMEM] + [VMEM] * 6,
         out_specs=[VMEM] * 4,
         out_shape=[
             jax.ShapeDtypeStruct((2, SLOTS, B, B), F32),
@@ -393,14 +408,15 @@
         cost_estimate=pl.CostEstimate(flops=10**6, bytes_accessed=10**4, transcendentals=0),
         compiler_params=params,
         name="square",
-    )(core, p_out[0], mate_p, *zipped(p_far, p_mate), g_out[0])
-
-    *g_far, t_all = lax.optimization_barrier((*g_far, t_all))
-    g_mate = [to_mate(g_far[0]), to_mate(g_far[1]), *both_to_mate(g_far[2:])]
+    )(core, own, mate, n2_r, f2_r, n4_r, p_parts)
+
+    w2_r, w4_g, w6_r, t_all = lax.optimization_barrier((w2_r, w4_r, w6_r, t_all))
+    g_parts = to_mate(w4_g, w6_r)
+    w2_x = to_mate(w2_r)
 
     gradient = pl.pallas_call(
         gradient_kernel,
-        in_specs=[SMEM, SMEM] + [VMEM] * 16,
+        in_specs=[SMEM, SMEM] + [VMEM] * 10,
         out_specs=VMEM,
         out_shape=jax.ShapeDtypeStruct((2, SLOTS, B, B), F32),
         scratch_shapes=[
@@ -410,7 +426,7 @@
         cost_estimate=pl.CostEstimate(flops=7 * 10**9, bytes_accessed=16 * 10**6, transcendentals=0),
         compiler_params=params,
         name="gradient",
-    )(core, s_mask, g_out[0], mate_g, *zipped(g_far, g_mate), p_out[0], pk, third, t_all)
+    )(core, s_mask, own, mate, w2_r, w2_x, w4_g, w6_r, g_parts, pk, third, t_all)
     return (purified, gradient)
 
 

time: 90.4 us -> 84.6 us (0.936)
  the two profiles are of different devices: /device:TPU:57 before, /device:TPU:25 now
where the time goes in v3:
time: 84.6 us; the launch traced here: 84.3 us
  waiting for transfers between devices  28.7 us (34%)
  Pallas kernels  27.3 us (32%)
  starting transfers between devices  26.1 us (31%)
  local copies, waits for them, and re-layouts  1.37 us (2%)
    ppermute x6, waiting for transfers between devices, send(): return lax.ppermute(message, AXES, route(hop, near, devices))  25.6 us
    ppermute x6, starting transfers between devices, send(): return lax.ppermute(message, AXES, route(hop, near, devices))  21.8 us
    pallas_call x1, Pallas kernels, on_device(): pl.pallas_call(square_kernel, in_specs=[SMEM] + [VMEM] * 6, out_specs=[VM...  12.6 us
    pallas_call x1, Pallas kernels, on_device(): pl.pallas_call(gradient_kernel, in_specs=[SMEM, SMEM] + [VMEM] * 10, out_...  11.7 us
    ppermute x4, starting transfers between devices, to_mate(): return lax.ppermute(jnp.concatenate(messages, axis=0), AXES, swap)  4.33 us
    ppermute x4, waiting for transfers between devices, to_mate(): return lax.ppermute(jnp.concatenate(messages, axis=0), AXES, swap)  3.1 us
    pallas_call x1, Pallas kernels, on_device(): pl.pallas_call(pack_own, in_specs=[SMEM, HBM, HBM, HBM, HBM], out_specs=[...  2.93 us
  transfers between devices with their start and end apart: 10, of which 4 were waited for; matrix products, arithmetic and copies ran while one was open for 0% of the time, Pallas kernels for 15%

profile of v3, /device:TPU:25, one launch (start us, length us, event | category | flops | bytes accessed | tf_op | source)
XLA Modules:
  0.0 84.3 jit_solution(15206682611621765093)
XLA Ops:
  0.6 2.9 %pack_own.1 = (bf16[1696,128]{1,0:T(8,128)(2,1)}, bf16[1568,128]{1,0:T(8,128)(2,1)}, bf16[800,128]{1,0:T(8,128)(2,1)}, bf16[5664,128]{1,0:T(8,128)(2,1)}, bf16[384,128]{1,0:T(8,128)(2,1)}) custom-call(s32[1]{0:T(128)} %bitcast.core_ref, s32[2,11]{1,0:T(2,128)} %s_ref.1, s32[2,11]{1,0:T(2,128)} %t_any.1, bf16[2,11,128,128]{3,2,1,0:T(8,128)(2,1)} %density_any.1, ...), custom_call_target="tpu_custom_call" | custom-call | tf_op jit(solution)/shard_map/pack_own/pallas_call | solution.py:363
  3.6 0.8 collective-permute-start
  4.3 3.1 %collective-permute-start.1 = (bf16[1696,128]{1,0:T(8,128)(2,1)}, bf16[1696,128]{1,0:T(8,128)(2,1)S(1)}, u32[]{:S(2)}, u32[]{:S(2)}) collective-permute-start(bf16[1696,128]{1,0:T(8,128)(2,1)} %get-tuple-element.20), channel_id=1, source_target_pairs={{1,3},{2,0},{3,5},{4,2},{5,7},{6,4},{7,9},{8,6},{9,11},{10,8},{11,... | collective-permute-start | bytes 1302536 | tf_op jit(solution)/shard_map/ppermute | solution.py:357
  7.5 8.7 %collective-permute-start.2 = (bf16[1568,128]{1,0:T(8,128)(2,1)}, bf16[1568,128]{1,0:T(8,128)(2,1)S(1)}, u32[]{:S(2)}, u32[]{:S(2)}) collective-permute-start(bf16[1568,128]{1,0:T(8,128)(2,1)} %get-tuple-element.21), channel_id=1, source_target_pairs={{0,2},{2,4},{3,1},{4,6},{5,3},{6,8},{7,5},{8,10},{9,7},{10,12},{11... | collective-permute-start | bytes 1204232 | tf_op jit(solution)/shard_map/ppermute | solution.py:357
  16.1 1.9 %collective-permute-start.3 = (bf16[800,128]{1,0:T(8,128)(2,1)}, bf16[800,128]{1,0:T(8,128)(2,1)S(1)}, u32[]{:S(2)}, u32[]{:S(2)}) collective-permute-start(bf16[800,128]{1,0:T(8,128)(2,1)} %get-tuple-element.24), channel_id=1, source_target_pairs={{1,5},{3,7},{4,0},{5,9},{6,2},{7,11},{8,4},{9,13},{10,6},{11,15},{... | collective-permute-start | bytes 614408 | tf_op jit(solution)/shard_map/ppermute | solution.py:357
  18.1 0.0 collective-permute-done.mate_ref.mate
  18.1 0.0 copy-start
  18.1 1.4 %copy-done = bf16[5664,128]{1,0:T(8,128)(2,1)S(1)} copy-done((bf16[5664,128]{1,0:T(8,128)(2,1)S(1)}, bf16[5664,128]{1,0:T(8,128)(2,1)}, u32[]{:S(2)}) %copy-start) | copy-done | bytes 1450008
  19.4 0.1 pack_chip.1
  19.5 0.0 copy-start.3
  19.6 6.0 %collective-permute-done.2.f2_r = bf16[1568,128]{1,0:T(8,128)(2,1)S(1)} collective-permute-done((bf16[1568,128]{1,0:T(8,128)(2,1)}, bf16[1568,128]{1,0:T(8,128)(2,1)S(1)}, u32[]{:S(2)}, u32[]{:S(2)}) %collective-permute-start.2) | collective-permute-done | bytes 401440 | tf_op jit(solution)/shard_map/ppermute | solution.py:357
  25.6 1.9 %collective-permute-start.5 = (bf16[4352,128]{1,0:T(8,128)(2,1)S(1)}, bf16[4352,128]{1,0:T(8,128)(2,1)S(1)}, u32[]{:S(2)}, u32[]{:S(2)}) collective-permute-start(bf16[4352,128]{1,0:T(8,128)(2,1)S(1)} %get-tuple-element.26), channel_id=1, source_target_pairs={{1,3},{2,0},{3,5},{4,2},{5,7},{6,4},{7,9},{8,6},{9,11},{10,8},{11,... | collective-permute-start | bytes 3342344 | tf_op jit(solution)/shard_map/ppermute | solution.py:357
  27.5 2.4 %collective-permute-done.3.n4_r = bf16[800,128]{1,0:T(8,128)(2,1)S(1)} collective-permute-done((bf16[800,128]{1,0:T(8,128)(2,1)}, bf16[800,128]{1,0:T(8,128)(2,1)S(1)}, u32[]{:S(2)}, u32[]{:S(2)}) %collective-permute-start.3) | collective-permute-done | bytes 204832 | tf_op jit(solution)/shard_map/ppermute | solution.py:357
  29.9 0.0 collective-permute-done.1.n2_r
  29.9 0.1 pad_maximum_fusion
  30.0 3.0 %collective-permute-start.4 = (bf16[4064,128]{1,0:T(8,128)(2,1)S(1)}, bf16[4064,128]{1,0:T(8,128)(2,1)S(1)}, u32[]{:S(2)}, u32[]{:S(2)}) collective-permute-start(bf16[4064,128]{1,0:T(8,128)(2,1)S(1)} %pad_maximum_fusion), channel_id=1, source_target_pairs={{0,1},{1,0},{2,3},{3,2},{4,5},{5,4},{6,7},{7,6},{8,9},{9,8},{10,11... | collective-permute-start | bytes 3121160 | tf_op jit(solution)/shard_map/ppermute | solution.py:360
  33.0 3.5 %collective-permute-start.6 = (bf16[2304,128]{1,0:T(8,128)(2,1)S(1)}, bf16[2304,128]{1,0:T(8,128)(2,1)S(1)}, u32[]{:S(2)}, u32[]{:S(2)}) collective-permute-start(bf16[2304,128]{1,0:T(8,128)(2,1)S(1)} %get-tuple-element.27), channel_id=1, source_target_pairs={{1,5},{3,7},{4,0},{5,9},{6,2},{7,11},{8,4},{9,13},{10,6},{11,15},{... | collective-permute-start | bytes 1769480 | tf_op jit(solution)/shard_map/ppermute | solution.py:357
  36.5 0.0 copy-done.3
  36.5 0.0 copy-start.1
  36.5 0.0 copy-start.2
  36.5 2.7 %collective-permute-start.7 = (bf16[384,128]{1,0:T(8,128)(2,1)S(1)}, bf16[384,128]{1,0:T(8,128)(2,1)S(1)}, u32[]{:S(2)}, u32[]{:S(2)}) collective-permute-start(bf16[384,128]{1,0:T(8,128)(2,1)S(1)} %copy-done.3), channel_id=1, source_target_pairs={{1,7},{3,9},{5,11},{6,0},{7,13},{8,2},{9,15},{10,4},{11,17},{12,6}... | collective-permute-start | bytes 294920 | tf_op jit(solution)/shard_map/ppermute | solution.py:357
  39.2 0.0 collective-permute-done.4.parts_x
  39.2 12.6 %square.1 = (f32[2,11,128,128]{3,2,1,0:T(8,128)}, f32[256,1536]{1,0:T(8,128)S(1)}, bf16[7,256,1536]{2,1,0:T(8,128)(2,1)S(1)}, f32[224,128]{1,0:T(8,128)S(1)}) custom-call(s32[1]{0:T(128)} %bitcast.core_ref, bf16[5664,128]{1,0:T(8,128)(2,1)S(1)} %copy-done, bf16[5664,128]{1,0:T(8,128)(2,1)S(1)} %collective-permute-done.mate_ref.mate, ...), custom_call_target="tpu_custom_call" | custom-call | flops 1000000 | bytes 10000 | tf_op jit(solution)/shard_map/square/pallas_call | solution.py:397
  51.8 17.1 %collective-permute-done.7.w6_r = bf16[384,128]{1,0:T(8,128)(2,1)S(1)} collective-permute-done((bf16[384,128]{1,0:T(8,128)(2,1)S(1)}, bf16[384,128]{1,0:T(8,128)(2,1)S(1)}, u32[]{:S(2)}, u32[]{:S(2)}) %collective-permute-start.7) | collective-permute-done | bytes 98336 | tf_op jit(solution)/shard_map/ppermute | solution.py:357
  68.9 0.0 collective-permute-done.6.w4_r
  68.9 0.0 collective-permute-done.5.w2_r
  68.9 0.0 collective-permute-start.8
  69.0 0.6 collective-permute-start.9
  69.6 3.1 %collective-permute-done.9.parts_x = bf16[2688,128]{1,0:T(8,128)(2,1)S(1)} collective-permute-done((bf16[2688,128]{1,0:T(8,128)(2,1)S(1)}, bf16[2688,128]{1,0:T(8,128)(2,1)S(1)}, u32[]{:S(2)}, u32[]{:S(2)}) %collective-permute-start.9) | collective-permute-done | bytes 688160 | tf_op jit(solution)/shard_map/ppermute | solution.py:360
  72.7 0.0 collective-permute-done.8.w2_x
  72.7 0.0 copy-done.2
  72.7 11.7 %gradient.1 = f32[2,11,128,128]{3,2,1,0:T(8,128)} custom-call(s32[1]{0:T(128)} %bitcast.core_ref, s32[2,11]{1,0:T(2,128)S(1)} %copy-done.2, bf16[5664,128]{1,0:T(8,128)(2,1)S(1)} %copy-done.1, bf16[5664,128]{1,0:T(8,128)(2,1)S(1)} %collective-permute-done.mate_ref.mate, bf16[4352,128]{1,0:T(8,128)(2,1)S(1)} %collective-permute-done.5.w2_r, ...), custom_call_target="tpu_custom_call" | custom-call | flops 7000000000 | bytes 16000000 | tf_op jit(solution)/shard_map/gradient/pallas_call | solution.py:417
  (2 shorter events, 0.0 us)
Async XLA Ops:
  3.6 14.5 %collective-permute-start = (bf16[5664,128]{1,0:T(8,128)(2,1)}, bf16[5664,128]{1,0:T(8,128)(2,1)S(1)}, u32[]{:S(2)}, u32[]{:S(2)}) collective-permute-start(bf16[5664,128]{1,0:T(8,128)(2,1)} %get-tuple-element.19.own_ref.own), channel_id=1, source_target_pairs={{0,1},{1,0},{2,3},{3,2},{4,5},{5,4},{6,7},{7,6},{8,9},{9,8},{10,11... | collective-permute-start | bytes 4349960 | tf_op jit(solution)/shard_map/ppermute | solution.py:360
  4.3 25.6 %collective-permute-start.1 = (bf16[1696,128]{1,0:T(8,128)(2,1)}, bf16[1696,128]{1,0:T(8,128)(2,1)S(1)}, u32[]{:S(2)}, u32[]{:S(2)}) collective-permute-start(bf16[1696,128]{1,0:T(8,128)(2,1)} %get-tuple-element.20), channel_id=1, source_target_pairs={{1,3},{2,0},{3,5},{4,2},{5,7},{6,4},{7,9},{8,6},{9,11},{10,8},{11,... | collective-permute-start | bytes 1302536 | tf_op jit(solution)/shard_map/ppermute | solution.py:357
  7.5 18.1 %collective-permute-start.2 = (bf16[1568,128]{1,0:T(8,128)(2,1)}, bf16[1568,128]{1,0:T(8,128)(2,1)S(1)}, u32[]{:S(2)}, u32[]{:S(2)}) collective-permute-start(bf16[1568,128]{1,0:T(8,128)(2,1)} %get-tuple-element.21), channel_id=1, source_target_pairs={{0,2},{2,4},{3,1},{4,6},{5,3},{6,8},{7,5},{8,10},{9,7},{10,12},{11... | collective-permute-start | bytes 1204232 | tf_op jit(solution)/shard_map/ppermute | solution.py:357
  16.1 13.8 %collective-permute-start.3 = (bf16[800,128]{1,0:T(8,128)(2,1)}, bf16[800,128]{1,0:T(8,128)(2,1)S(1)}, u32[]{:S(2)}, u32[]{:S(2)}) collective-permute-start(bf16[800,128]{1,0:T(8,128)(2,1)} %get-tuple-element.24), channel_id=1, source_target_pairs={{1,5},{3,7},{4,0},{5,9},{6,2},{7,11},{8,4},{9,13},{10,6},{11,15},{... | collective-permute-start | bytes 614408 | tf_op jit(solution)/shard_map/ppermute | solution.py:357
  18.1 1.4 %copy-start = (bf16[5664,128]{1,0:T(8,128)(2,1)S(1)}, bf16[5664,128]{1,0:T(8,128)(2,1)}, u32[]{:S(2)}) copy-start(bf16[5664,128]{1,0:T(8,128)(2,1)} %get-tuple-element.19.own_ref.own) | copy-start | bytes 4349956
  19.5 17.0 %copy-start.3 = (bf16[384,128]{1,0:T(8,128)(2,1)S(1)}, bf16[384,128]{1,0:T(8,128)(2,1)}, u32[]{:S(2)}) copy-start(bf16[384,128]{1,0:T(8,128)(2,1)} %get-tuple-element.28) | copy-start | bytes 294916
  25.6 43.3 %collective-permute-start.5 = (bf16[4352,128]{1,0:T(8,128)(2,1)S(1)}, bf16[4352,128]{1,0:T(8,128)(2,1)S(1)}, u32[]{:S(2)}, u32[]{:S(2)}) collective-permute-start(bf16[4352,128]{1,0:T(8,128)(2,1)S(1)} %get-tuple-element.26), channel_id=1, source_target_pairs={{1,3},{2,0},{3,5},{4,2},{5,7},{6,4},{7,9},{8,6},{9,11},{10,8},{11,... | collective-permute-start | bytes 3342344 | tf_op jit(solution)/shard_map/ppermute | solution.py:357
  30.0 9.2 %collective-permute-start.4 = (bf16[4064,128]{1,0:T(8,128)(2,1)S(1)}, bf16[4064,128]{1,0:T(8,128)(2,1)S(1)}, u32[]{:S(2)}, u32[]{:S(2)}) collective-permute-start(bf16[4064,128]{1,0:T(8,128)(2,1)S(1)} %pad_maximum_fusion), channel_id=1, source_target_pairs={{0,1},{1,0},{2,3},{3,2},{4,5},{5,4},{6,7},{7,6},{8,9},{9,8},{10,11... | collective-permute-start | bytes 3121160 | tf_op jit(solution)/shard_map/ppermute | solution.py:360
  33.0 35.9 %collective-permute-start.6 = (bf16[2304,128]{1,0:T(8,128)(2,1)S(1)}, bf16[2304,128]{1,0:T(8,128)(2,1)S(1)}, u32[]{:S(2)}, u32[]{:S(2)}) collective-permute-start(bf16[2304,128]{1,0:T(8,128)(2,1)S(1)} %get-tuple-element.27), channel_id=1, source_target_pairs={{1,5},{3,7},{4,0},{5,9},{6,2},{7,11},{8,4},{9,13},{10,6},{11,15},{... | collective-permute-start | bytes 1769480 | tf_op jit(solution)/shard_map/ppermute | solution.py:357
  36.5 36.2 %copy-start.1 = (bf16[5664,128]{1,0:T(8,128)(2,1)S(1)}, bf16[5664,128]{1,0:T(8,128)(2,1)}, u32[]{:S(2)}) copy-start(bf16[5664,128]{1,0:T(8,128)(2,1)} %get-tuple-element.19.own_ref.own) | copy-start | bytes 4349956
  36.5 36.1 %copy-start.2 = (s32[2,11]{1,0:T(2,128)S(1)}, s32[2,11]{1,0:T(2,128)}, u32[]{:S(2)}) copy-start(s32[2,11]{1,0:T(2,128)} %s_ref.1) | copy-start | bytes 268
  36.5 32.4 %collective-permute-start.7 = (bf16[384,128]{1,0:T(8,128)(2,1)S(1)}, bf16[384,128]{1,0:T(8,128)(2,1)S(1)}, u32[]{:S(2)}, u32[]{:S(2)}) collective-permute-start(bf16[384,128]{1,0:T(8,128)(2,1)S(1)} %copy-done.3), channel_id=1, source_target_pairs={{1,7},{3,9},{5,11},{6,0},{7,13},{8,2},{9,15},{10,4},{11,17},{12,6}... | collective-permute-start | bytes 294920 | tf_op jit(solution)/shard_map/ppermute | solution.py:357
  68.9 3.7 %collective-permute-start.8 = (bf16[4352,128]{1,0:T(8,128)(2,1)S(1)}, bf16[4352,128]{1,0:T(8,128)(2,1)S(1)}, u32[]{:S(2)}, u32[]{:S(2)}) collective-permute-start(bf16[4352,128]{1,0:T(8,128)(2,1)S(1)} %collective-permute-done.5.w2_r), channel_id=1, source_target_pairs={{0,1},{1,0},{2,3},{3,2},{4,5},{5,4},{6,7},{7,6},{8,9},{9,8},{10,11... | collective-permute-start | bytes 3342344 | tf_op jit(solution)/shard_map/ppermute | solution.py:360
  69.0 3.7 %collective-permute-start.9 = (bf16[2688,128]{1,0:T(8,128)(2,1)S(1)}, bf16[2688,128]{1,0:T(8,128)(2,1)S(1)}, u32[]{:S(2)}, u32[]{:S(2)}) collective-permute-start(bf16[2688,128]{1,0:T(8,128)(2,1)S(1)} %pad_maximum_fusion.1), channel_id=1, source_target_pairs={{0,1},{1,0},{2,3},{3,2},{4,5},{5,4},{6,7},{7,6},{8,9},{9,8},{10,11... | collective-permute-start | bytes 2064392 | tf_op jit(solution)/shard_map/ppermute | solution.py:360

commit v4 on v3

--- a/solution.py
+++ b/solution.py
@@ -388,10 +388,10 @@
         compiler_params=params,
         name="pack_chip",
     )(core, own, mate)
-    f2_r, w2 = lax.optimization_barrier((f2_r, w2))
+    w6_r = send(w6, 6)
+    f2_r, w6_r, w2 = lax.optimization_barrier((f2_r, w6_r, w2))
     w2_r = send(w2, 2)
     w4_r = send(w4, 4)
-    w6_r = send(w6, 6)
     p_parts = to_mate(n2_r, f2_r, n4_r)
 
     purified, third, pk, t_all = pl.pallas_call(

time: 84.6 us -> 79.8 us (0.943)
  waiting for transfers between devices: 28.7 us -> 22.1 us
  starting transfers between devices: 26.1 us -> 27.2 us
    ppermute x6, waiting for transfers between devices: 25.6 us -> 18.8 us  [send(): return lax.ppermute(message, AXES, route(hop, near, devices))]
    ppermute x4, starting transfers between devices: 4.33 us -> 7.6 us  [to_mate(): return lax.ppermute(jnp.concatenate(messages, axis=0), AXES, swap)]
    ppermute x6, starting transfers between devices: 21.8 us -> 19.6 us  [send(): return lax.ppermute(message, AXES, route(hop, near, devices))]
  transfers between devices with their start and end apart: 10 -> 10, of which waited for: 4 -> 5; matrix products, arithmetic and copies ran while one was open for 0% -> 0% of each run, Pallas kernels for 15% -> 16%
where the time goes in v4:
time: 79.8 us; the launch traced here: 78.8 us
  Pallas kernels  27.3 us (34%)
  starting transfers between devices  27.2 us (34%)
  waiting for transfers between devices  22.1 us (28%)
  local copies, waits for them, and re-layouts  1.37 us (2%)
    ppermute x6, starting transfers between devices, send(): return lax.ppermute(message, AXES, route(hop, near, devices))  19.6 us
    ppermute x6, waiting for transfers between devices, send(): return lax.ppermute(message, AXES, route(hop, near, devices))  18.8 us
    pallas_call x1, Pallas kernels, on_device(): pl.pallas_call(square_kernel, in_specs=[SMEM] + [VMEM] * 6, out_specs=[VM...  12.6 us
    pallas_call x1, Pallas kernels, on_device(): pl.pallas_call(gradient_kernel, in_specs=[SMEM, SMEM] + [VMEM] * 10, out_...  11.7 us
    ppermute x4, starting transfers between devices, to_mate(): return lax.ppermute(jnp.concatenate(messages, axis=0), AXES, swap)  7.6 us
    ppermute x4, waiting for transfers between devices, to_mate(): return lax.ppermute(jnp.concatenate(messages, axis=0), AXES, swap)  3.32 us
    pallas_call x1, Pallas kernels, on_device(): pl.pallas_call(pack_own, in_specs=[SMEM, HBM, HBM, HBM, HBM], out_specs=[...  2.92 us
  transfers between devices with their start and end apart: 10, of which 5 were waited for; matrix products, arithmetic and copies ran while one was open for 0% of the time, Pallas kernels for 16%

profile of v4, /device:TPU:25, one launch (start us, length us, event | category | flops | bytes accessed | tf_op | source)
XLA Modules:
  0.0 78.8 jit_solution(11891424825062098378)
XLA Ops:
  0.6 2.9 %pack_own.1 = (bf16[1696,128]{1,0:T(8,128)(2,1)}, bf16[1568,128]{1,0:T(8,128)(2,1)}, bf16[800,128]{1,0:T(8,128)(2,1)}, bf16[5664,128]{1,0:T(8,128)(2,1)}, bf16[384,128]{1,0:T(8,128)(2,1)}) custom-call(s32[1]{0:T(128)} %bitcast.core_ref, s32[2,11]{1,0:T(2,128)} %s_ref.1, s32[2,11]{1,0:T(2,128)} %t_any.1, bf16[2,11,128,128]{3,2,1,0:T(8,128)(2,1)} %density_any.1, ...), custom_call_target="tpu_custom_call" | custom-call | tf_op jit(solution)/shard_map/pack_own/pallas_call | solution.py:363
  3.6 0.8 collective-permute-start
  4.3 3.1 %collective-permute-start.1 = (bf16[1696,128]{1,0:T(8,128)(2,1)}, bf16[1696,128]{1,0:T(8,128)(2,1)S(1)}, u32[]{:S(2)}, u32[]{:S(2)}) collective-permute-start(bf16[1696,128]{1,0:T(8,128)(2,1)} %get-tuple-element.21), channel_id=1, source_target_pairs={{1,3},{2,0},{3,5},{4,2},{5,7},{6,4},{7,9},{8,6},{9,11},{10,8},{11,... | collective-permute-start | bytes 1302536 | tf_op jit(solution)/shard_map/ppermute | solution.py:357
  7.4 8.7 %collective-permute-start.2 = (bf16[1568,128]{1,0:T(8,128)(2,1)}, bf16[1568,128]{1,0:T(8,128)(2,1)S(1)}, u32[]{:S(2)}, u32[]{:S(2)}) collective-permute-start(bf16[1568,128]{1,0:T(8,128)(2,1)} %get-tuple-element.22), channel_id=1, source_target_pairs={{0,2},{2,4},{3,1},{4,6},{5,3},{6,8},{7,5},{8,10},{9,7},{10,12},{11... | collective-permute-start | bytes 1204232 | tf_op jit(solution)/shard_map/ppermute | solution.py:357
  16.1 1.9 %collective-permute-start.4 = (bf16[800,128]{1,0:T(8,128)(2,1)}, bf16[800,128]{1,0:T(8,128)(2,1)S(1)}, u32[]{:S(2)}, u32[]{:S(2)}) collective-permute-start(bf16[800,128]{1,0:T(8,128)(2,1)} %get-tuple-element.26), channel_id=1, source_target_pairs={{1,5},{3,7},{4,0},{5,9},{6,2},{7,11},{8,4},{9,13},{10,6},{11,15},{... | collective-permute-start | bytes 614408 | tf_op jit(solution)/shard_map/ppermute | solution.py:357
  18.0 1.9 %collective-permute-start.3 = (bf16[384,128]{1,0:T(8,128)(2,1)}, bf16[384,128]{1,0:T(8,128)(2,1)S(1)}, u32[]{:S(2)}, u32[]{:S(2)}) collective-permute-start(bf16[384,128]{1,0:T(8,128)(2,1)} %get-tuple-element.23), channel_id=1, source_target_pairs={{1,7},{3,9},{5,11},{6,0},{7,13},{8,2},{9,15},{10,4},{11,17},{12,6}... | collective-permute-start | bytes 294920 | tf_op jit(solution)/shard_map/ppermute | solution.py:357
  20.0 0.0 collective-permute-done.mate_ref.mate
  20.0 0.0 copy-start
  20.0 1.4 %copy-done = bf16[5664,128]{1,0:T(8,128)(2,1)S(1)} copy-done((bf16[5664,128]{1,0:T(8,128)(2,1)S(1)}, bf16[5664,128]{1,0:T(8,128)(2,1)}, u32[]{:S(2)}) %copy-start) | copy-done | bytes 1450008
  21.3 0.1 pack_chip.1
  21.5 9.3 %collective-permute-done.3.w6_r = bf16[384,128]{1,0:T(8,128)(2,1)S(1)} collective-permute-done((bf16[384,128]{1,0:T(8,128)(2,1)}, bf16[384,128]{1,0:T(8,128)(2,1)S(1)}, u32[]{:S(2)}, u32[]{:S(2)}) %collective-permute-start.3) | collective-permute-done | bytes 98336 | tf_op jit(solution)/shard_map/ppermute | solution.py:357
  30.8 0.0 collective-permute-done.2.f2_r
  30.8 1.9 %collective-permute-start.6 = (bf16[4352,128]{1,0:T(8,128)(2,1)S(1)}, bf16[4352,128]{1,0:T(8,128)(2,1)S(1)}, u32[]{:S(2)}, u32[]{:S(2)}) collective-permute-start(bf16[4352,128]{1,0:T(8,128)(2,1)S(1)} %get-tuple-element.28), channel_id=1, source_target_pairs={{1,3},{2,0},{3,5},{4,2},{5,7},{6,4},{7,9},{8,6},{9,11},{10,8},{11,... | collective-permute-start | bytes 3342344 | tf_op jit(solution)/shard_map/ppermute | solution.py:357
  32.7 0.0 collective-permute-done.4.n4_r
  32.7 0.0 collective-permute-done.1.n2_r
  32.7 0.1 pad_maximum_fusion
  32.8 6.2 %collective-permute-start.5 = (bf16[4064,128]{1,0:T(8,128)(2,1)S(1)}, bf16[4064,128]{1,0:T(8,128)(2,1)S(1)}, u32[]{:S(2)}, u32[]{:S(2)}) collective-permute-start(bf16[4064,128]{1,0:T(8,128)(2,1)S(1)} %pad_maximum_fusion), channel_id=1, source_target_pairs={{0,1},{1,0},{2,3},{3,2},{4,5},{5,4},{6,7},{7,6},{8,9},{9,8},{10,11... | collective-permute-start | bytes 3121160 | tf_op jit(solution)/shard_map/ppermute | solution.py:360
  39.1 0.0 copy-start.1
  39.1 0.0 copy-start.2
  39.1 2.0 %collective-permute-start.7 = (bf16[2304,128]{1,0:T(8,128)(2,1)S(1)}, bf16[2304,128]{1,0:T(8,128)(2,1)S(1)}, u32[]{:S(2)}, u32[]{:S(2)}) collective-permute-start(bf16[2304,128]{1,0:T(8,128)(2,1)S(1)} %get-tuple-element.29), channel_id=1, source_target_pairs={{1,5},{3,7},{4,0},{5,9},{6,2},{7,11},{8,4},{9,13},{10,6},{11,15},{... | collective-permute-start | bytes 1769480 | tf_op jit(solution)/shard_map/ppermute | solution.py:357
  41.1 0.2 collective-permute-done.5.parts_x
  41.3 12.6 %square.1 = (f32[2,11,128,128]{3,2,1,0:T(8,128)}, f32[256,1536]{1,0:T(8,128)S(1)}, bf16[7,256,1536]{2,1,0:T(8,128)(2,1)S(1)}, f32[224,128]{1,0:T(8,128)S(1)}) custom-call(s32[1]{0:T(128)} %bitcast.core_ref, bf16[5664,128]{1,0:T(8,128)(2,1)S(1)} %copy-done, bf16[5664,128]{1,0:T(8,128)(2,1)S(1)} %collective-permute-done.mate_ref.mate, ...), custom_call_target="tpu_custom_call" | custom-call | flops 1000000 | bytes 10000 | tf_op jit(solution)/shard_map/square/pallas_call | solution.py:397
  53.9 4.3 %collective-permute-done.7.w4_r = bf16[2304,128]{1,0:T(8,128)(2,1)S(1)} collective-permute-done((bf16[2304,128]{1,0:T(8,128)(2,1)S(1)}, bf16[2304,128]{1,0:T(8,128)(2,1)S(1)}, u32[]{:S(2)}, u32[]{:S(2)}) %collective-permute-start.7) | collective-permute-done | bytes 589856 | tf_op jit(solution)/shard_map/ppermute | solution.py:357
  58.3 5.1 %collective-permute-done.6.w2_r = bf16[4352,128]{1,0:T(8,128)(2,1)S(1)} collective-permute-done((bf16[4352,128]{1,0:T(8,128)(2,1)S(1)}, bf16[4352,128]{1,0:T(8,128)(2,1)S(1)}, u32[]{:S(2)}, u32[]{:S(2)}) %collective-permute-start.6) | collective-permute-done | bytes 1114144 | tf_op jit(solution)/shard_map/ppermute | solution.py:357
  63.4 0.2 collective-permute-start.8
  63.7 0.4 collective-permute-start.9
  64.0 3.1 %collective-permute-done.9.parts_x = bf16[2688,128]{1,0:T(8,128)(2,1)S(1)} collective-permute-done((bf16[2688,128]{1,0:T(8,128)(2,1)S(1)}, bf16[2688,128]{1,0:T(8,128)(2,1)S(1)}, u32[]{:S(2)}, u32[]{:S(2)}) %collective-permute-start.9) | collective-permute-done | bytes 688160 | tf_op jit(solution)/shard_map/ppermute | solution.py:360
  67.1 0.0 collective-permute-done.8.w2_x
  67.1 0.0 copy-done.1
  67.1 0.0 copy-done.2
  67.2 11.7 %gradient.1 = f32[2,11,128,128]{3,2,1,0:T(8,128)} custom-call(s32[1]{0:T(128)} %bitcast.core_ref, s32[2,11]{1,0:T(2,128)S(1)} %copy-done.2, bf16[5664,128]{1,0:T(8,128)(2,1)S(1)} %copy-done.1, bf16[5664,128]{1,0:T(8,128)(2,1)S(1)} %collective-permute-done.mate_ref.mate, bf16[4352,128]{1,0:T(8,128)(2,1)S(1)} %collective-permute-done.6.w2_r, ...), custom_call_target="tpu_custom_call" | custom-call | flops 7000000000 | bytes 16000000 | tf_op jit(solution)/shard_map/gradient/pallas_call | solution.py:417
  (1 shorter events, 0.0 us)
Async XLA Ops:
  3.6 16.4 %collective-permute-start = (bf16[5664,128]{1,0:T(8,128)(2,1)}, bf16[5664,128]{1,0:T(8,128)(2,1)S(1)}, u32[]{:S(2)}, u32[]{:S(2)}) collective-permute-start(bf16[5664,128]{1,0:T(8,128)(2,1)} %get-tuple-element.20.own_ref.own), channel_id=1, source_target_pairs={{0,1},{1,0},{2,3},{3,2},{4,5},{5,4},{6,7},{7,6},{8,9},{9,8},{10,11... | collective-permute-start | bytes 4349960 | tf_op jit(solution)/shard_map/ppermute | solution.py:360
  4.3 28.4 %collective-permute-start.1 = (bf16[1696,128]{1,0:T(8,128)(2,1)}, bf16[1696,128]{1,0:T(8,128)(2,1)S(1)}, u32[]{:S(2)}, u32[]{:S(2)}) collective-permute-start(bf16[1696,128]{1,0:T(8,128)(2,1)} %get-tuple-element.21), channel_id=1, source_target_pairs={{1,3},{2,0},{3,5},{4,2},{5,7},{6,4},{7,9},{8,6},{9,11},{10,8},{11,... | collective-permute-start | bytes 1302536 | tf_op jit(solution)/shard_map/ppermute | solution.py:357
  7.4 23.4 %collective-permute-start.2 = (bf16[1568,128]{1,0:T(8,128)(2,1)}, bf16[1568,128]{1,0:T(8,128)(2,1)S(1)}, u32[]{:S(2)}, u32[]{:S(2)}) collective-permute-start(bf16[1568,128]{1,0:T(8,128)(2,1)} %get-tuple-element.22), channel_id=1, source_target_pairs={{0,2},{2,4},{3,1},{4,6},{5,3},{6,8},{7,5},{8,10},{9,7},{10,12},{11... | collective-permute-start | bytes 1204232 | tf_op jit(solution)/shard_map/ppermute | solution.py:357
  16.1 16.6 %collective-permute-start.4 = (bf16[800,128]{1,0:T(8,128)(2,1)}, bf16[800,128]{1,0:T(8,128)(2,1)S(1)}, u32[]{:S(2)}, u32[]{:S(2)}) collective-permute-start(bf16[800,128]{1,0:T(8,128)(2,1)} %get-tuple-element.26), channel_id=1, source_target_pairs={{1,5},{3,7},{4,0},{5,9},{6,2},{7,11},{8,4},{9,13},{10,6},{11,15},{... | collective-permute-start | bytes 614408 | tf_op jit(solution)/shard_map/ppermute | solution.py:357
  18.0 12.8 %collective-permute-start.3 = (bf16[384,128]{1,0:T(8,128)(2,1)}, bf16[384,128]{1,0:T(8,128)(2,1)S(1)}, u32[]{:S(2)}, u32[]{:S(2)}) collective-permute-start(bf16[384,128]{1,0:T(8,128)(2,1)} %get-tuple-element.23), channel_id=1, source_target_pairs={{1,7},{3,9},{5,11},{6,0},{7,13},{8,2},{9,15},{10,4},{11,17},{12,6}... | collective-permute-start | bytes 294920 | tf_op jit(solution)/shard_map/ppermute | solution.py:357
  20.0 1.4 %copy-start = (bf16[5664,128]{1,0:T(8,128)(2,1)S(1)}, bf16[5664,128]{1,0:T(8,128)(2,1)}, u32[]{:S(2)}) copy-start(bf16[5664,128]{1,0:T(8,128)(2,1)} %get-tuple-element.20.own_ref.own) | copy-start | bytes 4349956
  30.8 32.6 %collective-permute-start.6 = (bf16[4352,128]{1,0:T(8,128)(2,1)S(1)}, bf16[4352,128]{1,0:T(8,128)(2,1)S(1)}, u32[]{:S(2)}, u32[]{:S(2)}) collective-permute-start(bf16[4352,128]{1,0:T(8,128)(2,1)S(1)} %get-tuple-element.28), channel_id=1, source_target_pairs={{1,3},{2,0},{3,5},{4,2},{5,7},{6,4},{7,9},{8,6},{9,11},{10,8},{11,... | collective-permute-start | bytes 3342344 | tf_op jit(solution)/shard_map/ppermute | solution.py:357
  32.8 8.5 %collective-permute-start.5 = (bf16[4064,128]{1,0:T(8,128)(2,1)S(1)}, bf16[4064,128]{1,0:T(8,128)(2,1)S(1)}, u32[]{:S(2)}, u32[]{:S(2)}) collective-permute-start(bf16[4064,128]{1,0:T(8,128)(2,1)S(1)} %pad_maximum_fusion), channel_id=1, source_target_pairs={{0,1},{1,0},{2,3},{3,2},{4,5},{5,4},{6,7},{7,6},{8,9},{9,8},{10,11... | collective-permute-start | bytes 3121160 | tf_op jit(solution)/shard_map/ppermute | solution.py:360
  39.1 28.1 %copy-start.1 = (bf16[5664,128]{1,0:T(8,128)(2,1)S(1)}, bf16[5664,128]{1,0:T(8,128)(2,1)}, u32[]{:S(2)}) copy-start(bf16[5664,128]{1,0:T(8,128)(2,1)} %get-tuple-element.20.own_ref.own) | copy-start | bytes 4349956
  39.1 28.1 %copy-start.2 = (s32[2,11]{1,0:T(2,128)S(1)}, s32[2,11]{1,0:T(2,128)}, u32[]{:S(2)}) copy-start(s32[2,11]{1,0:T(2,128)} %s_ref.1) | copy-start | bytes 268
  39.1 19.2 %collective-permute-start.7 = (bf16[2304,128]{1,0:T(8,128)(2,1)S(1)}, bf16[2304,128]{1,0:T(8,128)(2,1)S(1)}, u32[]{:S(2)}, u32[]{:S(2)}) collective-permute-start(bf16[2304,128]{1,0:T(8,128)(2,1)S(1)} %get-tuple-element.29), channel_id=1, source_target_pairs={{1,5},{3,7},{4,0},{5,9},{6,2},{7,11},{8,4},{9,13},{10,6},{11,15},{... | collective-permute-start | bytes 1769480 | tf_op jit(solution)/shard_map/ppermute | solution.py:357
  63.4 3.7 %collective-permute-start.8 = (bf16[4352,128]{1,0:T(8,128)(2,1)S(1)}, bf16[4352,128]{1,0:T(8,128)(2,1)S(1)}, u32[]{:S(2)}, u32[]{:S(2)}) collective-permute-start(bf16[4352,128]{1,0:T(8,128)(2,1)S(1)} %collective-permute-done.6.w2_r), channel_id=1, source_target_pairs={{0,1},{1,0},{2,3},{3,2},{4,5},{5,4},{6,7},{7,6},{8,9},{9,8},{10,11... | collective-permute-start | bytes 3342344 | tf_op jit(solution)/shard_map/ppermute | solution.py:360
  63.7 3.5 %collective-permute-start.9 = (bf16[2688,128]{1,0:T(8,128)(2,1)S(1)}, bf16[2688,128]{1,0:T(8,128)(2,1)S(1)}, u32[]{:S(2)}, u32[]{:S(2)}) collective-permute-start(bf16[2688,128]{1,0:T(8,128)(2,1)S(1)} %pad_maximum_fusion.1), channel_id=1, source_target_pairs={{0,1},{1,0},{2,3},{3,2},{4,5},{5,4},{6,7},{7,6},{8,9},{9,8},{10,11... | collective-permute-start | bytes 2064392 | tf_op jit(solution)/shard_map/ppermute | solution.py:360

commit v5 on v4

--- a/solution.py
+++ b/solution.py
@@ -263,8 +263,8 @@
 
 def gradient_kernel(
     core_ref, s_ref, own, mate, w2_r, w2_x, w4_r, w6_r, parts_x, pk_ref, third_s, t_ref,
-    grad_ref,
-    gk, gb, lhs,
+    grad_any,
+    gk, gb, lhs, grad_ref, sems,
 ):
     p = core_ref[0]
     zero = jnp.zeros((B, B), BF16)
@@ -335,8 +335,21 @@
                     keep = s_ref[r, slot].astype(F32)
                     grad_ref[r, slot] = total[r * B : r * B + B, e * B : e * B + B] * keep
 
+    def leave(j):
+        ends = ((0, 2 * j, min(2 * j + 2, SLOTS)), (1, max(0, 2 * j - 1), 2 * j + 1))
+        places = [(r, pl.ds(low, high - low)) for r, low, high in ends]
+        return [
+            pltpu.make_async_copy(grad_ref.at[at], grad_any.at[at], sems.at[2 * j + at[0]])
+            for at in places
+        ]
+
     for j in range(6):
         in_block(core_ref, functools.partial(finish, j))
+        for copy in leave(j):
+            copy.start()
+    for j in range(6):
+        for copy in leave(j):
+            copy.wait()
 
 
 SMEM = pl.BlockSpec(memory_space=pltpu.SMEM)
@@ -417,11 +430,12 @@
     gradient = pl.pallas_call(
         gradient_kernel,
         in_specs=[SMEM, SMEM] + [VMEM] * 10,
-        out_specs=VMEM,
+        out_specs=HBM,
         out_shape=jax.ShapeDtypeStruct((2, SLOTS, B, B), F32),
         scratch_shapes=[
             pltpu.VMEM((7, 14 * B, 256), BF16), pltpu.VMEM((1536, 1536), BF16),
-            pltpu.VMEM((256, 1536), BF16),
+            pltpu.VMEM((256, 1536), BF16), pltpu.VMEM((2, SLOTS, B, B), F32),
+            pltpu.SemaphoreType.DMA((12,)),
         ],
         cost_estimate=pl.CostEstimate(flops=7 * 10**9, bytes_accessed=16 * 10**6, transcendentals=0),
         compiler_params=params,

time: 79.8 us -> 79.7 us (level)
  no operation moved by 1% of the time
where the time goes in v5:
time: 79.7 us; the launch traced here: 78.7 us
  starting transfers between devices  27.2 us (34%)
  Pallas kernels  27 us (34%)
  waiting for transfers between devices  22.1 us (28%)
  local copies, waits for them, and re-layouts  1.37 us (2%)
  between operations  0.92 us (1%)
    ppermute x6, starting transfers between devices, send(): return lax.ppermute(message, AXES, route(hop, near, devices))  19.6 us
    ppermute x6, waiting for transfers between devices, send(): return lax.ppermute(message, AXES, route(hop, near, devices))  18.8 us
    pallas_call x1, Pallas kernels, on_device(): pl.pallas_call(square_kernel, in_specs=[SMEM] + [VMEM] * 6, out_specs=[VM...  12.6 us
    pallas_call x1, Pallas kernels, on_device(): pl.pallas_call(gradient_kernel, in_specs=[SMEM, SMEM] + [VMEM] * 10, out_...  11.3 us
    ppermute x4, starting transfers between devices, to_mate(): return lax.ppermute(jnp.concatenate(messages, axis=0), AXES, swap)  7.6 us
    ppermute x4, waiting for transfers between devices, to_mate(): return lax.ppermute(jnp.concatenate(messages, axis=0), AXES, swap)  3.32 us
    pallas_call x1, Pallas kernels, on_device(): pl.pallas_call(pack_own, in_specs=[SMEM, HBM, HBM, HBM, HBM], out_specs=[...  2.92 us
  transfers between devices with their start and end apart: 10, of which 5 were waited for; matrix products, arithmetic and copies ran while one was open for 0% of the time, Pallas kernels for 16%

profile of v5, /device:TPU:25, one launch (start us, length us, event | category | flops | bytes accessed | tf_op | source)
XLA Modules:
  0.0 78.7 jit_solution(6134803304140783152)
XLA Ops:
  0.6 2.9 %pack_own.1 = (bf16[1696,128]{1,0:T(8,128)(2,1)}, bf16[1568,128]{1,0:T(8,128)(2,1)}, bf16[800,128]{1,0:T(8,128)(2,1)}, bf16[5664,128]{1,0:T(8,128)(2,1)}, bf16[384,128]{1,0:T(8,128)(2,1)}) custom-call(s32[1]{0:T(128)} %bitcast.core_ref, s32[2,11]{1,0:T(2,128)} %s_ref.1, s32[2,11]{1,0:T(2,128)} %t_any.1, bf16[2,11,128,128]{3,2,1,0:T(8,128)(2,1)} %density_any.1, ...), custom_call_target="tpu_custom_call" | custom-call | tf_op jit(solution)/shard_map/pack_own/pallas_call | solution.py:376
  3.6 0.8 collective-permute-start
  4.3 3.1 %collective-permute-start.1 = (bf16[1696,128]{1,0:T(8,128)(2,1)}, bf16[1696,128]{1,0:T(8,128)(2,1)S(1)}, u32[]{:S(2)}, u32[]{:S(2)}) collective-permute-start(bf16[1696,128]{1,0:T(8,128)(2,1)} %get-tuple-element.21), channel_id=1, source_target_pairs={{1,3},{2,0},{3,5},{4,2},{5,7},{6,4},{7,9},{8,6},{9,11},{10,8},{11,... | collective-permute-start | bytes 1302536 | tf_op jit(solution)/shard_map/ppermute | solution.py:370
  7.4 8.7 %collective-permute-start.2 = (bf16[1568,128]{1,0:T(8,128)(2,1)}, bf16[1568,128]{1,0:T(8,128)(2,1)S(1)}, u32[]{:S(2)}, u32[]{:S(2)}) collective-permute-start(bf16[1568,128]{1,0:T(8,128)(2,1)} %get-tuple-element.22), channel_id=1, source_target_pairs={{0,2},{2,4},{3,1},{4,6},{5,3},{6,8},{7,5},{8,10},{9,7},{10,12},{11... | collective-permute-start | bytes 1204232 | tf_op jit(solution)/shard_map/ppermute | solution.py:370
  16.1 1.9 %collective-permute-start.4 = (bf16[800,128]{1,0:T(8,128)(2,1)}, bf16[800,128]{1,0:T(8,128)(2,1)S(1)}, u32[]{:S(2)}, u32[]{:S(2)}) collective-permute-start(bf16[800,128]{1,0:T(8,128)(2,1)} %get-tuple-element.26), channel_id=1, source_target_pairs={{1,5},{3,7},{4,0},{5,9},{6,2},{7,11},{8,4},{9,13},{10,6},{11,15},{... | collective-permute-start | bytes 614408 | tf_op jit(solution)/shard_map/ppermute | solution.py:370
  18.0 1.9 %collective-permute-start.3 = (bf16[384,128]{1,0:T(8,128)(2,1)}, bf16[384,128]{1,0:T(8,128)(2,1)S(1)}, u32[]{:S(2)}, u32[]{:S(2)}) collective-permute-start(bf16[384,128]{1,0:T(8,128)(2,1)} %get-tuple-element.23), channel_id=1, source_target_pairs={{1,7},{3,9},{5,11},{6,0},{7,13},{8,2},{9,15},{10,4},{11,17},{12,6}... | collective-permute-start | bytes 294920 | tf_op jit(solution)/shard_map/ppermute | solution.py:370
  20.0 0.0 collective-permute-done.mate_ref.mate
  20.0 0.0 copy-start
  20.0 1.4 %copy-done = bf16[5664,128]{1,0:T(8,128)(2,1)S(1)} copy-done((bf16[5664,128]{1,0:T(8,128)(2,1)S(1)}, bf16[5664,128]{1,0:T(8,128)(2,1)}, u32[]{:S(2)}) %copy-start) | copy-done | bytes 1450008
  21.3 0.1 pack_chip.1
  21.5 9.3 %collective-permute-done.3.w6_r = bf16[384,128]{1,0:T(8,128)(2,1)S(1)} collective-permute-done((bf16[384,128]{1,0:T(8,128)(2,1)}, bf16[384,128]{1,0:T(8,128)(2,1)S(1)}, u32[]{:S(2)}, u32[]{:S(2)}) %collective-permute-start.3) | collective-permute-done | bytes 98336 | tf_op jit(solution)/shard_map/ppermute | solution.py:370
  30.8 0.0 collective-permute-done.2.f2_r
  30.8 1.9 %collective-permute-start.6 = (bf16[4352,128]{1,0:T(8,128)(2,1)S(1)}, bf16[4352,128]{1,0:T(8,128)(2,1)S(1)}, u32[]{:S(2)}, u32[]{:S(2)}) collective-permute-start(bf16[4352,128]{1,0:T(8,128)(2,1)S(1)} %get-tuple-element.28), channel_id=1, source_target_pairs={{1,3},{2,0},{3,5},{4,2},{5,7},{6,4},{7,9},{8,6},{9,11},{10,8},{11,... | collective-permute-start | bytes 3342344 | tf_op jit(solution)/shard_map/ppermute | solution.py:370
  32.7 0.0 collective-permute-done.4.n4_r
  32.7 0.0 collective-permute-done.1.n2_r
  32.7 0.1 pad_maximum_fusion
  32.8 6.2 %collective-permute-start.5 = (bf16[4064,128]{1,0:T(8,128)(2,1)S(1)}, bf16[4064,128]{1,0:T(8,128)(2,1)S(1)}, u32[]{:S(2)}, u32[]{:S(2)}) collective-permute-start(bf16[4064,128]{1,0:T(8,128)(2,1)S(1)} %pad_maximum_fusion), channel_id=1, source_target_pairs={{0,1},{1,0},{2,3},{3,2},{4,5},{5,4},{6,7},{7,6},{8,9},{9,8},{10,11... | collective-permute-start | bytes 3121160 | tf_op jit(solution)/shard_map/ppermute | solution.py:373
  39.1 0.0 copy-start.1
  39.1 0.0 copy-start.2
  39.1 2.0 %collective-permute-start.7 = (bf16[2304,128]{1,0:T(8,128)(2,1)S(1)}, bf16[2304,128]{1,0:T(8,128)(2,1)S(1)}, u32[]{:S(2)}, u32[]{:S(2)}) collective-permute-start(bf16[2304,128]{1,0:T(8,128)(2,1)S(1)} %get-tuple-element.29), channel_id=1, source_target_pairs={{1,5},{3,7},{4,0},{5,9},{6,2},{7,11},{8,4},{9,13},{10,6},{11,15},{... | collective-permute-start | bytes 1769480 | tf_op jit(solution)/shard_map/ppermute | solution.py:370
  41.1 0.2 collective-permute-done.5.parts_x
  41.3 12.6 %square.1 = (f32[2,11,128,128]{3,2,1,0:T(8,128)}, f32[256,1536]{1,0:T(8,128)S(1)}, bf16[7,256,1536]{2,1,0:T(8,128)(2,1)S(1)}, f32[224,128]{1,0:T(8,128)S(1)}) custom-call(s32[1]{0:T(128)} %bitcast.core_ref, bf16[5664,128]{1,0:T(8,128)(2,1)S(1)} %copy-done, bf16[5664,128]{1,0:T(8,128)(2,1)S(1)} %collective-permute-done.mate_ref.mate, ...), custom_call_target="tpu_custom_call" | custom-call | flops 1000000 | bytes 10000 | tf_op jit(solution)/shard_map/square/pallas_call | solution.py:410
  53.9 4.3 %collective-permute-done.7.w4_r = bf16[2304,128]{1,0:T(8,128)(2,1)S(1)} collective-permute-done((bf16[2304,128]{1,0:T(8,128)(2,1)S(1)}, bf16[2304,128]{1,0:T(8,128)(2,1)S(1)}, u32[]{:S(2)}, u32[]{:S(2)}) %collective-permute-start.7) | collective-permute-done | bytes 589856 | tf_op jit(solution)/shard_map/ppermute | solution.py:370
  58.3 5.1 %collective-permute-done.6.w2_r = bf16[4352,128]{1,0:T(8,128)(2,1)S(1)} collective-permute-done((bf16[4352,128]{1,0:T(8,128)(2,1)S(1)}, bf16[4352,128]{1,0:T(8,128)(2,1)S(1)}, u32[]{:S(2)}, u32[]{:S(2)}) %collective-permute-start.6) | collective-permute-done | bytes 1114144 | tf_op jit(solution)/shard_map/ppermute | solution.py:370
  63.4 0.2 collective-permute-start.8
  63.7 0.4 collective-permute-start.9
  64.0 3.1 %collective-permute-done.9.parts_x = bf16[2688,128]{1,0:T(8,128)(2,1)S(1)} collective-permute-done((bf16[2688,128]{1,0:T(8,128)(2,1)S(1)}, bf16[2688,128]{1,0:T(8,128)(2,1)S(1)}, u32[]{:S(2)}, u32[]{:S(2)}) %collective-permute-start.9) | collective-permute-done | bytes 688160 | tf_op jit(solution)/shard_map/ppermute | solution.py:373
  67.1 0.0 collective-permute-done.8.w2_x
  67.1 0.0 copy-done.1
  67.1 0.0 copy-done.2
  67.2 11.3 %gradient.1 = f32[2,11,128,128]{3,2,1,0:T(8,128)} custom-call(s32[1]{0:T(128)} %bitcast.core_ref, s32[2,11]{1,0:T(2,128)S(1)} %copy-done.2, bf16[5664,128]{1,0:T(8,128)(2,1)S(1)} %copy-done.1, bf16[5664,128]{1,0:T(8,128)(2,1)S(1)} %collective-permute-done.mate_ref.mate, bf16[4352,128]{1,0:T(8,128)(2,1)S(1)} %collective-permute-done.6.w2_r, ...), custom_call_target="tpu_custom_call" | custom-call | flops 7000000000 | bytes 16000000 | tf_op jit(solution)/shard_map/gradient/pallas_call | solution.py:430
  (1 shorter events, 0.0 us)
Async XLA Ops:
  3.6 16.4 %collective-permute-start = (bf16[5664,128]{1,0:T(8,128)(2,1)}, bf16[5664,128]{1,0:T(8,128)(2,1)S(1)}, u32[]{:S(2)}, u32[]{:S(2)}) collective-permute-start(bf16[5664,128]{1,0:T(8,128)(2,1)} %get-tuple-element.20.own_ref.own), channel_id=1, source_target_pairs={{0,1},{1,0},{2,3},{3,2},{4,5},{5,4},{6,7},{7,6},{8,9},{9,8},{10,11... | collective-permute-start | bytes 4349960 | tf_op jit(solution)/shard_map/ppermute | solution.py:373
  4.3 28.4 %collective-permute-start.1 = (bf16[1696,128]{1,0:T(8,128)(2,1)}, bf16[1696,128]{1,0:T(8,128)(2,1)S(1)}, u32[]{:S(2)}, u32[]{:S(2)}) collective-permute-start(bf16[1696,128]{1,0:T(8,128)(2,1)} %get-tuple-element.21), channel_id=1, source_target_pairs={{1,3},{2,0},{3,5},{4,2},{5,7},{6,4},{7,9},{8,6},{9,11},{10,8},{11,... | collective-permute-start | bytes 1302536 | tf_op jit(solution)/shard_map/ppermute | solution.py:370
  7.4 23.4 %collective-permute-start.2 = (bf16[1568,128]{1,0:T(8,128)(2,1)}, bf16[1568,128]{1,0:T(8,128)(2,1)S(1)}, u32[]{:S(2)}, u32[]{:S(2)}) collective-permute-start(bf16[1568,128]{1,0:T(8,128)(2,1)} %get-tuple-element.22), channel_id=1, source_target_pairs={{0,2},{2,4},{3,1},{4,6},{5,3},{6,8},{7,5},{8,10},{9,7},{10,12},{11... | collective-permute-start | bytes 1204232 | tf_op jit(solution)/shard_map/ppermute | solution.py:370
  16.1 16.6 %collective-permute-start.4 = (bf16[800,128]{1,0:T(8,128)(2,1)}, bf16[800,128]{1,0:T(8,128)(2,1)S(1)}, u32[]{:S(2)}, u32[]{:S(2)}) collective-permute-start(bf16[800,128]{1,0:T(8,128)(2,1)} %get-tuple-element.26), channel_id=1, source_target_pairs={{1,5},{3,7},{4,0},{5,9},{6,2},{7,11},{8,4},{9,13},{10,6},{11,15},{... | collective-permute-start | bytes 614408 | tf_op jit(solution)/shard_map/ppermute | solution.py:370
  18.0 12.8 %collective-permute-start.3 = (bf16[384,128]{1,0:T(8,128)(2,1)}, bf16[384,128]{1,0:T(8,128)(2,1)S(1)}, u32[]{:S(2)}, u32[]{:S(2)}) collective-permute-start(bf16[384,128]{1,0:T(8,128)(2,1)} %get-tuple-element.23), channel_id=1, source_target_pairs={{1,7},{3,9},{5,11},{6,0},{7,13},{8,2},{9,15},{10,4},{11,17},{12,6}... | collective-permute-start | bytes 294920 | tf_op jit(solution)/shard_map/ppermute | solution.py:370
  20.0 1.4 %copy-start = (bf16[5664,128]{1,0:T(8,128)(2,1)S(1)}, bf16[5664,128]{1,0:T(8,128)(2,1)}, u32[]{:S(2)}) copy-start(bf16[5664,128]{1,0:T(8,128)(2,1)} %get-tuple-element.20.own_ref.own) | copy-start | bytes 4349956
  30.8 32.6 %collective-permute-start.6 = (bf16[4352,128]{1,0:T(8,128)(2,1)S(1)}, bf16[4352,128]{1,0:T(8,128)(2,1)S(1)}, u32[]{:S(2)}, u32[]{:S(2)}) collective-permute-start(bf16[4352,128]{1,0:T(8,128)(2,1)S(1)} %get-tuple-element.28), channel_id=1, source_target_pairs={{1,3},{2,0},{3,5},{4,2},{5,7},{6,4},{7,9},{8,6},{9,11},{10,8},{11,... | collective-permute-start | bytes 3342344 | tf_op jit(solution)/shard_map/ppermute | solution.py:370
  32.8 8.5 %collective-permute-start.5 = (bf16[4064,128]{1,0:T(8,128)(2,1)S(1)}, bf16[4064,128]{1,0:T(8,128)(2,1)S(1)}, u32[]{:S(2)}, u32[]{:S(2)}) collective-permute-start(bf16[4064,128]{1,0:T(8,128)(2,1)S(1)} %pad_maximum_fusion), channel_id=1, source_target_pairs={{0,1},{1,0},{2,3},{3,2},{4,5},{5,4},{6,7},{7,6},{8,9},{9,8},{10,11... | collective-permute-start | bytes 3121160 | tf_op jit(solution)/shard_map/ppermute | solution.py:373
  39.1 28.1 %copy-start.1 = (bf16[5664,128]{1,0:T(8,128)(2,1)S(1)}, bf16[5664,128]{1,0:T(8,128)(2,1)}, u32[]{:S(2)}) copy-start(bf16[5664,128]{1,0:T(8,128)(2,1)} %get-tuple-element.20.own_ref.own) | copy-start | bytes 4349956
  39.1 28.1 %copy-start.2 = (s32[2,11]{1,0:T(2,128)S(1)}, s32[2,11]{1,0:T(2,128)}, u32[]{:S(2)}) copy-start(s32[2,11]{1,0:T(2,128)} %s_ref.1) | copy-start | bytes 268
  39.1 19.2 %collective-permute-start.7 = (bf16[2304,128]{1,0:T(8,128)(2,1)S(1)}, bf16[2304,128]{1,0:T(8,128)(2,1)S(1)}, u32[]{:S(2)}, u32[]{:S(2)}) collective-permute-start(bf16[2304,128]{1,0:T(8,128)(2,1)S(1)} %get-tuple-element.29), channel_id=1, source_target_pairs={{1,5},{3,7},{4,0},{5,9},{6,2},{7,11},{8,4},{9,13},{10,6},{11,15},{... | collective-permute-start | bytes 1769480 | tf_op jit(solution)/shard_map/ppermute | solution.py:370
  63.4 3.7 %collective-permute-start.8 = (bf16[4352,128]{1,0:T(8,128)(2,1)S(1)}, bf16[4352,128]{1,0:T(8,128)(2,1)S(1)}, u32[]{:S(2)}, u32[]{:S(2)}) collective-permute-start(bf16[4352,128]{1,0:T(8,128)(2,1)S(1)} %collective-permute-done.6.w2_r), channel_id=1, source_target_pairs={{0,1},{1,0},{2,3},{3,2},{4,5},{5,4},{6,7},{7,6},{8,9},{9,8},{10,11... | collective-permute-start | bytes 3342344 | tf_op jit(solution)/shard_map/ppermute | solution.py:373
  63.7 3.5 %collective-permute-start.9 = (bf16[2688,128]{1,0:T(8,128)(2,1)S(1)}, bf16[2688,128]{1,0:T(8,128)(2,1)S(1)}, u32[]{:S(2)}, u32[]{:S(2)}) collective-permute-start(bf16[2688,128]{1,0:T(8,128)(2,1)S(1)} %pad_maximum_fusion.1), channel_id=1, source_target_pairs={{0,1},{1,0},{2,3},{3,2},{4,5},{5,4},{6,7},{7,6},{8,9},{9,8},{10,11... | collective-permute-start | bytes 2064392 | tf_op jit(solution)/shard_map/ppermute | solution.py:373
